TPU v7x, 32 devices: a whole 2x2x4 slice. The times are simulated.
32 devices in a mesh: dp: 16 (over z, y, x), tensor: 2 (over core).
Axes of the slice: x: 2, y: 2, z: 4, core: 2. Of those that a mesh axis runs over, the one named last changes fastest.
Arguments:
- hidden_in: float32 [8192, 1536], P('dp'), may hold values from -6 to 6
- out_grad: float32 [8192, 1536], P('dp'), may hold values from -6 to 6
- prompt_states: bfloat16 [32, 128, 768], P('dp'), may hold values from -6 to 6
- row_split: int32 [16], P('dp'), may hold values from 256 to 512, as said below
- prompt_len: int32 [32], P('dp'), may hold values from 1 to 128, as said below
- gain_attn: float32 [1536], replicated, may hold values from 0.5 to 1.5
- bias_attn: float32 [1536], replicated, may hold values from -1.2 to 1.2
- gain_cross: float32 [1536], replicated, may hold values from 0.5 to 1.5
- bias_cross: float32 [1536], replicated, may hold values from -1.2 to 1.2
- gain_ff: float32 [1536], replicated, may hold values from 0.5 to 1.5
- bias_ff: float32 [1536], replicated, may hold values from -1.2 to 1.2
- w_query: bfloat16 [1536, 1536], P(None, 'tensor'), may hold values from -0.15625 to 0.15625
- w_key: bfloat16 [1536, 1536], P(None, 'tensor'), may hold values from -0.15625 to 0.15625
- w_value: bfloat16 [1536, 1536], P(None, 'tensor'), may hold values from -0.15625 to 0.15625
- w_out: bfloat16 [1536, 1536], P('tensor'), may hold values from -2.5 to 2.5
- c_query: bfloat16 [1536, 1536], P(None, 'tensor'), may hold values from -0.15625 to 0.15625
- c_key: bfloat16 [768, 1536], P(None, 'tensor'), may hold values from -0.21875 to 0.21875
- c_value: bfloat16 [768, 1536], P(None, 'tensor'), may hold values from -0.21875 to 0.21875
- c_out: bfloat16 [1536, 1536], P('tensor'), may hold values from -1.25 to 1.25
- w_gate: bfloat16 [1536, 6144], P(None, 'tensor'), may hold values from -0.15625 to 0.15625
- w_up: bfloat16 [1536, 6144], P(None, 'tensor'), may hold values from -0.15625 to 0.15625
- w_down: bfloat16 [6144, 1536], P('tensor'), may hold values from -0.078125 to 0.078125
Outputs:
- result: float32 [8192, 1536], P('dp')
- grad_hidden: float32 [8192, 1536], P('dp')
- grad_gain_attn: float32 [1536], P(('dp', 'tensor'))
- grad_bias_attn: float32 [1536], P(('dp', 'tensor'))
- grad_gain_cross: float32 [1536], P(('dp', 'tensor'))
- grad_bias_cross: float32 [1536], P(('dp', 'tensor'))
- grad_gain_ff: float32 [1536], P(('dp', 'tensor'))
- grad_bias_ff: float32 [1536], P(('dp', 'tensor'))
- grad_w_query: float32 [1536, 1536], P('dp', 'tensor')
- grad_w_key: float32 [1536, 1536], P('dp', 'tensor')
- grad_w_value: float32 [1536, 1536], P('dp', 'tensor')
- grad_w_out: float32 [1536, 1536], P('tensor', 'dp')
- grad_c_query: float32 [1536, 1536], P('dp', 'tensor')
- grad_c_key: float32 [768, 1536], P('dp', 'tensor')
- grad_c_value: float32 [768, 1536], P('dp', 'tensor')
- grad_c_out: float32 [1536, 1536], P('tensor', 'dp')
- grad_w_gate: float32 [1536, 6144], P('dp', 'tensor')
- grad_w_up: float32 [1536, 6144], P('dp', 'tensor')
- grad_w_down: float32 [6144, 1536], P('tensor', 'dp')
Inputs may be any that keep to these rules, and one draw needn't show every extreme that they name: `row_split`: each buffer holds either one row of 512 frames (value 512) or two rows of 256 frames (value 512 / 2); exactly half of the buffers hold one row, which ones is drawn. `prompt_len`: slot 2b + 1 is unused where buffer b holds one row; some slot has all 128 states.
All inputs are finite; a program needn't handle non-finite values.
Results may differ from a plain program's by a relative error of at most 0.029.
Values may be sent and summed in bfloat16 or wider, within the bound.
No kernel may reach another device: no remote copies, remote signals or barrier semaphores. Data moves between devices by JAX's collectives and lax.ppermute only.
A program may use at most 256 MiB of HBM per device.

v0:
```python
import math

import jax
import jax.numpy as jnp
from jax import lax
from jax.sharding import PartitionSpec as P

PROMPT = 128
HEAD = 64


norm_eps = 1e-05
score_scale = 0.125
masked_score = -1e30
block_most = 512


def product_plain(left_side, right_side):
    return jnp.dot(left_side, right_side, preferred_element_type=jnp.float32)


def product_over_rows(left_side, right_side):
    return lax.dot_general(
        left_side, right_side, (((0,), (0,)), ((), ())), preferred_element_type=jnp.float32
    )


def product_with_rows(left_side, right_side):
    return lax.dot_general(
        left_side, right_side, (((1,), (1,)), ((), ())), preferred_element_type=jnp.float32
    )


def rotary_tables(positions, width):
    dim_index = jnp.arange(width) % HEAD
    freq_index = (dim_index % 16).astype(jnp.float32)
    inverse_freq = jnp.exp(freq_index * (-math.log(10000.0) / 16.0))
    angles = positions[:, None] * inverse_freq[None, :]
    cosine = jnp.cos(angles)
    sine_part = jnp.sin(angles)
    cos_table = jnp.where(dim_index < 32, cosine, 1.0)
    sin_lower = jnp.where(dim_index < 16, -sine_part, 0.0)
    sin_upper = jnp.where((dim_index >= 16) & (dim_index < 32), sine_part, 0.0)
    return (cos_table, sin_lower, sin_upper)


def rotate(values, tables):
    cos_table, sin_lower, sin_upper = tables
    return (
        values * cos_table
        + jnp.roll(values, -16, axis=1) * sin_lower
        + jnp.roll(values, 16, axis=1) * sin_upper
    )


def rotate_back(incoming, tables):
    cos_table, sin_lower, sin_upper = tables
    return (
        incoming * cos_table
        + jnp.roll(incoming * sin_lower, 16, axis=1)
        + jnp.roll(incoming * sin_upper, -16, axis=1)
    )


def normalize(values, norm_gain, norm_shift):
    average = jnp.mean(values, axis=-1, keepdims=True)
    centered = values - average
    variance = jnp.mean(centered * centered, axis=-1, keepdims=True)
    inverse = lax.rsqrt(variance + norm_eps)
    scaled = centered * inverse
    return (scaled * norm_gain + norm_shift, scaled, inverse)


def normalize_back(incoming, scaled, inverse, norm_gain):
    grad_gain = jnp.sum(incoming * scaled, axis=0)
    grad_shift = jnp.sum(incoming, axis=0)
    weighted = incoming * norm_gain
    grad_input = inverse * (
        weighted
        - jnp.mean(weighted, axis=-1, keepdims=True)
        - scaled * jnp.mean(weighted * scaled, axis=-1, keepdims=True)
    )
    return (grad_input, grad_gain, grad_shift)


def heads_of(values):
    return values.reshape(values.shape[0], values.shape[1] // HEAD, HEAD)


def attend_forward(query_block, key_heads, value_heads, allowed):
    query_heads = heads_of(query_block)
    scores = (
        jnp.einsum("qhd,khd->hqk", query_heads, key_heads, preferred_element_type=jnp.float32)
        * score_scale
    )
    scores = jnp.where(allowed[None], scores, masked_score)
    largest = jnp.max(scores, axis=-1, keepdims=True)
    exp_scores = jnp.exp(scores - largest)
    totals = jnp.sum(exp_scores, axis=-1, keepdims=True)
    soft_weights = (exp_scores / totals).astype(jnp.bfloat16)
    mixed_heads = jnp.einsum(
        "hqk,khd->qhd", soft_weights, value_heads, preferred_element_type=jnp.float32
    )
    mixed_flat = mixed_heads.reshape(query_block.shape[0], query_block.shape[1]).astype(
        jnp.bfloat16
    )
    return (mixed_flat, largest[..., 0] + jnp.log(totals[..., 0]))


def attend_backward(query_block, key_heads, value_heads, allowed, grad_block, logsum_block):
    query_heads = heads_of(query_block)
    grad_heads = heads_of(grad_block)
    scores = (
        jnp.einsum("qhd,khd->hqk", query_heads, key_heads, preferred_element_type=jnp.float32)
        * score_scale
    )
    scores = jnp.where(allowed[None], scores, masked_score)
    soft_weights = jnp.exp(scores - logsum_block[..., None])
    grad_weights = jnp.einsum(
        "qhd,khd->hqk", grad_heads, value_heads, preferred_element_type=jnp.float32
    )
    inner_sum = jnp.sum(soft_weights * grad_weights, axis=-1, keepdims=True)
    grad_scores = (soft_weights * (grad_weights - inner_sum)).astype(jnp.bfloat16)
    grad_query = (
        jnp.einsum("hqk,khd->qhd", grad_scores, key_heads, preferred_element_type=jnp.float32)
        * score_scale
    )
    grad_key = (
        jnp.einsum("hqk,qhd->khd", grad_scores, query_heads, preferred_element_type=jnp.float32)
        * score_scale
    )
    grad_value = jnp.einsum(
        "hqk,qhd->khd",
        soft_weights.astype(jnp.bfloat16),
        grad_heads,
        preferred_element_type=jnp.float32,
    )
    return (
        grad_query.reshape(query_block.shape),
        grad_key.reshape(grad_key.shape[0], -1),
        grad_value.reshape(grad_value.shape[0], -1),
    )


def attend_all(queries, keys_in, values_in, allow_fn):
    key_heads = heads_of(keys_in)
    value_heads = heads_of(values_in)
    block_rows = min(block_most, queries.shape[0])

    def one_block(block_index):
        row_start = block_index * block_rows
        return attend_forward(queries, key_heads, value_heads, allow_fn(row_start, block_rows))

    mixed_blocks, logsum = lax.map(one_block, jnp.arange(queries.shape[0] // block_rows))
    return (mixed_blocks.reshape(queries.shape), logsum)


def attend_all_back(queries, keys_in, values_in, allow_fn, grad_out, logsum):
    key_heads = heads_of(keys_in)
    value_heads = heads_of(values_in)
    block_rows = min(block_most, queries.shape[0])

    def one_block(running, inputs_now):
        block_index, logsum_block = inputs_now
        row_start = block_index * block_rows
        grad_query, grad_key, grad_value = attend_backward(
            queries, key_heads, value_heads, allow_fn(row_start, block_rows), grad_out, logsum_block
        )
        return ((running[0] + grad_key, running[1] + grad_value), grad_query)

    zero_sums = (jnp.zeros(keys_in.shape, jnp.float32), jnp.zeros(values_in.shape, jnp.float32))
    (grad_keys, grad_values), grad_blocks = lax.scan(
        one_block, zero_sums, (jnp.arange(queries.shape[0] // block_rows), logsum)
    )
    return (grad_blocks.reshape(queries.shape), grad_keys, grad_values)


def summed_rows(left_side, right_side, share_rows):

    def row_terms(row_start, row_count):
        return product_plain(left_side, right_side)

    return lax.psum_scatter(
        row_terms(jnp.int32(0), share_rows * lax.axis_size("tensor")).astype(jnp.bfloat16),
        "tensor",
        scatter_dimension=0,
        tiled=True,
    ).astype(jnp.float32)


def summed_back(grad_pairs, share_rows):

    def row_terms(row_start, row_count):
        total_term = None
        for grad_part, weight_part in grad_pairs:
            partial_term = product_with_rows(grad_part, weight_part)
            total_term = partial_term if total_term is None else total_term + partial_term
        return total_term

    return lax.psum_scatter(
        row_terms(jnp.int32(0), share_rows * lax.axis_size("tensor")).astype(jnp.bfloat16),
        "tensor",
        scatter_dimension=0,
        tiled=True,
    ).astype(jnp.float32)


def spread_normed(share_low):
    return lax.all_gather(share_low, "tensor", axis=0, tiled=True)


def spread_grads(share_low):
    return lax.all_gather(share_low, "tensor", axis=0, tiled=True)


def spread_result(share_values):
    return lax.all_gather(share_values.astype(jnp.bfloat16), "tensor", axis=0, tiled=True).astype(
        share_values.dtype
    )


def on_device(
    hidden_in,
    out_grad,
    prompt_states,
    row_split,
    prompt_len,
    gain_attn,
    bias_attn,
    gain_cross,
    bias_cross,
    gain_ff,
    bias_ff,
    w_query,
    w_key,
    w_value,
    w_out,
    c_query,
    c_key,
    c_value,
    c_out,
    w_gate,
    w_up,
    w_down,
):
    frame_count = hidden_in.shape[0]
    share_rows = frame_count // lax.axis_size("tensor")
    first_row = lax.axis_index("tensor") * share_rows
    positions = jnp.arange(frame_count, dtype=jnp.int32)
    split_here = row_split[0]
    row_ids = (positions >= split_here).astype(jnp.int32)
    tables = rotary_tables((positions - row_ids * split_here).astype(jnp.float32), w_query.shape[1])
    key_index = jnp.arange(2 * PROMPT, dtype=jnp.int32)
    key_rows = key_index // PROMPT
    key_live = key_index % PROMPT < jnp.where(key_rows == 0, prompt_len[0], prompt_len[1])

    def self_allow(row_start, block_rows):
        return row_ids[:, None] == row_ids[None, :]

    def cross_allow(row_start, block_rows):
        return (row_ids[:, None] == key_rows[None, :]) & key_live[None, :]

    def own_share(values):
        return lax.dynamic_slice_in_dim(values, first_row, share_rows, 0)

    def self_inputs(normed_low):
        queries = rotate(product_plain(normed_low, w_query), tables).astype(jnp.bfloat16)
        keys_now = rotate(product_plain(normed_low, w_key), tables).astype(jnp.bfloat16)
        values_now = product_plain(normed_low, w_value).astype(jnp.bfloat16)
        return (queries, keys_now, values_now)

    def ff_inputs(normed_low):
        gate_pre = product_plain(normed_low, w_gate)
        up_pre = product_plain(normed_low, w_up)
        return (gate_pre, up_pre, (jax.nn.silu(gate_pre) * up_pre).astype(jnp.bfloat16))

    input_one = normalize(hidden_in, gain_attn, bias_attn)[0].astype(jnp.bfloat16)
    query_one, key_one, value_one = self_inputs(input_one)
    attended_one, logsum_one = attend_all(query_one, key_one, value_one, self_allow)
    resid_one = own_share(hidden_in) + summed_rows(attended_one, w_out, share_rows)
    input_two = spread_normed(normalize(resid_one, gain_cross, bias_cross)[0].astype(jnp.bfloat16))
    cross_query = product_plain(input_two, c_query).astype(jnp.bfloat16)
    context_flat = prompt_states.reshape(2 * PROMPT, prompt_states.shape[2])
    cross_key = product_plain(context_flat, c_key).astype(jnp.bfloat16)
    cross_value = product_plain(context_flat, c_value).astype(jnp.bfloat16)
    attended_two, logsum_two = attend_all(cross_query, cross_key, cross_value, cross_allow)
    resid_two = resid_one + summed_rows(attended_two, c_out, share_rows)
    input_three = spread_normed(normalize(resid_two, gain_ff, bias_ff)[0].astype(jnp.bfloat16))
    gate_pre, up_pre, mixed_low = ff_inputs(input_three)
    result_share = resid_two + summed_rows(mixed_low, w_down, share_rows)
    result = spread_result(result_share)
    hidden_again, resid_one_again, resid_two_again = lax.optimization_barrier(
        (hidden_in, resid_one, resid_two)
    )
    input_two, input_three = (
        lax.all_gather(
            normalize(resid_one_again, gain_cross, bias_cross)[0].astype(jnp.bfloat16),
            "tensor",
            axis=0,
            tiled=True,
        ),
        lax.all_gather(
            normalize(resid_two_again, gain_ff, bias_ff)[0].astype(jnp.bfloat16),
            "tensor",
            axis=0,
            tiled=True,
        ),
    )
    input_one = normalize(hidden_again, gain_attn, bias_attn)[0].astype(jnp.bfloat16)
    query_one, key_one, value_one = self_inputs(input_one)
    cross_query = product_plain(input_two, c_query).astype(jnp.bfloat16)
    gate_pre, up_pre, mixed_low = ff_inputs(input_three)
    grad_share = own_share(out_grad)
    grad_ff_out = out_grad.astype(jnp.bfloat16)
    grad_w_down = product_over_rows(mixed_low, grad_ff_out)
    grad_mixed = product_with_rows(grad_ff_out, w_down)
    sigmoid_gate = jax.nn.sigmoid(gate_pre)
    grad_gate = (
        grad_mixed * up_pre * sigmoid_gate * (1.0 + gate_pre * (1.0 - sigmoid_gate))
    ).astype(jnp.bfloat16)
    grad_up = (grad_mixed * gate_pre * sigmoid_gate).astype(jnp.bfloat16)
    grad_w_gate = product_over_rows(input_three, grad_gate)
    grad_w_up = product_over_rows(input_three, grad_up)
    normed_grad_three = summed_back(((grad_gate, w_gate), (grad_up, w_up)), share_rows)
    scaled_three, inverse_three = normalize(resid_two, gain_ff, bias_ff)[1:]
    back_three, grad_gain_ff, grad_bias_ff = normalize_back(
        normed_grad_three, scaled_three, inverse_three, gain_ff
    )
    grad_two = grad_share + back_three
    grad_cross_out = spread_grads(grad_two.astype(jnp.bfloat16))
    grad_c_out = product_over_rows(attended_two, grad_cross_out)
    grad_attended_two = product_with_rows(grad_cross_out, c_out).astype(jnp.bfloat16)
    cross_query_grad, cross_key_grad, cross_value_grad = attend_all_back(
        cross_query, cross_key, cross_value, cross_allow, grad_attended_two, logsum_two
    )
    cross_query_grad = cross_query_grad.astype(jnp.bfloat16)
    cross_key_grad = cross_key_grad.astype(jnp.bfloat16)
    cross_value_grad = cross_value_grad.astype(jnp.bfloat16)
    grad_c_query = product_over_rows(input_two, cross_query_grad)
    grad_c_key = product_over_rows(context_flat, cross_key_grad)
    grad_c_value = product_over_rows(context_flat, cross_value_grad)
    normed_grad_two = summed_back(((cross_query_grad, c_query),), share_rows)
    scaled_two, inverse_two = normalize(resid_one, gain_cross, bias_cross)[1:]
    back_two, grad_gain_cross, grad_bias_cross = normalize_back(
        normed_grad_two, scaled_two, inverse_two, gain_cross
    )
    grad_one = grad_two + back_two
    grad_self_out = spread_grads(grad_one.astype(jnp.bfloat16))
    grad_w_out = product_over_rows(attended_one, grad_self_out)
    grad_attended_one = product_with_rows(grad_self_out, w_out).astype(jnp.bfloat16)
    query_grad, key_grad, value_grad = attend_all_back(
        query_one, key_one, value_one, self_allow, grad_attended_one, logsum_one
    )
    query_grad = rotate_back(query_grad, tables).astype(jnp.bfloat16)
    key_grad = rotate_back(key_grad, tables).astype(jnp.bfloat16)
    value_grad = value_grad.astype(jnp.bfloat16)
    grad_w_query = product_over_rows(input_one, query_grad)
    grad_w_key = product_over_rows(input_one, key_grad)
    grad_w_value = product_over_rows(input_one, value_grad)
    normed_grad_one = summed_back(
        ((query_grad, w_query), (key_grad, w_key), (value_grad, w_value)), share_rows
    )
    scaled_one, inverse_one = normalize(own_share(hidden_in), gain_attn, bias_attn)[1:]
    back_one, grad_gain_attn, grad_bias_attn = normalize_back(
        normed_grad_one, scaled_one, inverse_one, gain_attn
    )
    grad_hidden = spread_result(grad_one + back_one)
    vector_sums = lax.psum_scatter(
        jnp.stack(
            [
                grad_gain_attn,
                grad_bias_attn,
                grad_gain_cross,
                grad_bias_cross,
                grad_gain_ff,
                grad_bias_ff,
            ]
        ),
        ("dp", "tensor"),
        scatter_dimension=1,
        tiled=True,
    )
    weight_sums = tuple(
        (
            lax.psum_scatter(
                grad_w_query.astype(jnp.bfloat16), "dp", scatter_dimension=0, tiled=True
            ).astype(jnp.float32),
            lax.psum_scatter(
                grad_w_key.astype(jnp.bfloat16), "dp", scatter_dimension=0, tiled=True
            ).astype(jnp.float32),
            lax.psum_scatter(
                grad_w_value.astype(jnp.bfloat16), "dp", scatter_dimension=0, tiled=True
            ).astype(jnp.float32),
            lax.psum_scatter(
                grad_w_out.astype(jnp.bfloat16), "dp", scatter_dimension=1, tiled=True
            ).astype(jnp.float32),
            lax.psum_scatter(
                grad_c_query.astype(jnp.bfloat16), "dp", scatter_dimension=0, tiled=True
            ).astype(jnp.float32),
            lax.psum_scatter(
                grad_c_key.astype(jnp.bfloat16), "dp", scatter_dimension=0, tiled=True
            ).astype(jnp.float32),
            lax.psum_scatter(
                grad_c_value.astype(jnp.bfloat16), "dp", scatter_dimension=0, tiled=True
            ).astype(jnp.float32),
            lax.psum_scatter(
                grad_c_out.astype(jnp.bfloat16), "dp", scatter_dimension=1, tiled=True
            ).astype(jnp.float32),
            lax.psum_scatter(
                grad_w_gate.astype(jnp.bfloat16), "dp", scatter_dimension=0, tiled=True
            ).astype(jnp.float32),
            lax.psum_scatter(
                grad_w_up.astype(jnp.bfloat16), "dp", scatter_dimension=0, tiled=True
            ).astype(jnp.float32),
            lax.psum_scatter(
                grad_w_down.astype(jnp.bfloat16), "dp", scatter_dimension=1, tiled=True
            ).astype(jnp.float32),
        )
    )
    return (
        result,
        grad_hidden,
        vector_sums[0],
        vector_sums[1],
        vector_sums[2],
        vector_sums[3],
        vector_sums[4],
        vector_sums[5],
        weight_sums[0],
        weight_sums[1],
        weight_sums[2],
        weight_sums[3],
        weight_sums[4],
        weight_sums[5],
        weight_sums[6],
        weight_sums[7],
        weight_sums[8],
        weight_sums[9],
        weight_sums[10],
    )


def solution(mesh):
    in_specs = (
        P("dp", None),
        P("dp", None),
        P("dp", None, None),
        P("dp"),
        P("dp"),
        P(),
        P(),
        P(),
        P(),
        P(),
        P(),
        P(None, "tensor"),
        P(None, "tensor"),
        P(None, "tensor"),
        P("tensor", None),
        P(None, "tensor"),
        P(None, "tensor"),
        P(None, "tensor"),
        P("tensor", None),
        P(None, "tensor"),
        P(None, "tensor"),
        P("tensor", None),
    )
    out_specs = (
        P("dp", None),
        P("dp", None),
        P(("dp", "tensor")),
        P(("dp", "tensor")),
        P(("dp", "tensor")),
        P(("dp", "tensor")),
        P(("dp", "tensor")),
        P(("dp", "tensor")),
        P("dp", "tensor"),
        P("dp", "tensor"),
        P("dp", "tensor"),
        P("tensor", "dp"),
        P("dp", "tensor"),
        P("dp", "tensor"),
        P("dp", "tensor"),
        P("tensor", "dp"),
        P("dp", "tensor"),
        P("dp", "tensor"),
        P("tensor", "dp"),
    )
    return jax.shard_map(
        on_device, mesh=mesh, in_specs=in_specs, out_specs=out_specs, check_vma=False
    )
```

profile of v0, /device:TPU:0, one launch (start us, length us, event | category | flops | bytes accessed | tf_op | source)
XLA Modules:
  0.0 2095.8 jit_solution(17209869919928130730)
XLA Ops:
  18.2 3.6 fusion.132
  27.4 11.5 fusion.50
  42.6 3.2 fusion
  48.5 3.6 fusion.88
  57.2 10.3 reduce-scatter.25.cloned.1.call-done
  80.8 2.8 all-gather.9.cloned.1.call-done
  83.7 3.7 convolution_convert_fusion.19
  98.7 10.3 reduce-scatter.27.cloned.1.call-done
  109.1 2.9 fusion.125
  119.8 8.1 all-gather.15.cloned.1.call-done
  127.9 11.1 fusion.141
  139.0 11.1 fusion.140
  150.1 13.7 multiply_convert_fusion.3
  163.9 10.8 fusion.142
  174.7 7.7 fusion.15
  196.1 3.1 fusion.79
  199.2 3.8 fusion.123
  203.1 5.1 fusion.145
  211.2 4.8 fusion.144
  216.0 3.8 convolution_convert_fusion.18
  221.2 3.6 fusion.143
  225.4 4.4 convolution_convert_fusion.17
  232.2 8.3 multiply_reduce_fusion.1
  240.5 4.7 multiply_convert_fusion.2
  255.9 8.1 fusion.54
  265.5 6.4 fusion.146
  271.9 9.8 fusion.139
  286.2 20.3 convolution_convert_fusion.12
  306.6 4.4 convolution_convert_fusion.16
  312.6 12.4 multiply_reduce_fusion
  326.2 7.0 multiply_convert_fusion
  333.2 3.2 convolution_multiply_fusion
  340.5 3.0 copy.121
  343.5 6.8 fusion.20
  352.2 6.2 fusion.78
  362.1 3.2 fusion.85
  370.0 4.3 fusion.90
  376.4 3.0 fusion.89
  381.4 4.2 convolution_convert_fusion.3
  387.2 2.9 convolution_convert_fusion.4
  397.7 4.2 convolution_convert_fusion.5
  403.6 2.9 convolution_convert_fusion.6
  406.5 2.8 convolution_convert_fusion.7
  410.5 2.8 convolution_convert_fusion.8
  415.0 2.9 fusion.37
  418.0 11.6 convolution_convert_fusion
  430.9 9.4 convolution_convert_fusion.1
  440.6 9.4 convolution_convert_fusion.2
  450.0 59.4 %reduce-scatter.59.cloned.1.call-done = bf16[48,768]{1,0:T(8,128)(2,1)} async-done(((bf16[768,768]{1,0:T(8,128)(2,1)}), bf16[48,768]{1,0:T(8,128)(2,1)}) %reduce-scatter.59.cloned.1.call-update) | async-done | bytes 73744
  511.3 126.0 %reduce-scatter.57.cloned.1.call-done = bf16[48,768]{1,0:T(8,128)(2,1)} async-done(((bf16[768,768]{1,0:T(8,128)(2,1)}), bf16[48,768]{1,0:T(8,128)(2,1)}) %reduce-scatter.57.cloned.1.call-update) | async-done | bytes 73744
  639.1 130.5 %reduce-scatter.47.cloned.1.call-done = bf16[768,96]{0,1:T(8,128)(2,1)} async-done(((bf16[768,1536]{0,1:T(8,128)(2,1)}), bf16[768,96]{0,1:T(8,128)(2,1)}) %reduce-scatter.47.cloned.1.call-update) | async-done | bytes 147472 | tf_op jit(solution)/shard_map/reduce_scatter | solution.py:406
  771.2 131.6 %reduce-scatter.45.cloned.1.call-done = bf16[96,768]{1,0:T(8,128)(2,1)} async-done(((bf16[1536,768]{1,0:T(8,128)(2,1)}), bf16[96,768]{1,0:T(8,128)(2,1)}) %reduce-scatter.45.cloned.1.call-update) | async-done | bytes 147472 | tf_op jit(solution)/shard_map/reduce_scatter | solution.py:397
  904.4 9.3 all-gather.13.cloned.1.call-done
  913.7 3.5 convert_element_type.334
  917.2 98.1 %reduce-scatter.55.cloned.1.call-done = f32[48,6]{1,0:T(8,128)} async-done(((f32[1536,6]{1,0:T(8,128)}), f32[48,6]{1,0:T(8,128)}) %reduce-scatter.55.cloned.1.call-update) | async-done | bytes 1168
  1019.9 127.7 %reduce-scatter.43.cloned.1.call-done = bf16[768,96]{0,1:T(8,128)(2,1)} async-done(((bf16[768,1536]{0,1:T(8,128)(2,1)}), bf16[768,96]{0,1:T(8,128)(2,1)}) %reduce-scatter.43.cloned.1.call-update) | async-done | bytes 147472 | tf_op jit(solution)/shard_map/reduce_scatter | solution.py:394
  1149.3 131.5 %reduce-scatter.41.cloned.1.call-done = bf16[96,768]{1,0:T(8,128)(2,1)} async-done(((bf16[1536,768]{1,0:T(8,128)(2,1)}), bf16[96,768]{1,0:T(8,128)(2,1)}) %reduce-scatter.41.cloned.1.call-update) | async-done | bytes 147472 | tf_op jit(solution)/shard_map/reduce_scatter | solution.py:391
  1282.4 130.9 %reduce-scatter.39.cloned.1.call-done = bf16[96,768]{1,0:T(8,128)(2,1)} async-done(((bf16[1536,768]{1,0:T(8,128)(2,1)}), bf16[96,768]{1,0:T(8,128)(2,1)}) %reduce-scatter.39.cloned.1.call-update) | async-done | bytes 147472 | tf_op jit(solution)/shard_map/reduce_scatter | solution.py:388
  1414.9 131.7 %reduce-scatter.37.cloned.1.call-done = bf16[96,768]{1,0:T(8,128)(2,1)} async-done(((bf16[1536,768]{1,0:T(8,128)(2,1)}), bf16[96,768]{1,0:T(8,128)(2,1)}) %reduce-scatter.37.cloned.1.call-update) | async-done | bytes 147472 | tf_op jit(solution)/shard_map/reduce_scatter | solution.py:385
  1548.3 8.9 all-gather.23.cloned.1.call-done
  1557.2 3.5 convert_element_type.367
  1560.7 174.1 %reduce-scatter.53.cloned.1.call-done = bf16[3072,96]{0,1:T(8,128)(2,1)} async-done(((bf16[3072,1536]{0,1:T(8,128)(2,1)}), bf16[3072,96]{0,1:T(8,128)(2,1)}) %reduce-scatter.53.cloned.1.call-update) | async-done | bytes 589840 | tf_op jit(solution)/shard_map/reduce_scatter | solution.py:415
  1737.1 174.2 %reduce-scatter.51.cloned.1.call-done = bf16[96,3072]{1,0:T(8,128)(2,1)} async-done(((bf16[1536,3072]{1,0:T(8,128)(2,1)}), bf16[96,3072]{1,0:T(8,128)(2,1)}) %reduce-scatter.51.cloned.1.call-update) | async-done | bytes 589840 | tf_op jit(solution)/shard_map/reduce_scatter | solution.py:412
  1913.4 173.4 %reduce-scatter.49.cloned.1.call-done = bf16[96,3072]{1,0:T(8,128)(2,1)} async-done(((bf16[1536,3072]{1,0:T(8,128)(2,1)}), bf16[96,3072]{1,0:T(8,128)(2,1)}) %reduce-scatter.49.cloned.1.call-update) | async-done | bytes 589840 | tf_op jit(solution)/shard_map/reduce_scatter | solution.py:409
  (429 shorter events, 157.8 us)
Async XLA Ops:
  7.2 76.5 %copy-start = (bf16[1536,768]{1,0:T(8,128)(2,1)S(1)}, bf16[1536,768]{1,0:T(8,128)(2,1)}, u32[]{:S(2)}) copy-start(bf16[1536,768]{1,0:T(8,128)(2,1)} %param.37) | copy-start | bytes 7077892
  7.2 60.2 %reduce-scatter.25.cloned.1.call-start = ((), (), s32[]{:S(2)}) async-start(), calls=%async_computation.18 | async-start | bytes 2359296 | tf_op jit(solution)/shard_map/reduce_scatter | solution.py:183
  7.3 20.1 copy-start.94
  7.3 20.1 copy-start.87
  7.3 20.1 copy-start.89
  7.3 20.1 copy-start.64
  7.3 4.8 copy-start.70
  17.2 4.7 copy-start.14
  18.2 4.6 copy-start.99
  22.5 4.9 copy-start.68
  22.8 25.6 %copy-start.18 = (pred[512,512]{0,1:T(8,128)(4,1)}, pred[512,512]{0,1:T(8,128)(4,1)S(1)}, u32[]{:S(2)}) copy-start(pred[512,512]{0,1:T(8,128)(4,1)S(1)} %broadcast_compare_fusion) | copy-start | bytes 786436
  48.4 4.5 copy-start.36
  55.5 28.1 %all-gather.9.cloned.1.call-start = ((), (), s32[]{:S(2)}) async-start(), calls=%async_computation.19 | async-start | bytes 2359296 | tf_op jit(solution)/shard_map/all_gather | solution.py:209
  57.2 12.9 copy-start.83
  72.5 36.6 %reduce-scatter.27.cloned.1.call-start = ((), (), s32[]{:S(2)}) async-start(), calls=%async_computation.20 | async-start | bytes 2359296 | tf_op jit(solution)/shard_map/reduce_scatter | solution.py:183
  80.8 12.4 copy-start.24
  98.7 29.2 %all-gather.15.cloned.1.call-start = ((), (), s32[]{:S(2)}) async-start(), calls=%async_computation.24 | async-start | bytes 2359296 | tf_op jit(solution)/shard_map/all_gather | solution.py:302
  116.7 79.3 %reduce-scatter.31.cloned.1.call-start = ((), (), s32[]{:S(2)}) async-start(), calls=%async_computation.25 | async-start | bytes 2359296 | tf_op jit(solution)/shard_map/reduce_scatter | solution.py:200
  127.9 11.1 copy-start.102
  139.0 11.1 copy-start.52
  150.1 24.5 %slice-start.8 = ((s8[9437184]{0:T(1024)(128)(4,1)}), s8[1048576]{0:T(1024)(128)(4,1)S(1)}, s32[]{:S(2)}) async-start(s8[9437184]{0:T(1024)(128)(4,1)} %bitcast.202), calls=%async_computation.52 | async-start | bytes 2097152
  150.1 24.5 %slice-start.9 = ((s8[9437184]{0:T(1024)(128)(4,1)}), s8[4194304]{0:T(1024)(128)(4,1)S(1)}, s32[]{:S(2)}) async-start(s8[9437184]{0:T(1024)(128)(4,1)} %bitcast.202), calls=%async_computation.53 | async-start | bytes 8388608
  163.9 10.8 slice-start.10
  163.9 10.8 copy-start.107
  182.4 33.6 %all-gather.17.cloned.1.call-start = ((), (), s32[]{:S(2)}) async-start(), calls=%async_computation.26 | async-start | bytes 2359296 | tf_op jit(solution)/shard_map/all_gather | solution.py:296
  184.8 4.2 copy-start.3
  194.7 30.6 %all-gather.19.cloned.1.call-start = ((), (), s32[]{:S(2)}) async-start(), calls=%async_computation.27 | async-start | bytes 2359296 | tf_op jit(solution)/shard_map/all_gather | solution.py:213
  203.0 68.9 %all-gather.11.cloned.1.call-start = ((), (), s32[]{:S(2)}) async-start(), calls=%async_computation.21 | async-start | bytes 2359296 | tf_op jit(solution)/shard_map/all_gather | solution.py:209
  224.8 56.9 %reduce-scatter.33.cloned.1.call-start = ((), (), s32[]{:S(2)}) async-start(), calls=%async_computation.28 | async-start | bytes 2359296 | tf_op jit(solution)/shard_map/reduce_scatter | solution.py:200
  232.2 8.3 slice-start.6
  232.2 8.3 slice-start.7
  250.5 56.1 %all-gather.21.cloned.1.call-start = ((), (), s32[]{:S(2)}) async-start(), calls=%async_computation.29 | async-start | bytes 2359296 | tf_op jit(solution)/shard_map/all_gather | solution.py:213
  271.9 9.9 copy-start.6
  271.9 9.9 copy-start.80
  271.9 9.9 copy-start.86
  285.9 104.4 %reduce-scatter.29.cloned.1.call-start = ((), (), s32[]{:S(2)}) async-start(), calls=%async_computation.22 | async-start | bytes 2359296 | tf_op jit(solution)/shard_map/reduce_scatter | solution.py:183
  306.5 87.4 %reduce-scatter.35.cloned.1.call-start = ((), (), s32[]{:S(2)}) async-start(), calls=%async_computation.30 | async-start | bytes 2359296 | tf_op jit(solution)/shard_map/reduce_scatter | solution.py:200
  312.6 12.5 copy-start.28
  312.6 12.5 slice-start
  312.6 12.4 slice-start.1
  312.6 13.6 slice-start.2
  352.2 6.2 copy-start.98
  352.2 9.6 slice-start.3
  352.2 9.6 slice-start.4
  362.1 4.1 copy-start.101
  368.8 5.5 copy-start.23
  368.9 140.6 %reduce-scatter.59.cloned.1.call-start = ((), (), s32[]{:S(2)}) async-start(), calls=%async_computation.43 | async-start | bytes 1253376
  376.3 260.9 %reduce-scatter.57.cloned.1.call-start = ((), (), s32[]{:S(2)}) async-start(), calls=%async_computation.42 | async-start | bytes 1253376
  381.3 388.2 %reduce-scatter.47.cloned.1.call-start = ((), (), s32[]{:S(2)}) async-start(), calls=%async_computation.37 | async-start | bytes 2506752 | tf_op jit(solution)/shard_map/reduce_scatter | solution.py:406
  385.6 517.1 %reduce-scatter.45.cloned.1.call-start = ((), (), s32[]{:S(2)}) async-start(), calls=%async_computation.36 | async-start | bytes 2506752 | tf_op jit(solution)/shard_map/reduce_scatter | solution.py:397
  390.2 3.7 copy-start.77
  390.2 3.8 copy-start.84
  390.2 523.5 %all-gather.13.cloned.1.call-start = ((), (), s32[]{:S(2)}) async-start(), calls=%async_computation.23 | async-start | bytes 2359296 | tf_op jit(solution)/shard_map/all_gather | solution.py:217
  393.7 621.6 %reduce-scatter.55.cloned.1.call-start = ((), (), s32[]{:S(2)}) async-start(), calls=%async_computation.41 | async-start | bytes 811008
  393.9 3.8 copy-start.46
  397.7 750.0 %reduce-scatter.43.cloned.1.call-start = ((), (), s32[]{:S(2)}) async-start(), calls=%async_computation.35 | async-start | bytes 2506752 | tf_op jit(solution)/shard_map/reduce_scatter | solution.py:394
  402.0 878.8 %reduce-scatter.41.cloned.1.call-start = ((), (), s32[]{:S(2)}) async-start(), calls=%async_computation.34 | async-start | bytes 2506752 | tf_op jit(solution)/shard_map/reduce_scatter | solution.py:391
  406.5 1006.8 %reduce-scatter.39.cloned.1.call-start = ((), (), s32[]{:S(2)}) async-start(), calls=%async_computation.33 | async-start | bytes 2506752 | tf_op jit(solution)/shard_map/reduce_scatter | solution.py:388
  409.4 1137.2 %reduce-scatter.37.cloned.1.call-start = ((), (), s32[]{:S(2)}) async-start(), calls=%async_computation.32 | async-start | bytes 2506752 | tf_op jit(solution)/shard_map/reduce_scatter | solution.py:385
  413.4 1143.8 %all-gather.23.cloned.1.call-start = ((), (), s32[]{:S(2)}) async-start(), calls=%async_computation.31 | async-start | bytes 2359296 | tf_op jit(solution)/shard_map/all_gather | solution.py:217
  417.9 1316.9 %reduce-scatter.53.cloned.1.call-start = ((), (), s32[]{:S(2)}) async-start(), calls=%async_computation.40 | async-start | bytes 10027008 | tf_op jit(solution)/shard_map/reduce_scatter | solution.py:415
  429.5 1481.7 %reduce-scatter.51.cloned.1.call-start = ((), (), s32[]{:S(2)}) async-start(), calls=%async_computation.39 | async-start | bytes 10027008 | tf_op jit(solution)/shard_map/reduce_scatter | solution.py:412
  440.3 1646.5 %reduce-scatter.49.cloned.1.call-start = ((), (), s32[]{:S(2)}) async-start(), calls=%async_computation.38 | async-start | bytes 10027008 | tf_op jit(solution)/shard_map/reduce_scatter | solution.py:409
  1734.8 354.2 %copy-start.1 = (bf16[1536,768]{1,0:T(8,128)(2,1)S(1)}, bf16[1536,768]{1,0:T(8,128)(2,1)}, u32[]{:S(2)}) copy-start(bf16[1536,768]{1,0:T(8,128)(2,1)} %param.37) | copy-start | bytes 7077892
  (81 other events, 157.0 us)
Sparse Core Ops, SparseCore 0:
  55.7 11.7 reduce-scatter.24
  72.6 11.0 all-gather.8
  98.8 10.2 reduce-scatter.26
  116.9 10.9 all-gather.14
  182.5 10.2 reduce-scatter.30
  194.8 10.9 all-gather.16
  208.1 10.9 all-gather.18
  224.9 11.0 all-gather.10
  250.6 10.2 reduce-scatter.32
  286.0 11.0 all-gather.20
  306.6 10.2 reduce-scatter.28
  369.0 10.2 reduce-scatter.34
  384.6 124.7 reduce-scatter.58
  514.6 122.5 reduce-scatter.56
  642.0 127.4 reduce-scatter.46
  775.1 127.6 reduce-scatter.44
  904.7 8.9 all-gather.12
  918.7 96.6 reduce-scatter.54
  1020.3 127.3 reduce-scatter.42
  1153.2 127.5 reduce-scatter.40
  1285.7 127.5 reduce-scatter.38
  1419.0 127.6 reduce-scatter.36
  1548.2 8.9 all-gather.22
  1562.7 172.0 reduce-scatter.52
  1741.4 169.8 reduce-scatter.50
  1916.8 169.9 reduce-scatter.48
where the time goes:
time: 2100 us
  waiting for transfers between devices  1640 us (78%)
  matrix products  243 us (12%)
  other arithmetic  124 us (6%)
  local copies, waits for them, and re-layouts  70 us (3%)
    unnamed x29, waiting for transfers between devices  284 us
    reduce_scatter x1, waiting for transfers between devices, on_device(): lax.psum_scatter(grad_w_up.astype(jnp.bfloat16), 'dp', scatter_dimension=...  174 us
    reduce_scatter x1, waiting for transfers between devices, on_device(): lax.psum_scatter(grad_w_down.astype(jnp.bfloat16), 'dp', scatter_dimensio...  174 us
    reduce_scatter x1, waiting for transfers between devices, on_device(): lax.psum_scatter(grad_w_gate.astype(jnp.bfloat16), 'dp', scatter_dimensio...  173 us
    reduce_scatter x1, waiting for transfers between devices, on_device(): lax.psum_scatter(grad_w_query.astype(jnp.bfloat16), 'dp', scatter_dimensi...  132 us
    reduce_scatter x1, waiting for transfers between devices, on_device(): lax.psum_scatter(grad_c_query.astype(jnp.bfloat16), 'dp', scatter_dimensi...  132 us
    reduce_scatter x1, waiting for transfers between devices, on_device(): lax.psum_scatter(grad_w_value.astype(jnp.bfloat16), 'dp', scatter_dimensi...  131 us
    reduce_scatter x1, waiting for transfers between devices, on_device(): lax.psum_scatter(grad_w_key.astype(jnp.bfloat16), 'dp', scatter_dimension...  131 us
  transfers between devices with their start and end apart: 26, of which 18 were waited for; matrix products, arithmetic and copies ran while one was open for 13% of the time, Pallas kernels for 0%

commit v1 on v0

v1 whole, which is shorter than its diff:
```python
import math

import jax
import jax.numpy as jnp
from jax import lax
from jax.sharding import PartitionSpec as P

PROMPT = 128
HEAD = 64


norm_eps = 1e-05
score_scale = 0.125
masked_score = -1e30


def product_plain(left_side, right_side):
    return jnp.dot(left_side, right_side, preferred_element_type=jnp.float32)


def product_over_rows(left_side, right_side):
    return lax.dot_general(
        left_side, right_side, (((0,), (0,)), ((), ())), preferred_element_type=jnp.float32
    )


def product_with_rows(left_side, right_side):
    return lax.dot_general(
        left_side, right_side, (((1,), (1,)), ((), ())), preferred_element_type=jnp.float32
    )


def rotary_tables(positions, width):
    dim_index = jnp.arange(width) % HEAD
    freq_index = (dim_index % 16).astype(jnp.float32)
    inverse_freq = jnp.exp(freq_index * (-math.log(10000.0) / 16.0))
    angles = positions[:, None] * inverse_freq[None, :]
    cosine = jnp.cos(angles)
    sine_part = jnp.sin(angles)
    cos_table = jnp.where(dim_index < 32, cosine, 1.0)
    sin_lower = jnp.where(dim_index < 16, -sine_part, 0.0)
    sin_upper = jnp.where((dim_index >= 16) & (dim_index < 32), sine_part, 0.0)
    return (cos_table, sin_lower, sin_upper)


def rotate(values, tables):
    cos_table, sin_lower, sin_upper = tables
    return (
        values * cos_table
        + jnp.roll(values, -16, axis=1) * sin_lower
        + jnp.roll(values, 16, axis=1) * sin_upper
    )


def rotate_back(incoming, tables):
    cos_table, sin_lower, sin_upper = tables
    return (
        incoming * cos_table
        + jnp.roll(incoming * sin_lower, 16, axis=1)
        + jnp.roll(incoming * sin_upper, -16, axis=1)
    )


def normalize(values, norm_gain, norm_shift):
    average = jnp.mean(values, axis=-1, keepdims=True)
    centered = values - average
    variance = jnp.mean(centered * centered, axis=-1, keepdims=True)
    inverse = lax.rsqrt(variance + norm_eps)
    scaled = centered * inverse
    return (scaled * norm_gain + norm_shift, scaled, inverse)


def normalize_back(incoming, scaled, inverse, norm_gain):
    grad_gain = jnp.sum(incoming * scaled, axis=0)
    grad_shift = jnp.sum(incoming, axis=0)
    weighted = incoming * norm_gain
    grad_input = inverse * (
        weighted
        - jnp.mean(weighted, axis=-1, keepdims=True)
        - scaled * jnp.mean(weighted * scaled, axis=-1, keepdims=True)
    )
    return (grad_input, grad_gain, grad_shift)


def heads_of(values):
    return values.reshape(values.shape[0], values.shape[1] // HEAD, HEAD)


def attend_forward(query_block, key_heads, value_heads, allowed):
    query_heads = heads_of(query_block)
    scores = (
        jnp.einsum("qhd,khd->hqk", query_heads, key_heads, preferred_element_type=jnp.float32)
        * score_scale
    )
    scores = jnp.where(allowed[None], scores, masked_score)
    largest = jnp.max(scores, axis=-1, keepdims=True)
    exp_scores = jnp.exp(scores - largest)
    totals = jnp.sum(exp_scores, axis=-1, keepdims=True)
    soft_weights = (exp_scores / totals).astype(jnp.bfloat16)
    mixed_heads = jnp.einsum(
        "hqk,khd->qhd", soft_weights, value_heads, preferred_element_type=jnp.float32
    )
    mixed_flat = mixed_heads.reshape(query_block.shape[0], query_block.shape[1]).astype(
        jnp.bfloat16
    )
    return (mixed_flat, largest[..., 0] + jnp.log(totals[..., 0]))


def attend_backward(query_block, key_heads, value_heads, allowed, grad_block, logsum_block):
    query_heads = heads_of(query_block)
    grad_heads = heads_of(grad_block)
    scores = (
        jnp.einsum("qhd,khd->hqk", query_heads, key_heads, preferred_element_type=jnp.float32)
        * score_scale
    )
    scores = jnp.where(allowed[None], scores, masked_score)
    soft_weights = jnp.exp(scores - logsum_block[..., None])
    grad_weights = jnp.einsum(
        "qhd,khd->hqk", grad_heads, value_heads, preferred_element_type=jnp.float32
    )
    inner_sum = jnp.sum(soft_weights * grad_weights, axis=-1, keepdims=True)
    grad_scores = (soft_weights * (grad_weights - inner_sum)).astype(jnp.bfloat16)
    grad_query = (
        jnp.einsum("hqk,khd->qhd", grad_scores, key_heads, preferred_element_type=jnp.float32)
        * score_scale
    )
    grad_key = (
        jnp.einsum("hqk,qhd->khd", grad_scores, query_heads, preferred_element_type=jnp.float32)
        * score_scale
    )
    grad_value = jnp.einsum(
        "hqk,qhd->khd",
        soft_weights.astype(jnp.bfloat16),
        grad_heads,
        preferred_element_type=jnp.float32,
    )
    return (
        grad_query.reshape(query_block.shape),
        grad_key.reshape(grad_key.shape[0], -1),
        grad_value.reshape(grad_value.shape[0], -1),
    )


def swap_sum(partial):
    low = partial.astype(jnp.bfloat16)
    if lax.axis_size("tensor") == 2:
        other = lax.ppermute(low, "tensor", [(0, 1), (1, 0)])
        return low.astype(jnp.float32) + other.astype(jnp.float32)
    return lax.psum(low, "tensor").astype(jnp.float32)


def pairs(mask):
    return [(i, i ^ mask) for i in range(16)]


def quarters(rows_side, mine):
    blocks = rows_side.reshape(4, 4, rows_side.shape[0] // 16, rows_side.shape[1])
    out = []
    for flip in range(4):
        part = lax.dynamic_index_in_dim(blocks, mine ^ flip, 1, keepdims=False)
        out.append(part.reshape(rows_side.shape[0] // 4, rows_side.shape[1]))
    return out


def add_low(*terms):
    total = terms[0].astype(jnp.float32)
    for term in terms[1:]:
        total = total + term.astype(jnp.float32)
    return total


def z_scatter(own, z_index):
    def block(offset):
        return lax.dynamic_index_in_dim(own, jnp.clip(z_index + offset, 0, 3), 0, keepdims=False)

    up = down = None
    for step in range(1, 4):
        up_perm = [(i, i + 4) for i in range(16) if i // 4 <= step - 1 and i // 4 < 3]
        down_perm = [(i, i - 4) for i in range(16) if i // 4 >= 4 - step and i // 4 > 0]
        up_send, down_send = block(4 - step), block(step - 4)
        if up is not None:
            up_send = add_low(up_send, up).astype(jnp.bfloat16)
            down_send = add_low(down_send, down).astype(jnp.bfloat16)
        up = lax.ppermute(up_send, "dp", up_perm)
        down = lax.ppermute(down_send, "dp", down_perm)
    return add_low(block(0), up, down)


def plane_scatter(parts):
    own, to_x, to_y, to_d = parts
    half = own.shape[1] // 2
    low = jnp.bfloat16
    pieces = []
    for first, second, cut in ((1, 2, slice(0, half)), (2, 1, slice(half, 2 * half))):
        to_first = to_x if first == 1 else to_y
        to_second = to_y if first == 1 else to_x
        got_diag = lax.ppermute(to_d[:, cut], "dp", pairs(first))
        got_own = lax.ppermute(to_first[:, cut], "dp", pairs(first))
        passed = add_low(to_second[:, cut], got_diag).astype(low)
        got_last = lax.ppermute(passed, "dp", pairs(second))
        pieces.append(add_low(own[:, cut], got_own, got_last).astype(low))
    return jnp.concatenate(pieces, axis=1)


def weight_sum(rows_side, column_side, turned=False):
    if lax.axis_size("dp") == 16 and lax.axis_size("tensor") == 2:
        index = lax.axis_index("dp")
        turned_rows = rows_side.T
        parts = [
            product_plain(part, column_side).astype(jnp.bfloat16)
            for part in quarters(turned_rows, index % 4)
        ]
        own = plane_scatter(parts)
        own = own.reshape(4, own.shape[0] // 4, own.shape[1])
        total = z_scatter(own, index // 4)
    else:
        total = lax.psum_scatter(
            product_over_rows(rows_side, column_side).astype(jnp.bfloat16),
            "dp",
            scatter_dimension=0,
            tiled=True,
        ).astype(jnp.float32)
    return total.T if turned else total


def vector_sum(vectors):
    if lax.axis_size("dp") == 16:
        for mask in (1, 2, 4, 8):
            vectors = vectors + lax.ppermute(vectors, "dp", pairs(mask))
    else:
        vectors = lax.psum(vectors, "dp")
    share = vectors.shape[1] // (lax.axis_size("dp") * lax.axis_size("tensor"))
    index = lax.axis_index("dp") * lax.axis_size("tensor") + lax.axis_index("tensor")
    return lax.dynamic_slice_in_dim(vectors, index * share, share, 1)


def on_device(
    hidden_in,
    out_grad,
    prompt_states,
    row_split,
    prompt_len,
    gain_attn,
    bias_attn,
    gain_cross,
    bias_cross,
    gain_ff,
    bias_ff,
    w_query,
    w_key,
    w_value,
    w_out,
    c_query,
    c_key,
    c_value,
    c_out,
    w_gate,
    w_up,
    w_down,
):
    low = jnp.bfloat16
    frame_count = hidden_in.shape[0]
    positions = jnp.arange(frame_count, dtype=jnp.int32)
    split_here = row_split[0]
    row_ids = (positions >= split_here).astype(jnp.int32)
    tables = rotary_tables((positions - row_ids * split_here).astype(jnp.float32), w_query.shape[1])
    key_index = jnp.arange(2 * PROMPT, dtype=jnp.int32)
    key_rows = key_index // PROMPT
    key_live = key_index % PROMPT < jnp.where(key_rows == 0, prompt_len[0], prompt_len[1])
    self_ok = row_ids[:, None] == row_ids[None, :]
    cross_ok = (row_ids[:, None] == key_rows[None, :]) & key_live[None, :]

    normed, scaled_one, inverse_one = normalize(hidden_in, gain_attn, bias_attn)
    input_one = normed.astype(low)
    query_one = rotate(product_plain(input_one, w_query), tables).astype(low)
    key_one = rotate(product_plain(input_one, w_key), tables).astype(low)
    value_one = product_plain(input_one, w_value).astype(low)
    attended_one, logsum_one = attend_forward(query_one, heads_of(key_one), heads_of(value_one), self_ok)
    resid_one = hidden_in + swap_sum(product_plain(attended_one, w_out))

    normed, scaled_two, inverse_two = normalize(resid_one, gain_cross, bias_cross)
    input_two = normed.astype(low)
    cross_query = product_plain(input_two, c_query).astype(low)
    context_flat = prompt_states.reshape(2 * PROMPT, prompt_states.shape[2])
    cross_key = product_plain(context_flat, c_key).astype(low)
    cross_value = product_plain(context_flat, c_value).astype(low)
    attended_two, logsum_two = attend_forward(
        cross_query, heads_of(cross_key), heads_of(cross_value), cross_ok
    )
    resid_two = resid_one + swap_sum(product_plain(attended_two, c_out))

    normed, scaled_three, inverse_three = normalize(resid_two, gain_ff, bias_ff)
    input_three = normed.astype(low)
    gate_pre = product_plain(input_three, w_gate)
    up_pre = product_plain(input_three, w_up)
    sigmoid_gate = jax.nn.sigmoid(gate_pre)
    mixed_low = (gate_pre * sigmoid_gate * up_pre).astype(low)
    result = resid_two + swap_sum(product_plain(mixed_low, w_down))

    grad_ff_out = out_grad.astype(low)
    grad_w_down = weight_sum(grad_ff_out, mixed_low, True)
    grad_mixed = product_with_rows(grad_ff_out, w_down)
    grad_gate = (
        grad_mixed * up_pre * sigmoid_gate * (1.0 + gate_pre * (1.0 - sigmoid_gate))
    ).astype(low)
    grad_up = (grad_mixed * gate_pre * sigmoid_gate).astype(low)
    grad_w_gate = weight_sum(input_three, grad_gate)
    grad_w_up = weight_sum(input_three, grad_up)
    normed_grad_three = swap_sum(
        product_with_rows(grad_gate, w_gate) + product_with_rows(grad_up, w_up)
    )
    back_three, grad_gain_ff, grad_bias_ff = normalize_back(
        normed_grad_three, scaled_three, inverse_three, gain_ff
    )
    grad_two = out_grad + back_three
    grad_cross_out = grad_two.astype(low)
    grad_c_out = weight_sum(grad_cross_out, attended_two, True)
    grad_attended_two = product_with_rows(grad_cross_out, c_out).astype(low)
    cross_query_grad, cross_key_grad, cross_value_grad = attend_backward(
        cross_query,
        heads_of(cross_key),
        heads_of(cross_value),
        cross_ok,
        grad_attended_two,
        logsum_two,
    )
    cross_query_grad = cross_query_grad.astype(low)
    cross_key_grad = cross_key_grad.astype(low)
    cross_value_grad = cross_value_grad.astype(low)
    grad_c_query = weight_sum(input_two, cross_query_grad)
    grad_c_key = weight_sum(context_flat, cross_key_grad)
    grad_c_value = weight_sum(context_flat, cross_value_grad)
    normed_grad_two = swap_sum(product_with_rows(cross_query_grad, c_query))
    back_two, grad_gain_cross, grad_bias_cross = normalize_back(
        normed_grad_two, scaled_two, inverse_two, gain_cross
    )
    grad_one = grad_two + back_two
    grad_self_out = grad_one.astype(low)
    grad_w_out = weight_sum(grad_self_out, attended_one, True)
    grad_attended_one = product_with_rows(grad_self_out, w_out).astype(low)
    query_grad, key_grad, value_grad = attend_backward(
        query_one, heads_of(key_one), heads_of(value_one), self_ok, grad_attended_one, logsum_one
    )
    query_grad = rotate_back(query_grad, tables).astype(low)
    key_grad = rotate_back(key_grad, tables).astype(low)
    value_grad = value_grad.astype(low)
    grad_w_query = weight_sum(input_one, query_grad)
    grad_w_key = weight_sum(input_one, key_grad)
    grad_w_value = weight_sum(input_one, value_grad)
    normed_grad_one = swap_sum(
        product_with_rows(query_grad, w_query)
        + product_with_rows(key_grad, w_key)
        + product_with_rows(value_grad, w_value)
    )
    back_one, grad_gain_attn, grad_bias_attn = normalize_back(
        normed_grad_one, scaled_one, inverse_one, gain_attn
    )
    grad_hidden = grad_one + back_one
    vectors = vector_sum(
        jnp.stack(
            [
                grad_gain_attn,
                grad_bias_attn,
                grad_gain_cross,
                grad_bias_cross,
                grad_gain_ff,
                grad_bias_ff,
            ]
        )
    )
    return (
        result,
        grad_hidden,
        vectors[0],
        vectors[1],
        vectors[2],
        vectors[3],
        vectors[4],
        vectors[5],
        grad_w_query,
        grad_w_key,
        grad_w_value,
        grad_w_out,
        grad_c_query,
        grad_c_key,
        grad_c_value,
        grad_c_out,
        grad_w_gate,
        grad_w_up,
        grad_w_down,
    )


def solution(mesh):
    in_specs = (
        P("dp", None),
        P("dp", None),
        P("dp", None, None),
        P("dp"),
        P("dp"),
        P(),
        P(),
        P(),
        P(),
        P(),
        P(),
        P(None, "tensor"),
        P(None, "tensor"),
        P(None, "tensor"),
        P("tensor", None),
        P(None, "tensor"),
        P(None, "tensor"),
        P(None, "tensor"),
        P("tensor", None),
        P(None, "tensor"),
        P(None, "tensor"),
        P("tensor", None),
    )
    out_specs = (
        P("dp", None),
        P("dp", None),
        P(("dp", "tensor")),
        P(("dp", "tensor")),
        P(("dp", "tensor")),
        P(("dp", "tensor")),
        P(("dp", "tensor")),
        P(("dp", "tensor")),
        P("dp", "tensor"),
        P("dp", "tensor"),
        P("dp", "tensor"),
        P("tensor", "dp"),
        P("dp", "tensor"),
        P("dp", "tensor"),
        P("dp", "tensor"),
        P("tensor", "dp"),
        P("dp", "tensor"),
        P("dp", "tensor"),
        P("tensor", "dp"),
    )
    return jax.shard_map(
        on_device, mesh=mesh, in_specs=in_specs, out_specs=out_specs, check_vma=False
    )
```

time: 2100 us -> 1020 us (0.49)
  waiting for transfers between devices: 1640 us -> 290 us
  starting transfers between devices: 3.03 us -> 284 us
  matrix products: 243 us -> 204 us
  local copies, waits for them, and re-layouts: 70 us -> 97.8 us
    reduce_scatter x15 -> x0, waiting for transfers between devices: 1330 us -> none  [the longest x1 174 us: on_device(): lax.psum_scatter(grad_w_up.astype(jnp.bfloat16), 'dp', scatter_dimension=...]
    ppermute x0 -> x142, waiting for transfers between devices: none -> 290 us  [the longest x22 89.8 us: plane_scatter(): got_last = lax.ppermute(passed, 'dp', pairs(second))]
    unnamed x29 -> x0, waiting for transfers between devices: 284 us -> none
    ppermute x0 -> x142, starting transfers between devices: none -> 284 us  [the longest x33 173 us: z_scatter(): up = lax.ppermute(up_send, 'dp', up_perm)]
    dot_general x13 -> x0, matrix products: 61.2 us -> none  [the longest x11 51.1 us: product_over_rows(): lax.dot_general(left_side, right_side, (((0,), (0,)), ((), ())), preferre...]
    all_gather x8 -> x0, waiting for transfers between devices: 29.2 us -> none  [the longest x2 18.2 us: spread_result(): lax.all_gather(share_values.astype(jnp.bfloat16), 'tensor', axis=0, tiled...]
    dot_general x16 -> x55, matrix products: 84.7 us -> 108 us  [product_plain(): return jnp.dot(left_side, right_side, preferred_element_type=jnp.float32)]
    convert_element_type x23 -> x69, other arithmetic: 65.1 us -> 43 us  [the longest x22 10.6 us: plane_scatter(): passed = add_low(to_second[:, cut], got_diag).astype(low)]
  transfers between devices with their start and end apart: 26 -> 142, of which waited for: 18 -> 63; matrix products, arithmetic and copies ran while one was open for 13% -> 25% of each run, Pallas kernels for 0% -> 0%
where the time goes in v1:
time: 1020 us; the launch traced here: 1010 us
  waiting for transfers between devices  290 us (28%)
  starting transfers between devices  284 us (28%)
  matrix products  204 us (20%)
  other arithmetic  131 us (13%)
  local copies, waits for them, and re-layouts  97.8 us (10%)
    ppermute x33, starting transfers between devices, z_scatter(): up = lax.ppermute(up_send, 'dp', up_perm)  173 us
    dot_general x55, matrix products, product_plain(): return jnp.dot(left_side, right_side, preferred_element_type=jnp.float32)  108 us
    ppermute x22, waiting for transfers between devices, plane_scatter(): got_last = lax.ppermute(passed, 'dp', pairs(second))  89.8 us
    ppermute x22, waiting for transfers between devices, plane_scatter(): got_diag = lax.ppermute(to_d[:, cut], 'dp', pairs(first))  83.6 us
    ppermute x22, waiting for transfers between devices, plane_scatter(): got_own = lax.ppermute(to_first[:, cut], 'dp', pairs(first))  62.1 us
    dot_general x9, matrix products, product_with_rows(): lax.dot_general(left_side, right_side, (((1,), (1,)), ((), ())), preferre...  52.7 us
    ppermute x33, waiting for transfers between devices, z_scatter(): up = lax.ppermute(up_send, 'dp', up_perm)  38.2 us
    ppermute x33, starting transfers between devices, z_scatter(): down = lax.ppermute(down_send, 'dp', down_perm)  30.9 us
  transfers between devices with their start and end apart: 142, of which 63 were waited for; matrix products, arithmetic and copies ran while one was open for 25% of the time, Pallas kernels for 0%

profile of v1, /device:TPU:0, one launch (start us, length us, event | category | flops | bytes accessed | tf_op | source)
XLA Modules:
  0.0 1011.3 jit_solution(7208244338449354473)
XLA Ops:
  13.1 8.3 fusion.33
  24.3 4.5 convolution_convert_fusion.19
  39.0 3.8 fusion.62
  57.5 10.4 %fusion.190 = f32[512,3072]{1,0:T(8,128)} fusion(bf16[512,1536]{0,1:T(8,128)(2,1)} %copy.80, bf16[3072,1536]{1,0:T(8,128)(2,1)} %param.43), kind=kOutput, calls=%fused_computation.496 | convolution fusion | flops 4831838208 | bytes 17301504 | tf_op jit(solution)/shard_map/dot_general | solution.py:28
  108.9 11.1 %fusion.189 = f32[512,3072]{1,0:T(8,128)} fusion(bf16[1536,3072]{1,0:T(8,128)(2,1)} %param.42, f32[512,1536]{1,0:T(8,128)S(1)} %get-tuple-element.36, f32[1536]{0:T(1024)S(1)} %copy-done.166, f32[1536]{0:T(1024)S(1)} %copy-done.136, f32[512]{0:T(512)S(1)} %add_rsqrt_fusion, f32[512]{0:T(512)S(1)} %broadcast_multiply_fusion.6), kind=kOutput, calls=%fused_computation.495 | convolution fusion | flops 4835770368 | bytes 18890752 | tf_op jit(solution)/shard_map/dot_general | solution.py:18
  125.1 15.3 %multiply_convert_fusion.2 = (bf16[512,3072]{1,0:T(8,128)(2,1)}, bf16[512,3072]{1,0:T(8,128)(2,1)S(1)}, bf16[512,3072]{1,0:T(8,128)(2,1)}) fusion(f32[512,3072]{1,0:T(8,128)} %fusion.190, f32[512,3072]{1,0:T(8,128)} %fusion.189, bf16[1536,3072]{1,0:T(8,128)(2,1)} %param.41, f32[512,1536]{1,0:T(8,128)S(1)} %copy-done.13, f32[1536]{0:T(1024)} %param.32, ...), kind=kOutput, calls=%fused_computation.13 | convolution fusion | flops 4860936192 | bytes 34619392 | tf_op jit(solution)/shard_map/dot_general | solution.py:18
  140.5 4.5 convolution_convert_fusion.4
  152.0 9.7 fusion.191
  161.7 9.0 convolution_convert_fusion.15
  187.7 10.3 %fusion.13 = bf16[512,1536]{1,0:T(8,128)(2,1)S(1)} fusion(f32[512,1536]{1,0:T(8,128)} %fusion.191, bf16[512,3072]{1,0:T(8,128)(2,1)} %get-tuple-element.39, bf16[1536,3072]{1,0:T(8,128)(2,1)} %param.42), kind=kOutput, calls=%fused_computation.63 | convolution fusion | flops 4833411072 | bytes 17301504 | tf_op jit(solution)/shard_map/dot_general | solution.py:28
  220.4 10.1 collective-permute-done.134
  231.9 23.9 %collective-permute-done.122 = bf16[384,1536]{1,0:T(8,128)(2,1)S(1)} collective-permute-done((bf16[384,1536]{1,0:T(8,128)(2,1)S(1)}, bf16[384,1536]{1,0:T(8,128)(2,1)S(1)}, u32[]{:S(2)}, u32[]{:S(2)}) %collective-permute-start.122) | collective-permute-done | bytes 1179680 | tf_op jit(solution)/shard_map/ppermute | solution.py:197
  258.6 21.2 %collective-permute-done.110 = bf16[384,1536]{1,0:T(8,128)(2,1)S(1)} collective-permute-done((bf16[384,1536]{1,0:T(8,128)(2,1)S(1)}, bf16[384,1536]{1,0:T(8,128)(2,1)S(1)}, u32[]{:S(2)}, u32[]{:S(2)}) %collective-permute-start.110) | collective-permute-done | bytes 1179680 | tf_op jit(solution)/shard_map/ppermute | solution.py:197
  293.7 4.0 fusion.64
  297.8 6.9 multiply_reduce_fusion.1
  306.7 4.7 multiply_convert_fusion.1
  362.3 4.0 collective-permute-start.88
  368.6 4.4 collective-permute-start.76
  375.1 4.4 collective-permute-start.89
  381.5 4.3 collective-permute-start.77
  387.7 4.3 collective-permute-start.90
  400.4 26.3 %collective-permute-done.58 = bf16[384,384]{1,0:T(8,128)(2,1)S(1)} collective-permute-done((bf16[384,384]{1,0:T(8,128)(2,1)S(1)}, bf16[384,384]{1,0:T(8,128)(2,1)S(1)}, u32[]{:S(2)}, u32[]{:S(2)}) %collective-permute-start.58) | collective-permute-done | bytes 294944 | tf_op jit(solution)/shard_map/ppermute | solution.py:198
  432.7 7.5 collective-permute-done.63
  441.3 29.7 %collective-permute-done.60 = bf16[384,384]{1,0:T(8,128)(2,1)S(1)} collective-permute-done((bf16[384,384]{1,0:T(8,128)(2,1)S(1)}, bf16[384,384]{1,0:T(8,128)(2,1)S(1)}, u32[]{:S(2)}, u32[]{:S(2)}) %collective-permute-start.60) | collective-permute-done | bytes 294944 | tf_op jit(solution)/shard_map/ppermute | solution.py:200
  470.9 5.2 collective-permute-start.78
  478.2 5.4 collective-permute-start.100
  483.9 5.6 collective-permute-start.64
  497.1 21.9 %collective-permute-done.118 = bf16[384,1536]{1,0:T(8,128)(2,1)S(1)} collective-permute-done((bf16[384,1536]{1,0:T(8,128)(2,1)S(1)}, bf16[384,1536]{1,0:T(8,128)(2,1)S(1)}, u32[]{:S(2)}, u32[]{:S(2)}) %collective-permute-start.118) | collective-permute-done | bytes 1179680 | tf_op jit(solution)/shard_map/ppermute | solution.py:198
  521.1 23.2 %collective-permute-done.123 = bf16[384,1536]{1,0:T(8,128)(2,1)S(1)} collective-permute-done((bf16[384,1536]{1,0:T(8,128)(2,1)S(1)}, bf16[384,1536]{1,0:T(8,128)(2,1)S(1)}, u32[]{:S(2)}, u32[]{:S(2)}) %collective-permute-start.123) | collective-permute-done | bytes 1179680 | tf_op jit(solution)/shard_map/ppermute | solution.py:200
  549.5 10.1 %collective-permute-done.106 = bf16[384,1536]{1,0:T(8,128)(2,1)S(1)} collective-permute-done((bf16[384,1536]{1,0:T(8,128)(2,1)S(1)}, bf16[384,1536]{1,0:T(8,128)(2,1)S(1)}, u32[]{:S(2)}, u32[]{:S(2)}) %collective-permute-start.106) | collective-permute-done | bytes 1179680 | tf_op jit(solution)/shard_map/ppermute | solution.py:198
  561.3 11.0 %collective-permute-done.111 = bf16[384,1536]{1,0:T(8,128)(2,1)S(1)} collective-permute-done((bf16[384,1536]{1,0:T(8,128)(2,1)S(1)}, bf16[384,1536]{1,0:T(8,128)(2,1)S(1)}, u32[]{:S(2)}, u32[]{:S(2)}) %collective-permute-start.111) | collective-permute-done | bytes 1179680 | tf_op jit(solution)/shard_map/ppermute | solution.py:200
  588.5 4.8 collective-permute-done.102
  593.4 12.2 %collective-permute-start.66 = (bf16[96,768]{1,0:T(8,128)(2,1)S(1)}, bf16[96,768]{1,0:T(8,128)(2,1)S(1)}, u32[]{:S(2)}, u32[]{:S(2)}) collective-permute-start(bf16[96,768]{1,0:T(8,128)(2,1)S(1)} %get-tuple-element.111), channel_id=1, source_target_pairs={{0,8},{2,10},{4,12},{6,14},{8,16},{10,18},{12,20},{14,22},{16,24},... | collective-permute-start | bytes 442376 | tf_op jit(solution)/shard_map/ppermute | solution.py:184
  609.9 5.0 collective-permute-start.124
  617.5 4.2 collective-permute-start.112
  622.8 4.7 collective-permute-start.137
  638.4 6.5 fusion.59
  644.9 9.5 multiply_reduce_fusion
  654.4 7.1 multiply_convert_fusion
  670.5 7.8 fusion.36
  708.7 7.5 fusion.54
  729.6 9.3 fusion.84
  746.9 6.3 convolution_add_fusion.1
  773.5 6.1 collective-permute-done.23
  782.4 7.0 collective-permute-done.11
  809.6 4.0 collective-permute-done.48
  821.8 6.7 collective-permute-done.27
  831.6 5.8 collective-permute-start.138
  842.3 4.9 collective-permute-done.52
  847.1 4.4 collective-permute-start.40
  854.2 4.4 collective-permute-start.28
  861.2 4.4 collective-permute-start.16
  868.7 4.4 collective-permute-start.53
  877.3 4.4 collective-permute-start.41
  884.9 4.4 collective-permute-start.29
  893.6 4.4 collective-permute-start.17
  900.6 5.2 collective-permute-start.126
  909.2 11.9 %collective-permute-start.54 = (bf16[96,768]{1,0:T(8,128)(2,1)S(1)}, bf16[96,768]{1,0:T(8,128)(2,1)S(1)}, u32[]{:S(2)}, u32[]{:S(2)}) collective-permute-start(bf16[96,768]{1,0:T(8,128)(2,1)S(1)} %get-tuple-element.119), channel_id=1, source_target_pairs={{0,8},{2,10},{4,12},{6,14},{8,16},{10,18},{12,20},{14,22},{16,24},... | collective-permute-start | bytes 442376 | tf_op jit(solution)/shard_map/ppermute | solution.py:184
  926.0 22.3 %collective-permute-start.42 = (bf16[96,768]{1,0:T(8,128)(2,1)S(1)}, bf16[96,768]{1,0:T(8,128)(2,1)S(1)}, u32[]{:S(2)}, u32[]{:S(2)}) collective-permute-start(bf16[96,768]{1,0:T(8,128)(2,1)S(1)} %get-tuple-element.127), channel_id=1, source_target_pairs={{0,8},{2,10},{4,12},{6,14},{8,16},{10,18},{12,20},{14,22},{16,24},... | collective-permute-start | bytes 442376 | tf_op jit(solution)/shard_map/ppermute | solution.py:184
  952.9 4.5 collective-permute-start.30
  961.5 4.5 collective-permute-start.18
  969.3 5.4 collective-permute-start.114
  979.8 5.6 multiply_add_fusion
  1000.3 4.4 collective-permute-done.8
  (904 shorter events, 467.3 us)
Async XLA Ops:
  45.5 22.5 %collective-permute-start = (bf16[512,1536]{1,0:T(8,128)(2,1)}, bf16[512,1536]{1,0:T(8,128)(2,1)}, u32[]{:S(2)}, u32[]{:S(2)}) collective-permute-start(bf16[512,1536]{1,0:T(8,128)(2,1)} %convolution_convert_fusion.14), channel_id=1, source_target_pairs={{0,1},{1,0},{2,3},{3,2},{4,5},{5,4},{6,7},{7,6},{8,9},{9,8},{10,11... | collective-permute-start | bytes 4718600 | tf_op jit(solution)/shard_map/ppermute | solution.py:147
  86.3 17.6 %collective-permute-start.1 = (bf16[512,1536]{1,0:T(8,128)(2,1)}, bf16[512,1536]{1,0:T(8,128)(2,1)}, u32[]{:S(2)}, u32[]{:S(2)}) collective-permute-start(bf16[512,1536]{1,0:T(8,128)(2,1)} %convolution_convert_fusion.13), channel_id=1, source_target_pairs={{0,1},{1,0},{2,3},{3,2},{4,5},{5,4},{6,7},{7,6},{8,9},{9,8},{10,11... | collective-permute-start | bytes 4718600 | tf_op jit(solution)/shard_map/ppermute | solution.py:147
  173.8 42.6 %collective-permute-start.131 = (bf16[384,1536]{1,0:T(8,128)(2,1)}, bf16[384,1536]{1,0:T(8,128)(2,1)}, u32[]{:S(2)}, u32[]{:S(2)}) collective-permute-start(bf16[384,1536]{1,0:T(8,128)(2,1)} %get-tuple-element.49), channel_id=1, source_target_pairs={{0,2},{2,0},{4,6},{6,4},{8,10},{10,8},{12,14},{14,12},{16,18},{18,... | collective-permute-start | bytes 3538952 | tf_op jit(solution)/shard_map/ppermute | solution.py:197
  186.0 71.2 %collective-permute-start.119 = (bf16[384,1536]{1,0:T(8,128)(2,1)}, bf16[384,1536]{1,0:T(8,128)(2,1)S(1)}, u32[]{:S(2)}, u32[]{:S(2)}) collective-permute-start(bf16[384,1536]{1,0:T(8,128)(2,1)} %get-tuple-element.57), channel_id=1, source_target_pairs={{0,2},{2,0},{4,6},{6,4},{8,10},{10,8},{12,14},{14,12},{16,18},{18,... | collective-permute-start | bytes 3538952 | tf_op jit(solution)/shard_map/ppermute | solution.py:197
  201.6 29.0 %collective-permute-start.134 = (bf16[384,1536]{1,0:T(8,128)(2,1)S(1)}, bf16[384,1536]{1,0:T(8,128)(2,1)S(1)}, u32[]{:S(2)}, u32[]{:S(2)}) collective-permute-start(bf16[384,1536]{1,0:T(8,128)(2,1)S(1)} %copy-done.107), channel_id=1, source_target_pairs={{0,4},{2,6},{4,0},{6,2},{8,12},{10,14},{12,8},{14,10},{16,20},{18,... | collective-permute-start | bytes 3538952 | tf_op jit(solution)/shard_map/ppermute | solution.py:197
  203.7 52.1 %collective-permute-start.122 = (bf16[384,1536]{1,0:T(8,128)(2,1)S(1)}, bf16[384,1536]{1,0:T(8,128)(2,1)S(1)}, u32[]{:S(2)}, u32[]{:S(2)}) collective-permute-start(bf16[384,1536]{1,0:T(8,128)(2,1)S(1)} %copy-done.108), channel_id=1, source_target_pairs={{0,4},{2,6},{4,0},{6,2},{8,12},{10,14},{12,8},{14,10},{16,20},{18,... | collective-permute-start | bytes 3538952 | tf_op jit(solution)/shard_map/ppermute | solution.py:197
  212.2 67.6 %collective-permute-start.110 = (bf16[384,1536]{1,0:T(8,128)(2,1)S(1)}, bf16[384,1536]{1,0:T(8,128)(2,1)S(1)}, u32[]{:S(2)}, u32[]{:S(2)}) collective-permute-start(bf16[384,1536]{1,0:T(8,128)(2,1)S(1)} %copy-done.106), channel_id=1, source_target_pairs={{0,4},{2,6},{4,0},{6,2},{8,12},{10,14},{12,8},{14,10},{16,20},{18,... | collective-permute-start | bytes 3538952 | tf_op jit(solution)/shard_map/ppermute | solution.py:197
  216.3 64.9 %collective-permute-start.107 = (bf16[384,1536]{1,0:T(8,128)(2,1)S(1)}, bf16[384,1536]{1,0:T(8,128)(2,1)S(1)}, u32[]{:S(2)}, u32[]{:S(2)}) collective-permute-start(bf16[384,1536]{1,0:T(8,128)(2,1)S(1)} %copy-done.105), channel_id=1, source_target_pairs={{0,2},{2,0},{4,6},{6,4},{8,10},{10,8},{12,14},{14,12},{16,18},{18,... | collective-permute-start | bytes 3538952 | tf_op jit(solution)/shard_map/ppermute | solution.py:197
  230.5 52.0 %collective-permute-start.3 = (bf16[512,1536]{1,0:T(8,128)(2,1)S(1)}, bf16[512,1536]{1,0:T(8,128)(2,1)S(1)}, u32[]{:S(2)}, u32[]{:S(2)}) collective-permute-start(bf16[512,1536]{1,0:T(8,128)(2,1)S(1)} %fusion.13), channel_id=1, source_target_pairs={{0,1},{1,0},{2,3},{3,2},{4,5},{5,4},{6,7},{7,6},{8,9},{9,8},{10,11... | collective-permute-start | bytes 4718600 | tf_op jit(solution)/shard_map/ppermute | solution.py:147
  255.8 28.8 %collective-permute-start.2 = (bf16[512,1536]{1,0:T(8,128)(2,1)S(1)}, bf16[512,1536]{1,0:T(8,128)(2,1)S(1)}, u32[]{:S(2)}, u32[]{:S(2)}) collective-permute-start(bf16[512,1536]{1,0:T(8,128)(2,1)S(1)} %copy-done.75), channel_id=1, source_target_pairs={{0,1},{1,0},{2,3},{3,2},{4,5},{5,4},{6,7},{7,6},{8,9},{9,8},{10,11... | collective-permute-start | bytes 4718600 | tf_op jit(solution)/shard_map/ppermute | solution.py:147
  323.9 35.2 %collective-permute-start.98 = (bf16[384,384]{1,0:T(8,128)(2,1)S(1)}, bf16[384,384]{1,0:T(8,128)(2,1)S(1)}, u32[]{:S(2)}, u32[]{:S(2)}) collective-permute-start(bf16[384,384]{1,0:T(8,128)(2,1)S(1)} %get-tuple-element.110), channel_id=1, source_target_pairs={{0,4},{2,6},{4,0},{6,2},{8,12},{10,14},{12,8},{14,10},{16,20},{18,... | collective-permute-start | bytes 884744 | tf_op jit(solution)/shard_map/ppermute | solution.py:197
  327.8 17.8 %collective-permute-start.82 = (bf16[192,384]{1,0:T(8,128)(2,1)S(1)}, bf16[192,384]{1,0:T(8,128)(2,1)S(1)}, u32[]{:S(2)}, u32[]{:S(2)}) collective-permute-start(bf16[192,384]{1,0:T(8,128)(2,1)S(1)} %slice.517), channel_id=1, source_target_pairs={{0,2},{2,0},{4,6},{6,4},{8,10},{10,8},{12,14},{14,12},{16,18},{18,... | collective-permute-start | bytes 442376 | tf_op jit(solution)/shard_map/ppermute | solution.py:198
  329.9 17.1 %collective-permute-start.85 = (bf16[192,384]{1,0:T(8,128)(2,1)S(1)}, bf16[192,384]{1,0:T(8,128)(2,1)S(1)}, u32[]{:S(2)}, u32[]{:S(2)}) collective-permute-start(bf16[192,384]{1,0:T(8,128)(2,1)S(1)} %slice.521), channel_id=1, source_target_pairs={{0,4},{2,6},{4,0},{6,2},{8,12},{10,14},{12,8},{14,10},{16,20},{18,... | collective-permute-start | bytes 442376 | tf_op jit(solution)/shard_map/ppermute | solution.py:198
  353.8 40.3 %collective-permute-start.94 = (bf16[384,384]{1,0:T(8,128)(2,1)S(1)}, bf16[384,384]{1,0:T(8,128)(2,1)S(1)}, u32[]{:S(2)}, u32[]{:S(2)}) collective-permute-start(bf16[384,384]{1,0:T(8,128)(2,1)S(1)} %slice.525), channel_id=1, source_target_pairs={{0,2},{2,0},{4,6},{6,4},{8,10},{10,8},{12,14},{14,12},{16,18},{18,... | collective-permute-start | bytes 884744 | tf_op jit(solution)/shard_map/ppermute | solution.py:198
  355.8 39.5 %collective-permute-start.97 = (bf16[384,384]{1,0:T(8,128)(2,1)S(1)}, bf16[384,384]{1,0:T(8,128)(2,1)S(1)}, u32[]{:S(2)}, u32[]{:S(2)}) collective-permute-start(bf16[384,384]{1,0:T(8,128)(2,1)S(1)} %slice.529), channel_id=1, source_target_pairs={{0,4},{2,6},{4,0},{6,2},{8,12},{10,14},{12,8},{14,10},{16,20},{18,... | collective-permute-start | bytes 884744 | tf_op jit(solution)/shard_map/ppermute | solution.py:198
  359.1 33.6 %collective-permute-start.59 = (bf16[384,384]{1,0:T(8,128)(2,1)S(1)}, bf16[384,384]{1,0:T(8,128)(2,1)S(1)}, u32[]{:S(2)}, u32[]{:S(2)}) collective-permute-start(bf16[384,384]{1,0:T(8,128)(2,1)S(1)} %get-tuple-element.117), channel_id=1, source_target_pairs={{0,2},{2,0},{4,6},{6,4},{8,10},{10,8},{12,14},{14,12},{16,18},{18,... | collective-permute-start | bytes 884744 | tf_op jit(solution)/shard_map/ppermute | solution.py:197
  394.2 82.3 %collective-permute-start.130 = (bf16[384,1536]{1,0:T(8,128)(2,1)S(1)}, bf16[384,1536]{1,0:T(8,128)(2,1)S(1)}, u32[]{:S(2)}, u32[]{:S(2)}) collective-permute-start(bf16[384,1536]{1,0:T(8,128)(2,1)S(1)} %copy-done.100), channel_id=1, source_target_pairs={{0,2},{2,0},{4,6},{6,4},{8,10},{10,8},{12,14},{14,12},{16,18},{18,... | collective-permute-start | bytes 3538952 | tf_op jit(solution)/shard_map/ppermute | solution.py:198
  395.3 31.4 %collective-permute-start.58 = (bf16[384,384]{1,0:T(8,128)(2,1)S(1)}, bf16[384,384]{1,0:T(8,128)(2,1)S(1)}, u32[]{:S(2)}, u32[]{:S(2)}) collective-permute-start(bf16[384,384]{1,0:T(8,128)(2,1)S(1)} %slice.501), channel_id=1, source_target_pairs={{0,2},{2,0},{4,6},{6,4},{8,10},{10,8},{12,14},{14,12},{16,18},{18,... | collective-permute-start | bytes 884744 | tf_op jit(solution)/shard_map/ppermute | solution.py:198
  396.3 30.4 %collective-permute-start.61 = (bf16[384,384]{1,0:T(8,128)(2,1)S(1)}, bf16[384,384]{1,0:T(8,128)(2,1)S(1)}, u32[]{:S(2)}, u32[]{:S(2)}) collective-permute-start(bf16[384,384]{1,0:T(8,128)(2,1)S(1)} %slice.505), channel_id=1, source_target_pairs={{0,4},{2,6},{4,0},{6,2},{8,12},{10,14},{12,8},{14,10},{16,20},{18,... | collective-permute-start | bytes 884744 | tf_op jit(solution)/shard_map/ppermute | solution.py:198
  397.0 33.3 %collective-permute-start.99 = (bf16[384,384]{1,0:T(8,128)(2,1)S(1)}, bf16[384,384]{1,0:T(8,128)(2,1)S(1)}, u32[]{:S(2)}, u32[]{:S(2)}) collective-permute-start(bf16[384,384]{1,0:T(8,128)(2,1)S(1)} %add_convert_fusion.16), channel_id=1, source_target_pairs={{0,2},{2,0},{4,6},{6,4},{8,10},{10,8},{12,14},{14,12},{16,18},{18,... | collective-permute-start | bytes 884744 | tf_op jit(solution)/shard_map/ppermute | solution.py:200
  399.0 32.3 %collective-permute-start.96 = (bf16[384,384]{1,0:T(8,128)(2,1)S(1)}, bf16[384,384]{1,0:T(8,128)(2,1)S(1)}, u32[]{:S(2)}, u32[]{:S(2)}) collective-permute-start(bf16[384,384]{1,0:T(8,128)(2,1)S(1)} %add_convert_fusion.18), channel_id=1, source_target_pairs={{0,4},{2,6},{4,0},{6,2},{8,12},{10,14},{12,8},{14,10},{16,20},{18,... | collective-permute-start | bytes 884744 | tf_op jit(solution)/shard_map/ppermute | solution.py:200
  426.7 63.4 %collective-permute-start.133 = (bf16[384,1536]{1,0:T(8,128)(2,1)S(1)}, bf16[384,1536]{1,0:T(8,128)(2,1)S(1)}, u32[]{:S(2)}, u32[]{:S(2)}) collective-permute-start(bf16[384,1536]{1,0:T(8,128)(2,1)S(1)} %copy-done.99), channel_id=1, source_target_pairs={{0,4},{2,6},{4,0},{6,2},{8,12},{10,14},{12,8},{14,10},{16,20},{18,... | collective-permute-start | bytes 3538952 | tf_op jit(solution)/shard_map/ppermute | solution.py:198
  426.7 66.7 %collective-permute-start.132 = (bf16[384,1536]{1,0:T(8,128)(2,1)S(1)}, bf16[384,1536]{1,0:T(8,128)(2,1)S(1)}, u32[]{:S(2)}, u32[]{:S(2)}) collective-permute-start(bf16[384,1536]{1,0:T(8,128)(2,1)S(1)} %copy-done.88), channel_id=1, source_target_pairs={{0,4},{2,6},{4,0},{6,2},{8,12},{10,14},{12,8},{14,10},{16,20},{18,... | collective-permute-start | bytes 3538952 | tf_op jit(solution)/shard_map/ppermute | solution.py:200
  431.3 39.6 %collective-permute-start.60 = (bf16[384,384]{1,0:T(8,128)(2,1)S(1)}, bf16[384,384]{1,0:T(8,128)(2,1)S(1)}, u32[]{:S(2)}, u32[]{:S(2)}) collective-permute-start(bf16[384,384]{1,0:T(8,128)(2,1)S(1)} %add_convert_fusion.22), channel_id=1, source_target_pairs={{0,4},{2,6},{4,0},{6,2},{8,12},{10,14},{12,8},{14,10},{16,20},{18,... | collective-permute-start | bytes 884744 | tf_op jit(solution)/shard_map/ppermute | solution.py:200
  440.2 54.1 %collective-permute-start.135 = (bf16[384,1536]{1,0:T(8,128)(2,1)S(1)}, bf16[384,1536]{1,0:T(8,128)(2,1)S(1)}, u32[]{:S(2)}, u32[]{:S(2)}) collective-permute-start(bf16[384,1536]{1,0:T(8,128)(2,1)S(1)} %copy-done.87), channel_id=1, source_target_pairs={{0,2},{2,0},{4,6},{6,4},{8,10},{10,8},{12,14},{14,12},{16,18},{18,... | collective-permute-start | bytes 3538952 | tf_op jit(solution)/shard_map/ppermute | solution.py:200
  478.2 13.7 %collective-permute-start.100 = (bf16[96,768]{1,0:T(8,128)(2,1)S(1)}, bf16[96,768]{1,0:T(8,128)(2,1)S(1)}, u32[]{:S(2)}, u32[]{:S(2)}) collective-permute-start(bf16[96,768]{1,0:T(8,128)(2,1)S(1)} %get-tuple-element.105), channel_id=1, source_target_pairs={{0,8},{2,10},{4,12},{6,14},{1,9},{3,11},{5,13},{7,15}} | collective-permute-start | bytes 442376 | tf_op jit(solution)/shard_map/ppermute | solution.py:184
  490.1 28.9 %collective-permute-start.118 = (bf16[384,1536]{1,0:T(8,128)(2,1)S(1)}, bf16[384,1536]{1,0:T(8,128)(2,1)S(1)}, u32[]{:S(2)}, u32[]{:S(2)}) collective-permute-start(bf16[384,1536]{1,0:T(8,128)(2,1)S(1)} %copy-done.98), channel_id=1, source_target_pairs={{0,2},{2,0},{4,6},{6,4},{8,10},{10,8},{12,14},{14,12},{16,18},{18,... | collective-permute-start | bytes 3538952 | tf_op jit(solution)/shard_map/ppermute | solution.py:198
  491.9 28.9 %collective-permute-start.121 = (bf16[384,1536]{1,0:T(8,128)(2,1)S(1)}, bf16[384,1536]{1,0:T(8,128)(2,1)S(1)}, u32[]{:S(2)}, u32[]{:S(2)}) collective-permute-start(bf16[384,1536]{1,0:T(8,128)(2,1)S(1)} %copy-done.97), channel_id=1, source_target_pairs={{0,4},{2,6},{4,0},{6,2},{8,12},{10,14},{12,8},{14,10},{16,20},{18,... | collective-permute-start | bytes 3538952 | tf_op jit(solution)/shard_map/ppermute | solution.py:198
  491.9 52.4 %collective-permute-start.123 = (bf16[384,1536]{1,0:T(8,128)(2,1)S(1)}, bf16[384,1536]{1,0:T(8,128)(2,1)S(1)}, u32[]{:S(2)}, u32[]{:S(2)}) collective-permute-start(bf16[384,1536]{1,0:T(8,128)(2,1)S(1)} %copy-done.86), channel_id=1, source_target_pairs={{0,2},{2,0},{4,6},{6,4},{8,10},{10,8},{12,14},{14,12},{16,18},{18,... | collective-permute-start | bytes 3538952 | tf_op jit(solution)/shard_map/ppermute | solution.py:200
  493.4 52.6 %collective-permute-start.120 = (bf16[384,1536]{1,0:T(8,128)(2,1)S(1)}, bf16[384,1536]{1,0:T(8,128)(2,1)S(1)}, u32[]{:S(2)}, u32[]{:S(2)}) collective-permute-start(bf16[384,1536]{1,0:T(8,128)(2,1)S(1)} %copy-done.85), channel_id=1, source_target_pairs={{0,4},{2,6},{4,0},{6,2},{8,12},{10,14},{12,8},{14,10},{16,20},{18,... | collective-permute-start | bytes 3538952 | tf_op jit(solution)/shard_map/ppermute | solution.py:200
  494.4 65.3 %collective-permute-start.106 = (bf16[384,1536]{1,0:T(8,128)(2,1)S(1)}, bf16[384,1536]{1,0:T(8,128)(2,1)S(1)}, u32[]{:S(2)}, u32[]{:S(2)}) collective-permute-start(bf16[384,1536]{1,0:T(8,128)(2,1)S(1)} %copy-done.96), channel_id=1, source_target_pairs={{0,2},{2,0},{4,6},{6,4},{8,10},{10,8},{12,14},{14,12},{16,18},{18,... | collective-permute-start | bytes 3538952 | tf_op jit(solution)/shard_map/ppermute | solution.py:198
  519.0 41.6 %collective-permute-start.109 = (bf16[384,1536]{1,0:T(8,128)(2,1)S(1)}, bf16[384,1536]{1,0:T(8,128)(2,1)S(1)}, u32[]{:S(2)}, u32[]{:S(2)}) collective-permute-start(bf16[384,1536]{1,0:T(8,128)(2,1)S(1)} %copy-done.95), channel_id=1, source_target_pairs={{0,4},{2,6},{4,0},{6,2},{8,12},{10,14},{12,8},{14,10},{16,20},{18,... | collective-permute-start | bytes 3538952 | tf_op jit(solution)/shard_map/ppermute | solution.py:198
  520.8 51.5 %collective-permute-start.111 = (bf16[384,1536]{1,0:T(8,128)(2,1)S(1)}, bf16[384,1536]{1,0:T(8,128)(2,1)S(1)}, u32[]{:S(2)}, u32[]{:S(2)}) collective-permute-start(bf16[384,1536]{1,0:T(8,128)(2,1)S(1)} %copy-done.84), channel_id=1, source_target_pairs={{0,2},{2,0},{4,6},{6,4},{8,10},{10,8},{12,14},{14,12},{16,18},{18,... | collective-permute-start | bytes 3538952 | tf_op jit(solution)/shard_map/ppermute | solution.py:200
  544.3 29.6 %collective-permute-start.108 = (bf16[384,1536]{1,0:T(8,128)(2,1)S(1)}, bf16[384,1536]{1,0:T(8,128)(2,1)S(1)}, u32[]{:S(2)}, u32[]{:S(2)}) collective-permute-start(bf16[384,1536]{1,0:T(8,128)(2,1)S(1)} %copy-done.83), channel_id=1, source_target_pairs={{0,4},{2,6},{4,0},{6,2},{8,12},{10,14},{12,8},{14,10},{16,20},{18,... | collective-permute-start | bytes 3538952 | tf_op jit(solution)/shard_map/ppermute | solution.py:200
  546.0 84.0 %collective-permute-start.4 = (bf16[512,1536]{1,0:T(8,128)(2,1)S(1)}, bf16[512,1536]{1,0:T(8,128)(2,1)S(1)}, u32[]{:S(2)}, u32[]{:S(2)}) collective-permute-start(bf16[512,1536]{1,0:T(8,128)(2,1)S(1)} %convolution_convert_fusion.12), channel_id=1, source_target_pairs={{0,1},{1,0},{2,3},{3,2},{4,5},{5,4},{6,7},{7,6},{8,9},{9,8},{10,11... | collective-permute-start | bytes 4718600 | tf_op jit(solution)/shard_map/ppermute | solution.py:147
  559.7 19.0 %collective-permute-start.103 = (bf16[96,768]{1,0:T(8,128)(2,1)S(1)}, bf16[96,768]{1,0:T(8,128)(2,1)S(1)}, u32[]{:S(2)}, u32[]{:S(2)}) collective-permute-start(bf16[96,768]{1,0:T(8,128)(2,1)S(1)} %get-tuple-element.106), channel_id=1, source_target_pairs={{24,16},{26,18},{28,20},{30,22},{25,17},{27,19},{29,21},{31,23}} | collective-permute-start | bytes 442376 | tf_op jit(solution)/shard_map/ppermute | solution.py:185
  560.6 23.1 %collective-permute-start.67 = (bf16[96,768]{1,0:T(8,128)(2,1)S(1)}, bf16[96,768]{1,0:T(8,128)(2,1)S(1)}, u32[]{:S(2)}, u32[]{:S(2)}) collective-permute-start(bf16[96,768]{1,0:T(8,128)(2,1)S(1)} %get-tuple-element.114), channel_id=1, source_target_pairs={{24,16},{26,18},{28,20},{30,22},{25,17},{27,19},{29,21},{31,23}} | collective-permute-start | bytes 442376 | tf_op jit(solution)/shard_map/ppermute | solution.py:185
  578.7 38.8 %collective-permute-start.136 = (bf16[96,3072]{1,0:T(8,128)(2,1)S(1)}, bf16[96,3072]{1,0:T(8,128)(2,1)S(1)}, u32[]{:S(2)}, u32[]{:S(2)}) collective-permute-start(bf16[96,3072]{1,0:T(8,128)(2,1)S(1)} %get-tuple-element.45), channel_id=1, source_target_pairs={{0,8},{2,10},{4,12},{6,14},{1,9},{3,11},{5,13},{7,15}} | collective-permute-start | bytes 1769480 | tf_op jit(solution)/shard_map/ppermute | solution.py:184
  582.2 210.8 %collective-permute-start.139 = (bf16[96,3072]{1,0:T(8,128)(2,1)}, bf16[96,3072]{1,0:T(8,128)(2,1)}, u32[]{:S(2)}, u32[]{:S(2)}) collective-permute-start(bf16[96,3072]{1,0:T(8,128)(2,1)} %get-tuple-element.46), channel_id=1, source_target_pairs={{24,16},{26,18},{28,20},{30,22},{25,17},{27,19},{29,21},{31,23}} | collective-permute-start | bytes 1769480 | tf_op jit(solution)/shard_map/ppermute | solution.py:185
  587.2 19.5 %collective-permute-start.105 = (bf16[96,768]{1,0:T(8,128)(2,1)S(1)}, bf16[96,768]{1,0:T(8,128)(2,1)S(1)}, u32[]{:S(2)}, u32[]{:S(2)}) collective-permute-start(bf16[96,768]{1,0:T(8,128)(2,1)S(1)} %fusion.97), channel_id=1, source_target_pairs={{8,0},{10,2},{12,4},{14,6},{16,8},{18,10},{20,12},{22,14},{24,16},... | collective-permute-start | bytes 442376 | tf_op jit(solution)/shard_map/ppermute | solution.py:185
  593.4 16.5 %collective-permute-start.66 = (bf16[96,768]{1,0:T(8,128)(2,1)S(1)}, bf16[96,768]{1,0:T(8,128)(2,1)S(1)}, u32[]{:S(2)}, u32[]{:S(2)}) collective-permute-start(bf16[96,768]{1,0:T(8,128)(2,1)S(1)} %get-tuple-element.111), channel_id=1, source_target_pairs={{0,8},{2,10},{4,12},{6,14},{8,16},{10,18},{12,20},{14,22},{16,24},... | collective-permute-start | bytes 442376 | tf_op jit(solution)/shard_map/ppermute | solution.py:184
  609.9 12.9 %collective-permute-start.124 = (bf16[96,3072]{1,0:T(8,128)(2,1)S(1)}, bf16[96,3072]{1,0:T(8,128)(2,1)S(1)}, u32[]{:S(2)}, u32[]{:S(2)}) collective-permute-start(bf16[96,3072]{1,0:T(8,128)(2,1)S(1)} %get-tuple-element.53), channel_id=1, source_target_pairs={{0,8},{2,10},{4,12},{6,14},{1,9},{3,11},{5,13},{7,15}} | collective-permute-start | bytes 1769480 | tf_op jit(solution)/shard_map/ppermute | solution.py:184
  615.2 182.6 %collective-permute-start.127 = (bf16[96,3072]{1,0:T(8,128)(2,1)}, bf16[96,3072]{1,0:T(8,128)(2,1)}, u32[]{:S(2)}, u32[]{:S(2)}) collective-permute-start(bf16[96,3072]{1,0:T(8,128)(2,1)} %get-tuple-element.54), channel_id=1, source_target_pairs={{24,16},{26,18},{28,20},{30,22},{25,17},{27,19},{29,21},{31,23}} | collective-permute-start | bytes 1769480 | tf_op jit(solution)/shard_map/ppermute | solution.py:185
  622.8 172.3 %collective-permute-start.137 = (bf16[96,3072]{1,0:T(8,128)(2,1)}, bf16[96,3072]{1,0:T(8,128)(2,1)}, u32[]{:S(2)}, u32[]{:S(2)}) collective-permute-start(bf16[96,3072]{1,0:T(8,128)(2,1)} %fusion.69), channel_id=1, source_target_pairs={{0,8},{2,10},{4,12},{6,14},{8,16},{10,18},{12,20},{14,22},{1,9},{3... | collective-permute-start | bytes 1769480 | tf_op jit(solution)/shard_map/ppermute | solution.py:184
  742.7 15.1 %collective-permute-start.50 = (bf16[384,384]{1,0:T(8,128)(2,1)S(1)}, bf16[384,384]{1,0:T(8,128)(2,1)S(1)}, u32[]{:S(2)}, u32[]{:S(2)}) collective-permute-start(bf16[384,384]{1,0:T(8,128)(2,1)S(1)} %get-tuple-element.126), channel_id=1, source_target_pairs={{0,4},{2,6},{4,0},{6,2},{8,12},{10,14},{12,8},{14,10},{16,20},{18,... | collective-permute-start | bytes 884744 | tf_op jit(solution)/shard_map/ppermute | solution.py:197
  743.6 16.1 %collective-permute-start.47 = (bf16[384,384]{1,0:T(8,128)(2,1)S(1)}, bf16[384,384]{1,0:T(8,128)(2,1)S(1)}, u32[]{:S(2)}, u32[]{:S(2)}) collective-permute-start(bf16[384,384]{1,0:T(8,128)(2,1)S(1)} %get-tuple-element.125), channel_id=1, source_target_pairs={{0,2},{2,0},{4,6},{6,4},{8,10},{10,8},{12,14},{14,12},{16,18},{18,... | collective-permute-start | bytes 884744 | tf_op jit(solution)/shard_map/ppermute | solution.py:197
  781.6 21.1 %collective-permute-start.115 = (bf16[96,3072]{1,0:T(8,128)(2,1)S(1)}, bf16[96,3072]{1,0:T(8,128)(2,1)S(1)}, u32[]{:S(2)}, u32[]{:S(2)}) collective-permute-start(bf16[96,3072]{1,0:T(8,128)(2,1)S(1)} %copy-done.114), channel_id=1, source_target_pairs={{24,16},{26,18},{28,20},{30,22},{25,17},{27,19},{29,21},{31,23}} | collective-permute-start | bytes 1769480 | tf_op jit(solution)/shard_map/ppermute | solution.py:185
  793.0 13.6 %collective-permute-start.113 = (bf16[96,3072]{1,0:T(8,128)(2,1)S(1)}, bf16[96,3072]{1,0:T(8,128)(2,1)S(1)}, u32[]{:S(2)}, u32[]{:S(2)}) collective-permute-start(bf16[96,3072]{1,0:T(8,128)(2,1)S(1)} %copy-done.115), channel_id=1, source_target_pairs={{0,8},{2,10},{4,12},{6,14},{8,16},{10,18},{12,20},{14,22},{1,9},{3... | collective-permute-start | bytes 1769480 | tf_op jit(solution)/shard_map/ppermute | solution.py:184
  802.8 12.2 %collective-permute-start.34 = (bf16[384,384]{1,0:T(8,128)(2,1)S(1)}, bf16[384,384]{1,0:T(8,128)(2,1)S(1)}, u32[]{:S(2)}, u32[]{:S(2)}) collective-permute-start(bf16[384,384]{1,0:T(8,128)(2,1)S(1)} %slice.485), channel_id=1, source_target_pairs={{0,2},{2,0},{4,6},{6,4},{8,10},{10,8},{12,14},{14,12},{16,18},{18,... | collective-permute-start | bytes 884744 | tf_op jit(solution)/shard_map/ppermute | solution.py:198
  815.9 15.0 %collective-permute-start.10 = (bf16[384,384]{1,0:T(8,128)(2,1)S(1)}, bf16[384,384]{1,0:T(8,128)(2,1)S(1)}, u32[]{:S(2)}, u32[]{:S(2)}) collective-permute-start(bf16[384,384]{1,0:T(8,128)(2,1)S(1)} %slice.469), channel_id=1, source_target_pairs={{0,2},{2,0},{4,6},{6,4},{8,10},{10,8},{12,14},{14,12},{16,18},{18,... | collective-permute-start | bytes 884744 | tf_op jit(solution)/shard_map/ppermute | solution.py:198
  821.8 156.2 %collective-permute-start.5 = (bf16[512,1536]{1,0:T(8,128)(2,1)S(1)}, bf16[512,1536]{1,0:T(8,128)(2,1)S(1)}, u32[]{:S(2)}, u32[]{:S(2)}) collective-permute-start(bf16[512,1536]{1,0:T(8,128)(2,1)S(1)} %fusion.14), channel_id=1, source_target_pairs={{0,1},{1,0},{2,3},{3,2},{4,5},{5,4},{6,7},{7,6},{8,9},{9,8},{10,11... | collective-permute-start | bytes 4718600 | tf_op jit(solution)/shard_map/ppermute | solution.py:147
  830.9 75.0 %collective-permute-start.140 = (bf16[96,3072]{1,0:T(8,128)(2,1)S(1)}, bf16[96,3072]{1,0:T(8,128)(2,1)S(1)}, u32[]{:S(2)}, u32[]{:S(2)}) collective-permute-start(bf16[96,3072]{1,0:T(8,128)(2,1)S(1)} %get-tuple-element.44), channel_id=1, source_target_pairs={{16,8},{18,10},{20,12},{22,14},{24,16},{26,18},{28,20},{30,22},{17... | collective-permute-start | bytes 1769480 | tf_op jit(solution)/shard_map/ppermute | solution.py:185
  831.6 155.2 %collective-permute-start.138 = (bf16[96,3072]{1,0:T(8,128)(2,1)S(1)}, bf16[96,3072]{1,0:T(8,128)(2,1)}, u32[]{:S(2)}, u32[]{:S(2)}) collective-permute-start(bf16[96,3072]{1,0:T(8,128)(2,1)S(1)} %get-tuple-element.43), channel_id=1, source_target_pairs={{0,8},{2,10},{4,12},{6,14},{8,16},{10,18},{12,20},{14,22},{16,24},... | collective-permute-start | bytes 1769480 | tf_op jit(solution)/shard_map/ppermute | solution.py:184
  841.2 32.0 %collective-permute-start.55 = (bf16[96,768]{1,0:T(8,128)(2,1)S(1)}, bf16[96,768]{1,0:T(8,128)(2,1)S(1)}, u32[]{:S(2)}, u32[]{:S(2)}) collective-permute-start(bf16[96,768]{1,0:T(8,128)(2,1)S(1)} %get-tuple-element.122), channel_id=1, source_target_pairs={{24,16},{26,18},{28,20},{30,22},{25,17},{27,19},{29,21},{31,23}} | collective-permute-start | bytes 442376 | tf_op jit(solution)/shard_map/ppermute | solution.py:185
  900.6 95.6 %collective-permute-start.126 = (bf16[96,3072]{1,0:T(8,128)(2,1)S(1)}, bf16[96,3072]{1,0:T(8,128)(2,1)}, u32[]{:S(2)}, u32[]{:S(2)}) collective-permute-start(bf16[96,3072]{1,0:T(8,128)(2,1)S(1)} %get-tuple-element.51), channel_id=1, source_target_pairs={{0,8},{2,10},{4,12},{6,14},{8,16},{10,18},{12,20},{14,22},{16,24},... | collective-permute-start | bytes 1769480 | tf_op jit(solution)/shard_map/ppermute | solution.py:184
  907.6 14.6 %collective-permute-start.56 = (bf16[96,768]{1,0:T(8,128)(2,1)S(1)}, bf16[96,768]{1,0:T(8,128)(2,1)S(1)}, u32[]{:S(2)}, u32[]{:S(2)}) collective-permute-start(bf16[96,768]{1,0:T(8,128)(2,1)S(1)} %get-tuple-element.120), channel_id=1, source_target_pairs={{16,8},{18,10},{20,12},{22,14},{24,16},{26,18},{28,20},{30,22},{17... | collective-permute-start | bytes 442376 | tf_op jit(solution)/shard_map/ppermute | solution.py:185
  909.2 16.8 %collective-permute-start.54 = (bf16[96,768]{1,0:T(8,128)(2,1)S(1)}, bf16[96,768]{1,0:T(8,128)(2,1)S(1)}, u32[]{:S(2)}, u32[]{:S(2)}) collective-permute-start(bf16[96,768]{1,0:T(8,128)(2,1)S(1)} %get-tuple-element.119), channel_id=1, source_target_pairs={{0,8},{2,10},{4,12},{6,14},{8,16},{10,18},{12,20},{14,22},{16,24},... | collective-permute-start | bytes 442376 | tf_op jit(solution)/shard_map/ppermute | solution.py:184
  924.7 26.2 %collective-permute-start.57 = (bf16[96,768]{1,0:T(8,128)(2,1)S(1)}, bf16[96,768]{1,0:T(8,128)(2,1)S(1)}, u32[]{:S(2)}, u32[]{:S(2)}) collective-permute-start(bf16[96,768]{1,0:T(8,128)(2,1)S(1)} %fusion.108), channel_id=1, source_target_pairs={{8,0},{10,2},{12,4},{14,6},{16,8},{18,10},{20,12},{22,14},{24,16},... | collective-permute-start | bytes 442376 | tf_op jit(solution)/shard_map/ppermute | solution.py:185
  926.0 26.9 %collective-permute-start.42 = (bf16[96,768]{1,0:T(8,128)(2,1)S(1)}, bf16[96,768]{1,0:T(8,128)(2,1)S(1)}, u32[]{:S(2)}, u32[]{:S(2)}) collective-permute-start(bf16[96,768]{1,0:T(8,128)(2,1)S(1)} %get-tuple-element.127), channel_id=1, source_target_pairs={{0,8},{2,10},{4,12},{6,14},{8,16},{10,18},{12,20},{14,22},{16,24},... | collective-permute-start | bytes 442376 | tf_op jit(solution)/shard_map/ppermute | solution.py:184
  969.3 38.7 %collective-permute-start.114 = (bf16[96,3072]{1,0:T(8,128)(2,1)}, bf16[96,3072]{1,0:T(8,128)(2,1)}, u32[]{:S(2)}, u32[]{:S(2)}) collective-permute-start(bf16[96,3072]{1,0:T(8,128)(2,1)} %get-tuple-element.59), channel_id=1, source_target_pairs={{0,8},{2,10},{4,12},{6,14},{8,16},{10,18},{12,20},{14,22},{16,24},... | collective-permute-start | bytes 1769480 | tf_op jit(solution)/shard_map/ppermute | solution.py:184
  975.9 12.5 %collective-permute-start.141 = (bf16[96,3072]{1,0:T(8,128)(2,1)}, bf16[96,3072]{1,0:T(8,128)(2,1)S(1)}, u32[]{:S(2)}, u32[]{:S(2)}) collective-permute-start(bf16[96,3072]{1,0:T(8,128)(2,1)} %fusion.68), channel_id=1, source_target_pairs={{8,0},{10,2},{12,4},{14,6},{16,8},{18,10},{20,12},{22,14},{24,16},... | collective-permute-start | bytes 1769480 | tf_op jit(solution)/shard_map/ppermute | solution.py:185
  985.5 12.4 %collective-permute-start.129 = (bf16[96,3072]{1,0:T(8,128)(2,1)S(1)}, bf16[96,3072]{1,0:T(8,128)(2,1)S(1)}, u32[]{:S(2)}, u32[]{:S(2)}) collective-permute-start(bf16[96,3072]{1,0:T(8,128)(2,1)S(1)} %copy-done.117), channel_id=1, source_target_pairs={{8,0},{10,2},{12,4},{14,6},{16,8},{18,10},{20,12},{22,14},{24,16},... | collective-permute-start | bytes 1769480 | tf_op jit(solution)/shard_map/ppermute | solution.py:185
  986.8 21.2 %collective-permute-start.117 = (bf16[96,3072]{1,0:T(8,128)(2,1)}, bf16[96,3072]{1,0:T(8,128)(2,1)S(1)}, u32[]{:S(2)}, u32[]{:S(2)}) collective-permute-start(bf16[96,3072]{1,0:T(8,128)(2,1)} %fusion.79), channel_id=1, source_target_pairs={{8,0},{10,2},{12,4},{14,6},{16,8},{18,10},{20,12},{22,14},{24,16},... | collective-permute-start | bytes 1769480 | tf_op jit(solution)/shard_map/ppermute | solution.py:185
  992.5 12.2 %collective-permute-start.8 = (f32[6,1536]{1,0:T(8,128)S(1)}, f32[6,1536]{1,0:T(8,128)S(1)}, u32[]{:S(2)}, u32[]{:S(2)}) collective-permute-start(f32[6,1536]{1,0:T(8,128)S(1)} %add.895), channel_id=1, source_target_pairs={{0,8},{2,10},{4,12},{6,14},{8,0},{10,2},{12,4},{14,6},{16,24},{18,... | collective-permute-start | bytes 110600 | tf_op jit(solution)/shard_map/ppermute | solution.py:229
  (265 other events, 3094.0 us)

commit v2 on v1

--- a/solution.py
+++ b/solution.py
@@ -3,6 +3,8 @@
 import jax
 import jax.numpy as jnp
 from jax import lax
+from jax.experimental import pallas as pl
+from jax.experimental.pallas import tpu as pltpu
 from jax.sharding import PartitionSpec as P
 
 PROMPT = 128
@@ -153,15 +155,6 @@
     return [(i, i ^ mask) for i in range(16)]
 
 
-def quarters(rows_side, mine):
-    blocks = rows_side.reshape(4, 4, rows_side.shape[0] // 16, rows_side.shape[1])
-    out = []
-    for flip in range(4):
-        part = lax.dynamic_index_in_dim(blocks, mine ^ flip, 1, keepdims=False)
-        out.append(part.reshape(rows_side.shape[0] // 4, rows_side.shape[1]))
-    return out
-
-
 def add_low(*terms):
     total = terms[0].astype(jnp.float32)
     for term in terms[1:]:
@@ -186,41 +179,178 @@
     return add_low(block(0), up, down)
 
 
-def plane_scatter(parts):
-    own, to_x, to_y, to_d = parts
-    half = own.shape[1] // 2
+def plane_scatter(parts, first):
     low = jnp.bfloat16
-    pieces = []
-    for first, second, cut in ((1, 2, slice(0, half)), (2, 1, slice(half, 2 * half))):
-        to_first = to_x if first == 1 else to_y
-        to_second = to_y if first == 1 else to_x
-        got_diag = lax.ppermute(to_d[:, cut], "dp", pairs(first))
-        got_own = lax.ppermute(to_first[:, cut], "dp", pairs(first))
-        passed = add_low(to_second[:, cut], got_diag).astype(low)
-        got_last = lax.ppermute(passed, "dp", pairs(second))
-        pieces.append(add_low(own[:, cut], got_own, got_last).astype(low))
-    return jnp.concatenate(pieces, axis=1)
-
-
-def weight_sum(rows_side, column_side, turned=False):
-    if lax.axis_size("dp") == 16 and lax.axis_size("tensor") == 2:
-        index = lax.axis_index("dp")
-        turned_rows = rows_side.T
-        parts = [
-            product_plain(part, column_side).astype(jnp.bfloat16)
-            for part in quarters(turned_rows, index % 4)
-        ]
-        own = plane_scatter(parts)
-        own = own.reshape(4, own.shape[0] // 4, own.shape[1])
-        total = z_scatter(own, index // 4)
-    else:
-        total = lax.psum_scatter(
-            product_over_rows(rows_side, column_side).astype(jnp.bfloat16),
-            "dp",
-            scatter_dimension=0,
-            tiled=True,
-        ).astype(jnp.float32)
-    return total.T if turned else total
+    got_diag = lax.ppermute(parts[3], "dp", pairs(first))
+    got_own = lax.ppermute(parts[first], "dp", pairs(first))
+    passed = add_low(parts[3 - first], got_diag).astype(low)
+    got_last = lax.ppermute(passed, "dp", pairs(3 - first))
+    return add_low(parts[0], got_own, got_last).astype(low)
+
+
+def quarter_products(rows_side, column_side, mine):
+    turned = rows_side.T.reshape(4, 4, rows_side.shape[1] // 16, rows_side.shape[0])
+    out = []
+    for flip in range(4):
+        part = lax.dynamic_index_in_dim(turned, mine ^ flip, 1, keepdims=False)
+        product = product_plain(part.reshape(-1, part.shape[2]), column_side)
+        out.append(product.astype(jnp.bfloat16).reshape(4, -1, column_side.shape[1]))
+    return out
+
+
+def stacked(*products):
+    return [jnp.concatenate(part, axis=1) for part in zip(*products)]
+
+
+def plane_gather(own_half, mask_list=(1, 2, 3)):
+    got = [lax.ppermute(own_half, "dp", pairs(mask)) for mask in mask_list]
+    other = [lax.ppermute(part, "tensor", [(0, 1), (1, 0)]) for part in got]
+    return got + other
+
+
+def ff_parts(gate, up, grad_mixed):
+    sig = 1.0 / (1.0 + jnp.exp(-gate))
+    act = gate * sig
+    low = jnp.bfloat16
+    return (
+        (act * up).astype(low),
+        (grad_mixed * up * sig * (1.0 + gate * (1.0 - sig))).astype(low),
+        (grad_mixed * act).astype(low),
+    )
+
+
+def ff_kernel(in_ref, out_ref, gate_ref, up_ref, down_ref, sum_ref, back_ref, sum_acc, back_acc):
+    step = pl.program_id(0)
+
+    @pl.when(step == 0)
+    def _():
+        sum_acc[...] = jnp.zeros_like(sum_acc)
+        back_acc[...] = jnp.zeros_like(back_acc)
+
+    normed = in_ref[...]
+    mixed, grad_gate, grad_up = ff_parts(
+        product_plain(normed, gate_ref[...]),
+        product_plain(normed, up_ref[...]),
+        product_with_rows(out_ref[...], down_ref[...]),
+    )
+    sum_acc[...] += product_plain(mixed, down_ref[...])
+    back_acc[...] += product_with_rows(grad_gate, gate_ref[...]) + product_with_rows(
+        grad_up, up_ref[...]
+    )
+
+    @pl.when(step == pl.num_programs(0) - 1)
+    def _():
+        sum_ref[...] = sum_acc[...].astype(sum_ref.dtype)
+        back_ref[...] = back_acc[...].astype(back_ref.dtype)
+
+
+def ff_both(normed, grad_out, w_gate, w_up, w_down):
+    frames, width = normed.shape
+    units = w_gate.shape[1]
+    tile = min(512, units)
+    while units % tile:
+        tile -= 128
+    whole = pl.BlockSpec((frames, width), lambda j: (0, 0))
+    column = pl.BlockSpec((width, tile), lambda j: (0, j))
+    return pl.pallas_call(
+        ff_kernel,
+        grid=(units // tile,),
+        in_specs=[whole, whole, column, column, pl.BlockSpec((tile, width), lambda j: (j, 0))],
+        out_specs=[whole, whole],
+        out_shape=[jax.ShapeDtypeStruct((frames, width), jnp.bfloat16)] * 2,
+        scratch_shapes=[pltpu.VMEM((frames, width), jnp.float32)] * 2,
+        compiler_params=pltpu.CompilerParams(vmem_limit_bytes=44 * 2**20),
+        cost_estimate=pl.CostEstimate(
+            flops=12 * frames * width * units,
+            bytes_accessed=6 * width * units + 8 * frames * width,
+            transcendentals=frames * units,
+        ),
+    )(normed, grad_out, w_gate, w_up, w_down)
+
+
+def share_kernel(_, in_ref, out_ref, gate_ref, up_ref, down_ref, grad_ref, acc):
+    step = pl.program_id(0)
+    normed, grad_out = in_ref[...], out_ref[...]
+    mixed, grad_gate, grad_up = ff_parts(
+        product_plain(normed, gate_ref[...]),
+        product_plain(normed, up_ref[...]),
+        product_with_rows(grad_out, down_ref[...]),
+    )
+    fresh = (
+        product_over_rows(grad_out, mixed),
+        product_over_rows(normed, grad_gate),
+        product_over_rows(normed, grad_up),
+    )
+    for index, term in enumerate(fresh):
+
+        @pl.when(step == 0)
+        def _():
+            acc[index] = term
+
+        @pl.when(step != 0)
+        def _():
+            acc[index] += term
+
+    @pl.when(step == pl.num_programs(0) - 1)
+    def _():
+        rows = grad_ref.shape[2]
+        for block in range(grad_ref.shape[0]):
+            for index in range(3):
+                grad_ref[block, index] = acc[index, block * rows : (block + 1) * rows].astype(
+                    grad_ref.dtype
+                )
+
+
+def ff_share(normed, grad_out, w_gate, w_up, w_down, first_tile, tile):
+    frames, width = normed.shape
+    chunk = 512
+    rows = pl.BlockSpec((chunk, width), lambda j, first: (j, 0))
+    column = pl.BlockSpec((width, tile), lambda j, first: (0, first[0]))
+    return pl.pallas_call(
+        share_kernel,
+        grid_spec=pltpu.PrefetchScalarGridSpec(
+            num_scalar_prefetch=1,
+            grid=(frames // chunk,),
+            in_specs=[
+                rows,
+                rows,
+                column,
+                column,
+                pl.BlockSpec((tile, width), lambda j, first: (first[0], 0)),
+            ],
+            out_specs=pl.BlockSpec((4, 3, width // 4, tile), lambda j, first: (0, 0, 0, 0)),
+            scratch_shapes=[pltpu.VMEM((3, width, tile), jnp.float32)],
+        ),
+        out_shape=jax.ShapeDtypeStruct((4, 3, width // 4, tile), jnp.bfloat16),
+        compiler_params=pltpu.CompilerParams(vmem_limit_bytes=44 * 2**20),
+        cost_estimate=pl.CostEstimate(
+            flops=12 * frames * width * tile,
+            bytes_accessed=4 * frames * width + 12 * width * tile,
+            transcendentals=frames * tile,
+        ),
+    )(first_tile.reshape(1), normed, grad_out, w_gate, w_up, w_down)
+
+
+def spread_units(mine, plane, parts=3):
+    blocks = mine.reshape(3, 4, mine.shape[1] // 4, mine.shape[2]).astype(jnp.bfloat16)
+    got = []
+    for flip in range(4):
+        part = lax.dynamic_index_in_dim(blocks, plane ^ flip, 1, keepdims=False)
+        got.append(part if flip == 0 else lax.ppermute(part, "dp", pairs(flip)))
+    got = jnp.stack(got)
+    columns = [
+        lax.dynamic_index_in_dim(got, plane ^ owner, 0, keepdims=False) for owner in range(4)
+    ]
+    return jnp.concatenate(columns, axis=2).astype(jnp.float32)
+
+
+def generic_sum(rows_side, column_side):
+    return lax.psum_scatter(
+        product_over_rows(rows_side, column_side).astype(jnp.bfloat16),
+        "dp",
+        scatter_dimension=0,
+        tiled=True,
+    ).astype(jnp.float32)
 
 
 def vector_sum(vectors):
@@ -259,7 +389,18 @@
     w_down,
 ):
     low = jnp.bfloat16
+    known = lax.axis_size("dp") == 16 and lax.axis_size("tensor") == 2
     frame_count = hidden_in.shape[0]
+    plane, level = lax.axis_index("dp") % 4, lax.axis_index("dp") // 4
+    grad_ff_out = out_grad.astype(low)
+
+    def half_of(values):
+        return lax.dynamic_slice_in_dim(
+            values, lax.axis_index("tensor") * (frame_count // 2), frame_count // 2, 0
+        )
+
+    if known:
+        frames_out = jnp.concatenate([grad_ff_out, *plane_gather(half_of(grad_ff_out))])
     positions = jnp.arange(frame_count, dtype=jnp.int32)
     split_here = row_split[0]
     row_ids = (positions >= split_here).astype(jnp.int32)
@@ -291,30 +432,35 @@
 
     normed, scaled_three, inverse_three = normalize(resid_two, gain_ff, bias_ff)
     input_three = normed.astype(low)
-    gate_pre = product_plain(input_three, w_gate)
-    up_pre = product_plain(input_three, w_up)
-    sigmoid_gate = jax.nn.sigmoid(gate_pre)
-    mixed_low = (gate_pre * sigmoid_gate * up_pre).astype(low)
-    result = resid_two + swap_sum(product_plain(mixed_low, w_down))
-
-    grad_ff_out = out_grad.astype(low)
-    grad_w_down = weight_sum(grad_ff_out, mixed_low, True)
-    grad_mixed = product_with_rows(grad_ff_out, w_down)
-    grad_gate = (
-        grad_mixed * up_pre * sigmoid_gate * (1.0 + gate_pre * (1.0 - sigmoid_gate))
-    ).astype(low)
-    grad_up = (grad_mixed * gate_pre * sigmoid_gate).astype(low)
-    grad_w_gate = weight_sum(input_three, grad_gate)
-    grad_w_up = weight_sum(input_three, grad_up)
-    normed_grad_three = swap_sum(
-        product_with_rows(grad_gate, w_gate) + product_with_rows(grad_up, w_up)
-    )
+    if known:
+        frames_in = jnp.concatenate([input_three, *plane_gather(half_of(input_three))])
+    sum_part, back_part = ff_both(input_three, grad_ff_out, w_gate, w_up, w_down)
+    result = resid_two + swap_sum(sum_part)
+    normed_grad_three = swap_sum(back_part)
+    if known:
+        units = w_gate.shape[1] // 4
+        tile = 256
+        shares = []
+        for part in range(units // tile):
+            own = ff_share(
+                frames_in, frames_out, w_gate, w_up, w_down, plane * (units // tile) + part, tile
+            )
+            shares.append(z_scatter(own, level))
+        spread = spread_units(jnp.concatenate(shares, axis=2), plane)
+        grad_w_down, grad_w_gate, grad_w_up = spread[0].T, spread[1], spread[2]
+    else:
+        gate_pre = product_plain(input_three, w_gate)
+        up_pre = product_plain(input_three, w_up)
+        grad_mixed = product_with_rows(grad_ff_out, w_down)
+        mixed, grad_gate, grad_up = ff_parts(gate_pre, up_pre, grad_mixed)
+        grad_w_down = generic_sum(grad_ff_out, mixed).T
+        grad_w_gate = generic_sum(input_three, grad_gate)
+        grad_w_up = generic_sum(input_three, grad_up)
     back_three, grad_gain_ff, grad_bias_ff = normalize_back(
         normed_grad_three, scaled_three, inverse_three, gain_ff
     )
     grad_two = out_grad + back_three
     grad_cross_out = grad_two.astype(low)
-    grad_c_out = weight_sum(grad_cross_out, attended_two, True)
     grad_attended_two = product_with_rows(grad_cross_out, c_out).astype(low)
     cross_query_grad, cross_key_grad, cross_value_grad = attend_backward(
         cross_query,
@@ -327,16 +473,41 @@
     cross_query_grad = cross_query_grad.astype(low)
     cross_key_grad = cross_key_grad.astype(low)
     cross_value_grad = cross_value_grad.astype(low)
-    grad_c_query = weight_sum(input_two, cross_query_grad)
-    grad_c_key = weight_sum(context_flat, cross_key_grad)
-    grad_c_value = weight_sum(context_flat, cross_value_grad)
+    if known:
+        context_part = quarter_products(
+            context_flat, jnp.concatenate([cross_key_grad, cross_value_grad], axis=1), plane
+        )
+        width = cross_key_grad.shape[1]
+        first = plane_scatter(
+            stacked(
+                quarter_products(grad_cross_out, attended_two, plane),
+                [part[..., :width] for part in context_part],
+            ),
+            1,
+        )
+        second = plane_scatter(
+            stacked(
+                quarter_products(input_two, cross_query_grad, plane),
+                [part[..., width:] for part in context_part],
+            ),
+            2,
+        )
+        sums = z_scatter(jnp.concatenate([first, second], axis=1), level)
+        r = input_two.shape[1] // 16
+        c = context_flat.shape[1] // 16
+        grad_c_out, grad_c_key = sums[:r].T, sums[r : r + c]
+        grad_c_query, grad_c_value = sums[r + c : 2 * r + c], sums[2 * r + c :]
+    else:
+        grad_c_out = generic_sum(grad_cross_out, attended_two).T
+        grad_c_query = generic_sum(input_two, cross_query_grad)
+        grad_c_key = generic_sum(context_flat, cross_key_grad)
+        grad_c_value = generic_sum(context_flat, cross_value_grad)
     normed_grad_two = swap_sum(product_with_rows(cross_query_grad, c_query))
     back_two, grad_gain_cross, grad_bias_cross = normalize_back(
         normed_grad_two, scaled_two, inverse_two, gain_cross
     )
     grad_one = grad_two + back_two
     grad_self_out = grad_one.astype(low)
-    grad_w_out = weight_sum(grad_self_out, attended_one, True)
     grad_attended_one = product_with_rows(grad_self_out, w_out).astype(low)
     query_grad, key_grad, value_grad = attend_backward(
         query_one, heads_of(key_one), heads_of(value_one), self_ok, grad_attended_one, logsum_one
@@ -344,9 +515,30 @@
     query_grad = rotate_back(query_grad, tables).astype(low)
     key_grad = rotate_back(key_grad, tables).astype(low)
     value_grad = value_grad.astype(low)
-    grad_w_query = weight_sum(input_one, query_grad)
-    grad_w_key = weight_sum(input_one, key_grad)
-    grad_w_value = weight_sum(input_one, value_grad)
+    if known:
+        first = plane_scatter(
+            stacked(
+                quarter_products(grad_self_out, attended_one, plane),
+                quarter_products(input_one, value_grad, plane),
+            ),
+            1,
+        )
+        second = plane_scatter(
+            stacked(
+                quarter_products(input_one, query_grad, plane),
+                quarter_products(input_one, key_grad, plane),
+            ),
+            2,
+        )
+        sums = z_scatter(jnp.concatenate([first, second], axis=1), level)
+        r = input_one.shape[1] // 16
+        grad_w_out, grad_w_value = sums[:r].T, sums[r : 2 * r]
+        grad_w_query, grad_w_key = sums[2 * r : 3 * r], sums[3 * r :]
+    else:
+        grad_w_out = generic_sum(grad_self_out, attended_one).T
+        grad_w_query = generic_sum(input_one, query_grad)
+        grad_w_key = generic_sum(input_one, key_grad)
+        grad_w_value = generic_sum(input_one, value_grad)
     normed_grad_one = swap_sum(
         product_with_rows(query_grad, w_query)
         + product_with_rows(key_grad, w_key)

time: 1020 us -> 712 us (0.70)
  waiting for transfers between devices: 290 us -> 123 us
  starting transfers between devices: 284 us -> 151 us
  matrix products: 204 us -> 114 us
  Pallas kernels: 0 us -> 80.2 us
  local copies, waits for them, and re-layouts: 97.8 us -> 113 us
  other arithmetic: 131 us -> 120 us
    ppermute x66 -> x27, waiting for transfers between devices: 236 us -> 74.4 us  [the longest x6 28.1 us: plane_gather(): got = [lax.ppermute(own_half, 'dp', pairs(mask)) for mask in mask_list]]
    ppermute x33 -> x15, starting transfers between devices: 173 us -> 91.4 us  [z_scatter(): up = lax.ppermute(up_send, 'dp', up_perm)]
    pallas_call x0 -> x4, Pallas kernels: none -> 80.2 us  [the longest x3 45.5 us: ff_share(): pl.pallas_call(share_kernel, grid_spec=pltpu.PrefetchScalarGridSpec(num_s...]
    dot_general x55 -> x36, matrix products: 108 us -> 44.9 us  [product_plain(): return jnp.dot(left_side, right_side, preferred_element_type=jnp.float32)]
    ppermute x66 -> x27, starting transfers between devices: 71.7 us -> 26 us  [the longest x6 8.29 us: plane_gather(): got = [lax.ppermute(own_half, 'dp', pairs(mask)) for mask in mask_list]]
    dot_general x9 -> x6, matrix products: 52.7 us -> 27.5 us  [product_with_rows(): lax.dot_general(left_side, right_side, (((1,), (1,)), ((), ())), preferre...]
    ppermute x33 -> x15, waiting for transfers between devices: 38.2 us -> 20 us  [z_scatter(): up = lax.ppermute(up_send, 'dp', up_perm)]
    unnamed x375 -> x332, local copies, waits for them, and re-layouts: 22.5 us -> 37.4 us
  transfers between devices with their start and end apart: 142 -> 67, of which waited for: 63 -> 16; matrix products, arithmetic and copies ran while one was open for 25% -> 45% of each run, Pallas kernels for 0% -> 9%
where the time goes in v2:
time: 712 us; the launch traced here: 705 us
  starting transfers between devices  151 us (21%)
  waiting for transfers between devices  123 us (17%)
  other arithmetic  120 us (17%)
  matrix products  114 us (16%)
  local copies, waits for them, and re-layouts  113 us (16%)
  Pallas kernels  80.2 us (11%)
    ppermute x15, starting transfers between devices, z_scatter(): up = lax.ppermute(up_send, 'dp', up_perm)  91.4 us
    pallas_call x3, Pallas kernels, ff_share(): pl.pallas_call(share_kernel, grid_spec=pltpu.PrefetchScalarGridSpec(num_s...  45.5 us
    dot_general x36, matrix products, product_plain(): return jnp.dot(left_side, right_side, preferred_element_type=jnp.float32)  44.9 us
    unnamed x332, local copies, waits for them, and re-layouts  37.4 us
    pallas_call x1, Pallas kernels, ff_both(): pl.pallas_call(ff_kernel, grid=(units // tile,), in_specs=[whole, whole,...  34.6 us
    ppermute x6, waiting for transfers between devices, plane_gather(): got = [lax.ppermute(own_half, 'dp', pairs(mask)) for mask in mask_list]  28.1 us
    dot_general x6, matrix products, product_with_rows(): lax.dot_general(left_side, right_side, (((1,), (1,)), ((), ())), preferre...  27.5 us
    ppermute x15, waiting for transfers between devices, z_scatter(): down = lax.ppermute(down_send, 'dp', down_perm)  23.8 us
  transfers between devices with their start and end apart: 67, of which 16 were waited for; matrix products, arithmetic and copies ran while one was open for 45% of the time, Pallas kernels for 9%

profile of v2, /device:TPU:0, one launch (start us, length us, event | category | flops | bytes accessed | tf_op | source)
XLA Modules:
  0.0 705.4 jit_solution(11904137912293763694)
XLA Ops:
  0.7 4.0 constant_dynamic-update-slice_fusion.13
  6.8 2.9 collective-permute-start.40
  23.5 8.3 %fusion.32 = (bf16[512,768]{1,0:T(8,128)(2,1)}, bf16[512,768]{1,0:T(8,128)(2,1)S(1)}) fusion(f32[512,768]{1,0:T(8,128)S(1)} %fusion.179, f32[512,16]{1,0:T(8,128)S(1)} %get-tuple-element.104, f32[512,752]{1,0:T(8,128)S(1)} %get-tuple-element.106, f32[512,752]{1,0:T(8,128)S(1)} %get-tuple-element.105, f32[512,16]{1,0:T(8,128)S(1)} %get-tuple-element.103, ...), kind=kLoop, calls=%fused_computation.116 | loop fusion | flops 8257536 | bytes 11017472 | tf_op jit(solution)/shard_map/convert_element_type | solution.py:417
  34.6 4.5 convolution_convert_fusion.10
  41.4 3.2 fusion.8
  44.7 2.6 fusion
  49.4 3.8 fusion.61
  53.2 2.6 convolution_convert_fusion.2
  64.6 2.6 copy.93
  71.1 2.7 constant_dynamic-slice_fusion.21
  101.4 3.0 copy.101
  106.4 3.4 fusion.165
  114.1 34.6 %shard_map.357 = (bf16[512,1536]{1,0:T(8,128)(2,1)S(1)}, bf16[512,1536]{1,0:T(8,128)(2,1)S(1)}) custom-call(bf16[512,1536]{1,0:T(8,128)(2,1)S(1)} %get-tuple-element.38.in_ref, bf16[512,1536]{1,0:T(8,128)(2,1)S(1)} %copy-done.11, bf16[1536,3072]{1,0:T(8,128)(2,1)} %gate_ref.7, bf16[1536,3072]{1,0:T(8,128)(2,1)} %up_ref.7, bf16[3072,1536]{1,0:T(8,128)(2,1)} %down_ref.7), custom_call_target="tpu_custom_call" | custom-call | flops 28991029248 | bytes 34603008 | tf_op jit(solution)/shard_map/pallas_call | solution.py:255
  159.3 28.1 %collective-permute-done.35 = bf16[256,1536]{1,0:T(8,128)(2,1)} collective-permute-done((bf16[256,1536]{1,0:T(8,128)(2,1)}, bf16[256,1536]{1,0:T(8,128)(2,1)}, u32[]{:S(2)}, u32[]{:S(2)}) %collective-permute-start.35) | collective-permute-done | bytes 786464 | tf_op jit(solution)/shard_map/ppermute | solution.py:206
  194.4 3.6 convert_bitcast_fusion.1
  204.5 7.2 %multiply_reduce_fusion.1 = (f32[12,512]{1,0:T(8,128)S(1)}, f32[12,512,256]{1,2,0:T(8,128)}) fusion(f32[12,512,256]{1,2,0:T(8,128)} %copy-done.13, f32[12,512]{1,0:T(8,128)} %log_add_fusion.1, bf16[512,12,64]{0,2,1:T(8,128)(2,1)} %bitcast.428, bf16[256,12,64]{0,2,1:T(8,128)(2,1)} %bitcast.496), kind=kOutput, calls=%fused_computation.11 | convolution fusion | flops 206039040 | bytes 13811712 | tf_op jit(solution)/shard_map/qhd,khd->hqk/dot_general | solution.py:120
  212.9 6.6 multiply_convert_fusion.1
  225.9 15.1 %shard_map.358 = bf16[4,3,384,256]{3,2,1,0:T(8,128)(2,1)S(1)} custom-call(s32[1]{0:T(128)} %bitcast.121._, bf16[2048,1536]{1,0:T(8,128)(2,1)S(1)} %constant_dynamic-update-slice_fusion.in_ref, bf16[2048,1536]{1,0:T(8,128)(2,1)} %constant_dynamic-update-slice_fusion.7.out_ref, bf16[1536,3072]{1,0:T(8,128)(2,1)} %gate_ref.7, bf16[1536,3072]{1,0:T(8,128)(2,1)} %up_ref.7, ...), custom_call_target="tpu_custom_call" | custom-call | flops 9663676416 | bytes 17301504 | tf_op jit(solution)/shard_map/pallas_call | solution.py:309
  242.3 4.3 collective-permute-start.46
  248.1 15.3 %shard_map.359 = bf16[4,3,384,256]{3,2,1,0:T(8,128)(2,1)S(1)} custom-call(s32[1]{0:T(128)} %bitcast.129._, bf16[2048,1536]{1,0:T(8,128)(2,1)S(1)} %constant_dynamic-update-slice_fusion.in_ref, bf16[2048,1536]{1,0:T(8,128)(2,1)} %constant_dynamic-update-slice_fusion.7.out_ref, bf16[1536,3072]{1,0:T(8,128)(2,1)} %gate_ref.7, bf16[1536,3072]{1,0:T(8,128)(2,1)} %up_ref.7, ...), custom_call_target="tpu_custom_call" | custom-call | flops 9663676416 | bytes 17301504 | tf_op jit(solution)/shard_map/pallas_call | solution.py:309
  266.7 15.1 %shard_map.360 = bf16[4,3,384,256]{3,2,1,0:T(8,128)(2,1)S(1)} custom-call(s32[1]{0:T(128)} %bitcast.137._, bf16[2048,1536]{1,0:T(8,128)(2,1)S(1)} %constant_dynamic-update-slice_fusion.in_ref, bf16[2048,1536]{1,0:T(8,128)(2,1)} %constant_dynamic-update-slice_fusion.7.out_ref, bf16[1536,3072]{1,0:T(8,128)(2,1)} %gate_ref.7, bf16[1536,3072]{1,0:T(8,128)(2,1)} %up_ref.7, ...), custom_call_target="tpu_custom_call" | custom-call | flops 9663676416 | bytes 17301504 | tf_op jit(solution)/shard_map/pallas_call | solution.py:309
  286.6 2.6 convolution_convert_fusion
  318.2 10.3 %collective-permute-done.23 = bf16[4,144,768]{2,1,0:T(8,128)(2,1)S(1)} collective-permute-done((bf16[4,144,768]{2,1,0:T(8,128)(2,1)S(1)}, bf16[4,144,768]{2,1,0:T(8,128)(2,1)S(1)}, u32[]{:S(2)}, u32[]{:S(2)}) %collective-permute-start.23) | collective-permute-done | bytes 884768 | tf_op jit(solution)/shard_map/ppermute | solution.py:184
  334.6 2.9 collective-permute-done.53
  340.9 7.7 %collective-permute-done.59 = bf16[3,384,256]{2,1,0:T(8,128)(2,1)S(1)} collective-permute-done((bf16[3,384,256]{2,1,0:T(8,128)(2,1)S(1)}, bf16[3,384,256]{2,1,0:T(8,128)(2,1)S(1)}, u32[]{:S(2)}, u32[]{:S(2)}) %collective-permute-start.59) | collective-permute-done | bytes 589856 | tf_op jit(solution)/shard_map/ppermute | solution.py:177
  353.6 2.7 convert_bitcast_fusion
  362.7 11.4 %multiply_reduce_fusion = (f32[12,512]{1,0:T(8,128)S(1)}, f32[12,512,512]{1,2,0:T(8,128)}) fusion(f32[12,512]{1,0:T(8,128)S(1)} %copy-done.113, f32[12,512,512]{1,2,0:T(8,128)} %copy-done.12, pred[512,512]{0,1:T(8,128)(4,1)S(1)} %copy-done.46, bf16[512,12,64]{0,2,1:T(8,128)(2,1)} %bitcast.457, bf16[512,12,64]{0,2,1:T(8,128)(2,1)S(1)} %bitcast.456), kind=kOutput, calls=%fused_computation.1 | convolution fusion | flops 418375680 | bytes 27049984 | tf_op jit(solution)/shard_map/qhd,khd->hqk/dot_general | solution.py:120
  375.5 7.1 multiply_convert_fusion
  382.6 3.2 convolution_multiply_fusion
  388.1 3.0 copy.88
  391.1 3.0 copy.84
  394.2 7.9 %fusion.35 = (f32[512,768]{1,0:T(8,128)}, f32[512,768]{1,0:T(8,128)S(1)}, f32[512,768]{1,0:T(8,128)S(1)}, f32[512,768]{1,0:T(8,128)S(1)}) fusion(f32[512,768]{1,0:T(8,128)} %copy.84, f32[768]{0:T(1024)S(1)} %copy-done.120, f32[512]{0:T(512)S(1)} %copy-done.130, pred[768]{0:T(1024)(128)(4,1)S(1)} %copy-done.140, pred[768]{0:T(1024)(128)(4,1)S(1)} %copy-done.146, ...), kind=kLoop, calls=%fused_computation.119 | loop fusion | flops 3145728 | bytes 9443840 | tf_op jit(solution)/shard_map/mul | solution.py:61
  407.1 3.0 copy.96
  410.1 2.7 pad_maximum_fusion.5
  412.9 3.1 copy.97
  417.0 3.0 pad_maximum_fusion.2
  420.1 3.0 copy.94
  423.1 2.8 pad_maximum_fusion.3
  425.9 3.0 copy.95
  429.0 8.5 %fusion.56 = (bf16[512,12,64]{0,2,1:T(8,128)(2,1)S(1)}, bf16[512,12,64]{0,2,1:T(8,128)(2,1)S(1)}) fusion(f32[512,12,64]{0,2,1:T(8,128)} %bitcast.449, f32[512,12,64]{0,2,1:T(8,128)} %bitcast.448, f32[12,64,512]{2,1,0:T(8,128)} %convolution_multiply_fusion.1, f32[12,64]{1,0:T(8,128)S(1)} %copy-done.136, f32[512]{0:T(512)S(1)} %copy-done.130, ...), kind=kLoop, calls=%fused_computation.146 | loop fusion | flops 3932160 | bytes 11015936 | tf_op jit(solution)/shard_map/convert_element_type | solution.py:515
  448.2 3.0 fusion.58
  456.7 9.3 %fusion.95 = f32[512,1536]{1,0:T(8,128)} fusion(bf16[1536,768]{1,0:T(8,128)(2,1)S(1)} %copy-done.81, f32[512,768]{1,0:T(8,128)S(1)} %copy-done.31, f32[512,768]{1,0:T(8,128)S(1)} %copy-done.30, f32[512,768]{1,0:T(8,128)S(1)} %copy-done.33, f32[768]{0:T(1024)S(1)} %copy-done.120, f32[512]{0:T(512)S(1)} %copy-done.130, pred[768]{0:T(1024)(128)(4,1)S(1)} %copy-done.138), kind=kOutput, calls=%fused_computation.251 | convolution fusion | flops 1210318848 | bytes 10229504 | tf_op jit(solution)/shard_map/dot_general | solution.py:30
  466.0 3.0 copy.92
  473.2 9.6 %convolution_add_fusion.1 = f32[512,1536]{1,0:T(8,128)S(1)} fusion(f32[512,1536]{1,0:T(8,128)} %fusion.95, bf16[1536,768]{1,0:T(8,128)(2,1)S(1)} %copy-done.83, f32[512,768]{1,0:T(8,128)S(1)} %copy-done.29, f32[512,768]{1,0:T(8,128)S(1)} %copy-done.28, f32[512,768]{1,0:T(8,128)S(1)} %copy-done.32, f32[768]{0:T(1024)S(1)} %copy-done.120, ...), kind=kOutput, calls=%fused_computation.35 | convolution fusion | flops 1211105280 | bytes 13375232 | tf_op jit(solution)/shard_map/dot_general | solution.py:30
  488.3 4.5 collective-permute-start.48
  500.5 6.6 collective-permute-start.28
  508.2 9.6 %collective-permute-start.54 = (bf16[3,384,256]{2,1,0:T(8,128)(2,1)S(1)}, bf16[3,384,256]{2,1,0:T(8,128)(2,1)S(1)}, u32[]{:S(2)}, u32[]{:S(2)}) collective-permute-start(bf16[3,384,256]{2,1,0:T(8,128)(2,1)S(1)} %copy-done.97), channel_id=1, source_target_pairs={{0,8},{2,10},{4,12},{6,14},{8,16},{10,18},{12,20},{14,22},{16,24},... | collective-permute-start | bytes 1769480 | tf_op jit(solution)/shard_map/ppermute | solution.py:177
  519.2 12.2 %collective-permute-start.60 = (bf16[3,384,256]{2,1,0:T(8,128)(2,1)S(1)}, bf16[3,384,256]{2,1,0:T(8,128)(2,1)S(1)}, u32[]{:S(2)}, u32[]{:S(2)}) collective-permute-start(bf16[3,384,256]{2,1,0:T(8,128)(2,1)S(1)} %copy-done.98), channel_id=1, source_target_pairs={{0,8},{2,10},{4,12},{6,14},{8,16},{10,18},{12,20},{14,22},{16,24},... | collective-permute-start | bytes 1769480 | tf_op jit(solution)/shard_map/ppermute | solution.py:177
  535.4 7.7 %collective-permute-done.57 = bf16[3,384,256]{2,1,0:T(8,128)(2,1)S(1)} collective-permute-done((bf16[3,384,256]{2,1,0:T(8,128)(2,1)S(1)}, bf16[3,384,256]{2,1,0:T(8,128)(2,1)S(1)}, u32[]{:S(2)}, u32[]{:S(2)}) %collective-permute-start.57) | collective-permute-done | bytes 589856 | tf_op jit(solution)/shard_map/ppermute | solution.py:178
  544.8 11.4 %collective-permute-start.29 = (bf16[288,768]{1,0:T(8,128)(2,1)S(1)}, bf16[288,768]{1,0:T(8,128)(2,1)S(1)}, u32[]{:S(2)}, u32[]{:S(2)}) collective-permute-start(bf16[288,768]{1,0:T(8,128)(2,1)S(1)} %get-tuple-element.79), channel_id=1, source_target_pairs={{0,8},{2,10},{4,12},{6,14},{8,16},{10,18},{12,20},{14,22},{1,9},{3... | collective-permute-start | bytes 1327112 | tf_op jit(solution)/shard_map/ppermute | solution.py:177
  557.4 4.6 collective-permute-done.29
  567.1 7.9 %collective-permute-done.64 = bf16[3,96,768]{2,1,0:T(8,128)(2,1)S(1)} collective-permute-done((bf16[3,96,768]{2,1,0:T(8,128)(2,1)S(1)}, bf16[3,96,768]{2,1,0:T(8,128)(2,1)S(1)}, u32[]{:S(2)}, u32[]{:S(2)}) %collective-permute-start.64) | collective-permute-done | bytes 442400 | tf_op jit(solution)/shard_map/ppermute | solution.py:339
  575.0 12.9 %collective-permute-start.30 = (bf16[288,768]{1,0:T(8,128)(2,1)S(1)}, bf16[288,768]{1,0:T(8,128)(2,1)S(1)}, u32[]{:S(2)}, u32[]{:S(2)}) collective-permute-start(bf16[288,768]{1,0:T(8,128)(2,1)S(1)} %get-tuple-element.77), channel_id=1, source_target_pairs={{0,8},{2,10},{4,12},{6,14},{8,16},{10,18},{12,20},{14,22},{16,24},... | collective-permute-start | bytes 1327112 | tf_op jit(solution)/shard_map/ppermute | solution.py:177
  588.0 11.0 %collective-permute-done.65 = bf16[3,96,768]{2,1,0:T(8,128)(2,1)S(1)} collective-permute-done((bf16[3,96,768]{2,1,0:T(8,128)(2,1)S(1)}, bf16[3,96,768]{2,1,0:T(8,128)(2,1)S(1)}, u32[]{:S(2)}, u32[]{:S(2)}) %collective-permute-start.65) | collective-permute-done | bytes 442400 | tf_op jit(solution)/shard_map/ppermute | solution.py:339
  602.8 11.6 %collective-permute-done.33 = bf16[288,768]{1,0:T(8,128)(2,1)S(1)} collective-permute-done((bf16[288,768]{1,0:T(8,128)(2,1)S(1)}, bf16[288,768]{1,0:T(8,128)(2,1)S(1)}, u32[]{:S(2)}, u32[]{:S(2)}) %collective-permute-start.33) | collective-permute-done | bytes 442400 | tf_op jit(solution)/shard_map/ppermute | solution.py:178
  617.6 11.4 %collective-permute-done.15 = bf16[4,192,768]{2,1,0:T(8,128)(2,1)S(1)} collective-permute-done((bf16[4,192,768]{2,1,0:T(8,128)(2,1)S(1)}, bf16[4,192,768]{2,1,0:T(8,128)(2,1)S(1)}, u32[]{:S(2)}, u32[]{:S(2)}) %collective-permute-start.15) | collective-permute-done | bytes 1179680 | tf_op jit(solution)/shard_map/ppermute | solution.py:187
  629.4 5.7 collective-permute-done.12
  637.1 14.7 %collective-permute-start.16 = (bf16[384,768]{1,0:T(8,128)(2,1)}, bf16[384,768]{1,0:T(8,128)(2,1)}, u32[]{:S(2)}, u32[]{:S(2)}) collective-permute-start(bf16[384,768]{1,0:T(8,128)(2,1)} %get-tuple-element.67), channel_id=1, source_target_pairs={{0,8},{2,10},{4,12},{6,14},{1,9},{3,11},{5,13},{7,15}} | collective-permute-start | bytes 1769480 | tf_op jit(solution)/shard_map/ppermute | solution.py:177
  661.7 4.4 collective-permute-start.17
  672.7 9.1 %collective-permute-start.8 = (f32[6,1536]{1,0:T(8,128)S(1)}, f32[6,1536]{1,0:T(8,128)S(1)}, u32[]{:S(2)}, u32[]{:S(2)}) collective-permute-start(f32[6,1536]{1,0:T(8,128)S(1)} %add.529), channel_id=1, source_target_pairs={{0,8},{2,10},{4,12},{6,14},{8,0},{10,2},{12,4},{14,6},{16,24},{18,... | collective-permute-start | bytes 110600 | tf_op jit(solution)/shard_map/ppermute | solution.py:359
  684.1 4.6 collective-permute-start.9
  692.7 2.7 multiply_add_fusion
  696.0 2.7 collective-permute-done.18
  698.7 4.4 collective-permute-done.21
  (618 shorter events, 252.5 us)
Async XLA Ops:
  6.8 68.5 %collective-permute-start.40 = (bf16[256,1536]{1,0:T(8,128)(2,1)}, bf16[256,1536]{1,0:T(8,128)(2,1)}, u32[]{:S(2)}, u32[]{:S(2)}) collective-permute-start(bf16[256,1536]{1,0:T(8,128)(2,1)} %constant_dynamic-slice_fusion.1), channel_id=1, source_target_pairs={{0,2},{2,0},{4,6},{6,4},{8,10},{10,8},{12,14},{14,12},{16,18},{18,... | collective-permute-start | bytes 2359304 | tf_op jit(solution)/shard_map/ppermute | solution.py:206
  9.7 66.0 %collective-permute-start.41 = (bf16[256,1536]{1,0:T(8,128)(2,1)}, bf16[256,1536]{1,0:T(8,128)(2,1)}, u32[]{:S(2)}, u32[]{:S(2)}) collective-permute-start(bf16[256,1536]{1,0:T(8,128)(2,1)} %constant_dynamic-slice_fusion.1), channel_id=1, source_target_pairs={{0,4},{2,6},{4,0},{6,2},{8,12},{10,14},{12,8},{14,10},{16,20},{18,... | collective-permute-start | bytes 2359304 | tf_op jit(solution)/shard_map/ppermute | solution.py:206
  11.2 64.6 %collective-permute-start.42 = (bf16[256,1536]{1,0:T(8,128)(2,1)}, bf16[256,1536]{1,0:T(8,128)(2,1)}, u32[]{:S(2)}, u32[]{:S(2)}) collective-permute-start(bf16[256,1536]{1,0:T(8,128)(2,1)} %constant_dynamic-slice_fusion.1), channel_id=1, source_target_pairs={{0,6},{2,4},{4,2},{6,0},{8,14},{10,12},{12,10},{14,8},{16,22},{18,... | collective-permute-start | bytes 2359304 | tf_op jit(solution)/shard_map/ppermute | solution.py:206
  55.8 20.4 %collective-permute-start = (bf16[512,1536]{1,0:T(8,128)(2,1)}, bf16[512,1536]{1,0:T(8,128)(2,1)}, u32[]{:S(2)}, u32[]{:S(2)}) collective-permute-start(bf16[512,1536]{1,0:T(8,128)(2,1)} %convolution_convert_fusion.2), channel_id=1, source_target_pairs={{0,1},{1,0},{2,3},{3,2},{4,5},{5,4},{6,7},{7,6},{8,9},{9,8},{10,11... | collective-permute-start | bytes 4718600 | tf_op jit(solution)/shard_map/ppermute | solution.py:149
  75.2 29.1 %collective-permute-start.43 = (bf16[256,1536]{1,0:T(8,128)(2,1)}, bf16[256,1536]{1,0:T(8,128)(2,1)}, u32[]{:S(2)}, u32[]{:S(2)}) collective-permute-start(bf16[256,1536]{1,0:T(8,128)(2,1)} %collective-permute-done.40), channel_id=1, source_target_pairs={{0,1},{1,0},{2,3},{3,2},{4,5},{5,4},{6,7},{7,6},{8,9},{9,8},{10,11... | collective-permute-start | bytes 2359304 | tf_op jit(solution)/shard_map/ppermute | solution.py:207
  75.7 76.2 %collective-permute-start.44 = (bf16[256,1536]{1,0:T(8,128)(2,1)}, bf16[256,1536]{1,0:T(8,128)(2,1)}, u32[]{:S(2)}, u32[]{:S(2)}) collective-permute-start(bf16[256,1536]{1,0:T(8,128)(2,1)} %collective-permute-done.41), channel_id=1, source_target_pairs={{0,1},{1,0},{2,3},{3,2},{4,5},{5,4},{6,7},{7,6},{8,9},{9,8},{10,11... | collective-permute-start | bytes 2359304 | tf_op jit(solution)/shard_map/ppermute | solution.py:207
  75.8 79.7 %collective-permute-start.45 = (bf16[256,1536]{1,0:T(8,128)(2,1)}, bf16[256,1536]{1,0:T(8,128)(2,1)}, u32[]{:S(2)}, u32[]{:S(2)}) collective-permute-start(bf16[256,1536]{1,0:T(8,128)(2,1)} %collective-permute-done.42), channel_id=1, source_target_pairs={{0,1},{1,0},{2,3},{3,2},{4,5},{5,4},{6,7},{7,6},{8,9},{9,8},{10,11... | collective-permute-start | bytes 2359304 | tf_op jit(solution)/shard_map/ppermute | solution.py:207
  93.0 13.4 %collective-permute-start.1 = (bf16[512,1536]{1,0:T(8,128)(2,1)}, bf16[512,1536]{1,0:T(8,128)(2,1)}, u32[]{:S(2)}, u32[]{:S(2)}) collective-permute-start(bf16[512,1536]{1,0:T(8,128)(2,1)} %convolution_convert_fusion.1), channel_id=1, source_target_pairs={{0,1},{1,0},{2,3},{3,2},{4,5},{5,4},{6,7},{7,6},{8,9},{9,8},{10,11... | collective-permute-start | bytes 4718600 | tf_op jit(solution)/shard_map/ppermute | solution.py:149
  112.1 45.4 %collective-permute-start.34 = (bf16[256,1536]{1,0:T(8,128)(2,1)}, bf16[256,1536]{1,0:T(8,128)(2,1)}, u32[]{:S(2)}, u32[]{:S(2)}) collective-permute-start(bf16[256,1536]{1,0:T(8,128)(2,1)} %constant_dynamic-slice_fusion.2), channel_id=1, source_target_pairs={{0,2},{2,0},{4,6},{6,4},{8,10},{10,8},{12,14},{14,12},{16,18},{18,... | collective-permute-start | bytes 2359304 | tf_op jit(solution)/shard_map/ppermute | solution.py:206
  148.8 41.5 %collective-permute-start.3 = (bf16[512,1536]{1,0:T(8,128)(2,1)S(1)}, bf16[512,1536]{1,0:T(8,128)(2,1)S(1)}, u32[]{:S(2)}, u32[]{:S(2)}) collective-permute-start(bf16[512,1536]{1,0:T(8,128)(2,1)S(1)} %get-tuple-element.22), channel_id=1, source_target_pairs={{0,1},{1,0},{2,3},{3,2},{4,5},{5,4},{6,7},{7,6},{8,9},{9,8},{10,11... | collective-permute-start | bytes 4718600 | tf_op jit(solution)/shard_map/ppermute | solution.py:149
  150.4 37.0 %collective-permute-start.35 = (bf16[256,1536]{1,0:T(8,128)(2,1)}, bf16[256,1536]{1,0:T(8,128)(2,1)}, u32[]{:S(2)}, u32[]{:S(2)}) collective-permute-start(bf16[256,1536]{1,0:T(8,128)(2,1)} %constant_dynamic-slice_fusion.2), channel_id=1, source_target_pairs={{0,4},{2,6},{4,0},{6,2},{8,12},{10,14},{12,8},{14,10},{16,20},{18,... | collective-permute-start | bytes 2359304 | tf_op jit(solution)/shard_map/ppermute | solution.py:206
  151.9 35.5 %collective-permute-start.36 = (bf16[256,1536]{1,0:T(8,128)(2,1)}, bf16[256,1536]{1,0:T(8,128)(2,1)}, u32[]{:S(2)}, u32[]{:S(2)}) collective-permute-start(bf16[256,1536]{1,0:T(8,128)(2,1)} %constant_dynamic-slice_fusion.2), channel_id=1, source_target_pairs={{0,6},{2,4},{4,2},{6,0},{8,14},{10,12},{12,10},{14,8},{16,22},{18,... | collective-permute-start | bytes 2359304 | tf_op jit(solution)/shard_map/ppermute | solution.py:206
  157.6 35.9 %collective-permute-start.2 = (bf16[512,1536]{1,0:T(8,128)(2,1)S(1)}, bf16[512,1536]{1,0:T(8,128)(2,1)S(1)}, u32[]{:S(2)}, u32[]{:S(2)}) collective-permute-start(bf16[512,1536]{1,0:T(8,128)(2,1)S(1)} %get-tuple-element.21), channel_id=1, source_target_pairs={{0,1},{1,0},{2,3},{3,2},{4,5},{5,4},{6,7},{7,6},{8,9},{9,8},{10,11... | collective-permute-start | bytes 4718600 | tf_op jit(solution)/shard_map/ppermute | solution.py:149
  157.6 54.0 %collective-permute-start.37 = (bf16[256,1536]{1,0:T(8,128)(2,1)}, bf16[256,1536]{1,0:T(8,128)(2,1)}, u32[]{:S(2)}, u32[]{:S(2)}) collective-permute-start(bf16[256,1536]{1,0:T(8,128)(2,1)} %collective-permute-done.34), channel_id=1, source_target_pairs={{0,1},{1,0},{2,3},{3,2},{4,5},{5,4},{6,7},{7,6},{8,9},{9,8},{10,11... | collective-permute-start | bytes 2359304 | tf_op jit(solution)/shard_map/ppermute | solution.py:207
  187.3 33.6 %collective-permute-start.38 = (bf16[256,1536]{1,0:T(8,128)(2,1)}, bf16[256,1536]{1,0:T(8,128)(2,1)}, u32[]{:S(2)}, u32[]{:S(2)}) collective-permute-start(bf16[256,1536]{1,0:T(8,128)(2,1)} %collective-permute-done.35), channel_id=1, source_target_pairs={{0,1},{1,0},{2,3},{3,2},{4,5},{5,4},{6,7},{7,6},{8,9},{9,8},{10,11... | collective-permute-start | bytes 2359304 | tf_op jit(solution)/shard_map/ppermute | solution.py:207
  187.3 37.2 %collective-permute-start.39 = (bf16[256,1536]{1,0:T(8,128)(2,1)}, bf16[256,1536]{1,0:T(8,128)(2,1)}, u32[]{:S(2)}, u32[]{:S(2)}) collective-permute-start(bf16[256,1536]{1,0:T(8,128)(2,1)} %collective-permute-done.36), channel_id=1, source_target_pairs={{0,1},{1,0},{2,3},{3,2},{4,5},{5,4},{6,7},{7,6},{8,9},{9,8},{10,11... | collective-permute-start | bytes 2359304 | tf_op jit(solution)/shard_map/ppermute | solution.py:207
  242.3 65.1 %collective-permute-start.46 = (bf16[3,384,256]{2,1,0:T(8,128)(2,1)}, bf16[3,384,256]{2,1,0:T(8,128)(2,1)}, u32[]{:S(2)}, u32[]{:S(2)}) collective-permute-start(bf16[3,384,256]{2,1,0:T(8,128)(2,1)} %get-tuple-element.53), channel_id=1, source_target_pairs={{0,8},{2,10},{4,12},{6,14},{1,9},{3,11},{5,13},{7,15}} | collective-permute-start | bytes 1769480 | tf_op jit(solution)/shard_map/ppermute | solution.py:177
  246.6 67.1 %collective-permute-start.49 = (bf16[3,384,256]{2,1,0:T(8,128)(2,1)}, bf16[3,384,256]{2,1,0:T(8,128)(2,1)}, u32[]{:S(2)}, u32[]{:S(2)}) collective-permute-start(bf16[3,384,256]{2,1,0:T(8,128)(2,1)} %get-tuple-element.54), channel_id=1, source_target_pairs={{24,16},{26,18},{28,20},{30,22},{25,17},{27,19},{29,21},{31,23}} | collective-permute-start | bytes 1769480 | tf_op jit(solution)/shard_map/ppermute | solution.py:178
  264.6 45.0 %collective-permute-start.52 = (bf16[3,384,256]{2,1,0:T(8,128)(2,1)}, bf16[3,384,256]{2,1,0:T(8,128)(2,1)}, u32[]{:S(2)}, u32[]{:S(2)}) collective-permute-start(bf16[3,384,256]{2,1,0:T(8,128)(2,1)} %get-tuple-element.57), channel_id=1, source_target_pairs={{0,8},{2,10},{4,12},{6,14},{1,9},{3,11},{5,13},{7,15}} | collective-permute-start | bytes 1769480 | tf_op jit(solution)/shard_map/ppermute | solution.py:177
  283.0 29.4 %collective-permute-start.58 = (bf16[3,384,256]{2,1,0:T(8,128)(2,1)}, bf16[3,384,256]{2,1,0:T(8,128)(2,1)}, u32[]{:S(2)}, u32[]{:S(2)}) collective-permute-start(bf16[3,384,256]{2,1,0:T(8,128)(2,1)} %get-tuple-element.61), channel_id=1, source_target_pairs={{0,8},{2,10},{4,12},{6,14},{1,9},{3,11},{5,13},{7,15}} | collective-permute-start | bytes 1769480 | tf_op jit(solution)/shard_map/ppermute | solution.py:177
  292.2 22.4 %collective-permute-start.26 = (bf16[4,144,768]{2,1,0:T(8,128)(2,1)}, bf16[4,144,768]{2,1,0:T(8,128)(2,1)}, u32[]{:S(2)}, u32[]{:S(2)}) collective-permute-start(bf16[4,144,768]{2,1,0:T(8,128)(2,1)} %pad_maximum_fusion.13), channel_id=1, source_target_pairs={{0,4},{2,6},{4,0},{6,2},{8,12},{10,14},{12,8},{14,10},{16,20},{18,... | collective-permute-start | bytes 2654216 | tf_op jit(solution)/shard_map/ppermute | solution.py:184
  307.4 21.1 %collective-permute-start.23 = (bf16[4,144,768]{2,1,0:T(8,128)(2,1)S(1)}, bf16[4,144,768]{2,1,0:T(8,128)(2,1)S(1)}, u32[]{:S(2)}, u32[]{:S(2)}) collective-permute-start(bf16[4,144,768]{2,1,0:T(8,128)(2,1)S(1)} %pad_maximum_fusion.11), channel_id=1, source_target_pairs={{0,2},{2,0},{4,6},{6,4},{8,10},{10,8},{12,14},{14,12},{16,18},{18,... | collective-permute-start | bytes 2654216 | tf_op jit(solution)/shard_map/ppermute | solution.py:184
  309.6 19.6 %collective-permute-start.47 = (bf16[3,384,256]{2,1,0:T(8,128)(2,1)S(1)}, bf16[3,384,256]{2,1,0:T(8,128)(2,1)S(1)}, u32[]{:S(2)}, u32[]{:S(2)}) collective-permute-start(bf16[3,384,256]{2,1,0:T(8,128)(2,1)S(1)} %fusion.80), channel_id=1, source_target_pairs={{0,8},{2,10},{4,12},{6,14},{8,16},{10,18},{12,20},{14,22},{1,9},{3... | collective-permute-start | bytes 1769480 | tf_op jit(solution)/shard_map/ppermute | solution.py:177
  312.4 38.0 %collective-permute-start.4 = (bf16[512,1536]{1,0:T(8,128)(2,1)S(1)}, bf16[512,1536]{1,0:T(8,128)(2,1)S(1)}, u32[]{:S(2)}, u32[]{:S(2)}) collective-permute-start(bf16[512,1536]{1,0:T(8,128)(2,1)S(1)} %copy-done.57), channel_id=1, source_target_pairs={{0,1},{1,0},{2,3},{3,2},{4,5},{5,4},{6,7},{7,6},{8,9},{9,8},{10,11... | collective-permute-start | bytes 4718600 | tf_op jit(solution)/shard_map/ppermute | solution.py:149
  313.7 20.4 %collective-permute-start.55 = (bf16[3,384,256]{2,1,0:T(8,128)(2,1)S(1)}, bf16[3,384,256]{2,1,0:T(8,128)(2,1)S(1)}, u32[]{:S(2)}, u32[]{:S(2)}) collective-permute-start(bf16[3,384,256]{2,1,0:T(8,128)(2,1)S(1)} %copy-done.103), channel_id=1, source_target_pairs={{24,16},{26,18},{28,20},{30,22},{25,17},{27,19},{29,21},{31,23}} | collective-permute-start | bytes 1769480 | tf_op jit(solution)/shard_map/ppermute | solution.py:178
  314.6 22.9 %collective-permute-start.53 = (bf16[3,384,256]{2,1,0:T(8,128)(2,1)S(1)}, bf16[3,384,256]{2,1,0:T(8,128)(2,1)S(1)}, u32[]{:S(2)}, u32[]{:S(2)}) collective-permute-start(bf16[3,384,256]{2,1,0:T(8,128)(2,1)S(1)} %fusion.74), channel_id=1, source_target_pairs={{0,8},{2,10},{4,12},{6,14},{8,16},{10,18},{12,20},{14,22},{1,9},{3... | collective-permute-start | bytes 1769480 | tf_op jit(solution)/shard_map/ppermute | solution.py:177
  328.5 11.5 %collective-permute-start.61 = (bf16[3,384,256]{2,1,0:T(8,128)(2,1)S(1)}, bf16[3,384,256]{2,1,0:T(8,128)(2,1)S(1)}, u32[]{:S(2)}, u32[]{:S(2)}) collective-permute-start(bf16[3,384,256]{2,1,0:T(8,128)(2,1)S(1)} %copy-done.102), channel_id=1, source_target_pairs={{24,16},{26,18},{28,20},{30,22},{25,17},{27,19},{29,21},{31,23}} | collective-permute-start | bytes 1769480 | tf_op jit(solution)/shard_map/ppermute | solution.py:178
  329.2 19.3 %collective-permute-start.59 = (bf16[3,384,256]{2,1,0:T(8,128)(2,1)S(1)}, bf16[3,384,256]{2,1,0:T(8,128)(2,1)S(1)}, u32[]{:S(2)}, u32[]{:S(2)}) collective-permute-start(bf16[3,384,256]{2,1,0:T(8,128)(2,1)S(1)} %fusion.68), channel_id=1, source_target_pairs={{0,8},{2,10},{4,12},{6,14},{8,16},{10,18},{12,20},{14,22},{1,9},{3... | collective-permute-start | bytes 1769480 | tf_op jit(solution)/shard_map/ppermute | solution.py:177
  334.1 159.9 %collective-permute-start.25 = (bf16[4,144,768]{2,1,0:T(8,128)(2,1)}, bf16[4,144,768]{2,1,0:T(8,128)(2,1)}, u32[]{:S(2)}, u32[]{:S(2)}) collective-permute-start(bf16[4,144,768]{2,1,0:T(8,128)(2,1)} %pad_maximum_fusion.12), channel_id=1, source_target_pairs={{0,4},{2,6},{4,0},{6,2},{8,12},{10,14},{12,8},{14,10},{16,20},{18,... | collective-permute-start | bytes 2654216 | tf_op jit(solution)/shard_map/ppermute | solution.py:185
  337.5 159.8 %collective-permute-start.22 = (bf16[4,144,768]{2,1,0:T(8,128)(2,1)}, bf16[4,144,768]{2,1,0:T(8,128)(2,1)}, u32[]{:S(2)}, u32[]{:S(2)}) collective-permute-start(bf16[4,144,768]{2,1,0:T(8,128)(2,1)} %pad_maximum_fusion.10), channel_id=1, source_target_pairs={{0,2},{2,0},{4,6},{6,4},{8,10},{10,8},{12,14},{14,12},{16,18},{18,... | collective-permute-start | bytes 2654216 | tf_op jit(solution)/shard_map/ppermute | solution.py:185
  340.0 154.7 %collective-permute-start.27 = (bf16[4,144,768]{2,1,0:T(8,128)(2,1)}, bf16[4,144,768]{2,1,0:T(8,128)(2,1)}, u32[]{:S(2)}, u32[]{:S(2)}) collective-permute-start(bf16[4,144,768]{2,1,0:T(8,128)(2,1)} %add_convert_fusion.8), channel_id=1, source_target_pairs={{0,2},{2,0},{4,6},{6,4},{8,10},{10,8},{12,14},{14,12},{16,18},{18,... | collective-permute-start | bytes 2654216 | tf_op jit(solution)/shard_map/ppermute | solution.py:187
  348.5 150.1 %collective-permute-start.24 = (bf16[4,144,768]{2,1,0:T(8,128)(2,1)}, bf16[4,144,768]{2,1,0:T(8,128)(2,1)}, u32[]{:S(2)}, u32[]{:S(2)}) collective-permute-start(bf16[4,144,768]{2,1,0:T(8,128)(2,1)} %add_convert_fusion.10), channel_id=1, source_target_pairs={{0,4},{2,6},{4,0},{6,2},{8,12},{10,14},{12,8},{14,10},{16,20},{18,... | collective-permute-start | bytes 2654216 | tf_op jit(solution)/shard_map/ppermute | solution.py:187
  350.4 137.5 %collective-permute-start.50 = (bf16[3,384,256]{2,1,0:T(8,128)(2,1)}, bf16[3,384,256]{2,1,0:T(8,128)(2,1)}, u32[]{:S(2)}, u32[]{:S(2)}) collective-permute-start(bf16[3,384,256]{2,1,0:T(8,128)(2,1)} %get-tuple-element.52), channel_id=1, source_target_pairs={{16,8},{18,10},{20,12},{22,14},{24,16},{26,18},{28,20},{30,22},{17... | collective-permute-start | bytes 1769480 | tf_op jit(solution)/shard_map/ppermute | solution.py:178
  488.3 19.9 %collective-permute-start.48 = (bf16[3,384,256]{2,1,0:T(8,128)(2,1)S(1)}, bf16[3,384,256]{2,1,0:T(8,128)(2,1)S(1)}, u32[]{:S(2)}, u32[]{:S(2)}) collective-permute-start(bf16[3,384,256]{2,1,0:T(8,128)(2,1)S(1)} %copy-done.99), channel_id=1, source_target_pairs={{0,8},{2,10},{4,12},{6,14},{8,16},{10,18},{12,20},{14,22},{16,24},... | collective-permute-start | bytes 1769480 | tf_op jit(solution)/shard_map/ppermute | solution.py:177
  494.0 13.1 %collective-permute-start.56 = (bf16[3,384,256]{2,1,0:T(8,128)(2,1)S(1)}, bf16[3,384,256]{2,1,0:T(8,128)(2,1)S(1)}, u32[]{:S(2)}, u32[]{:S(2)}) collective-permute-start(bf16[3,384,256]{2,1,0:T(8,128)(2,1)S(1)} %copy-done.100), channel_id=1, source_target_pairs={{16,8},{18,10},{20,12},{22,14},{24,16},{26,18},{28,20},{30,22},{17... | collective-permute-start | bytes 1769480 | tf_op jit(solution)/shard_map/ppermute | solution.py:178
  494.7 23.0 %collective-permute-start.62 = (bf16[3,384,256]{2,1,0:T(8,128)(2,1)S(1)}, bf16[3,384,256]{2,1,0:T(8,128)(2,1)S(1)}, u32[]{:S(2)}, u32[]{:S(2)}) collective-permute-start(bf16[3,384,256]{2,1,0:T(8,128)(2,1)S(1)} %copy-done.101), channel_id=1, source_target_pairs={{16,8},{18,10},{20,12},{22,14},{24,16},{26,18},{28,20},{30,22},{17... | collective-permute-start | bytes 1769480 | tf_op jit(solution)/shard_map/ppermute | solution.py:178
  497.3 35.7 %collective-permute-start.51 = (bf16[3,384,256]{2,1,0:T(8,128)(2,1)S(1)}, bf16[3,384,256]{2,1,0:T(8,128)(2,1)S(1)}, u32[]{:S(2)}, u32[]{:S(2)}) collective-permute-start(bf16[3,384,256]{2,1,0:T(8,128)(2,1)S(1)} %fusion.79), channel_id=1, source_target_pairs={{8,0},{10,2},{12,4},{14,6},{16,8},{18,10},{20,12},{22,14},{24,16},... | collective-permute-start | bytes 1769480 | tf_op jit(solution)/shard_map/ppermute | solution.py:178
  500.5 18.7 %collective-permute-start.28 = (bf16[288,768]{1,0:T(8,128)(2,1)S(1)}, bf16[288,768]{1,0:T(8,128)(2,1)S(1)}, u32[]{:S(2)}, u32[]{:S(2)}) collective-permute-start(bf16[288,768]{1,0:T(8,128)(2,1)S(1)} %get-tuple-element.81), channel_id=1, source_target_pairs={{0,8},{2,10},{4,12},{6,14},{1,9},{3,11},{5,13},{7,15}} | collective-permute-start | bytes 1327112 | tf_op jit(solution)/shard_map/ppermute | solution.py:177
  507.1 24.3 %collective-permute-start.31 = (bf16[288,768]{1,0:T(8,128)(2,1)S(1)}, bf16[288,768]{1,0:T(8,128)(2,1)S(1)}, u32[]{:S(2)}, u32[]{:S(2)}) collective-permute-start(bf16[288,768]{1,0:T(8,128)(2,1)S(1)} %get-tuple-element.82), channel_id=1, source_target_pairs={{24,16},{26,18},{28,20},{30,22},{25,17},{27,19},{29,21},{31,23}} | collective-permute-start | bytes 1327112 | tf_op jit(solution)/shard_map/ppermute | solution.py:178
  508.2 26.7 %collective-permute-start.54 = (bf16[3,384,256]{2,1,0:T(8,128)(2,1)S(1)}, bf16[3,384,256]{2,1,0:T(8,128)(2,1)S(1)}, u32[]{:S(2)}, u32[]{:S(2)}) collective-permute-start(bf16[3,384,256]{2,1,0:T(8,128)(2,1)S(1)} %copy-done.97), channel_id=1, source_target_pairs={{0,8},{2,10},{4,12},{6,14},{8,16},{10,18},{12,20},{14,22},{16,24},... | collective-permute-start | bytes 1769480 | tf_op jit(solution)/shard_map/ppermute | solution.py:177
  517.8 25.4 %collective-permute-start.57 = (bf16[3,384,256]{2,1,0:T(8,128)(2,1)S(1)}, bf16[3,384,256]{2,1,0:T(8,128)(2,1)S(1)}, u32[]{:S(2)}, u32[]{:S(2)}) collective-permute-start(bf16[3,384,256]{2,1,0:T(8,128)(2,1)S(1)} %fusion.73), channel_id=1, source_target_pairs={{8,0},{10,2},{12,4},{14,6},{16,8},{18,10},{20,12},{22,14},{24,16},... | collective-permute-start | bytes 1769480 | tf_op jit(solution)/shard_map/ppermute | solution.py:178
  519.2 25.5 %collective-permute-start.60 = (bf16[3,384,256]{2,1,0:T(8,128)(2,1)S(1)}, bf16[3,384,256]{2,1,0:T(8,128)(2,1)S(1)}, u32[]{:S(2)}, u32[]{:S(2)}) collective-permute-start(bf16[3,384,256]{2,1,0:T(8,128)(2,1)S(1)} %copy-done.98), channel_id=1, source_target_pairs={{0,8},{2,10},{4,12},{6,14},{8,16},{10,18},{12,20},{14,22},{16,24},... | collective-permute-start | bytes 1769480 | tf_op jit(solution)/shard_map/ppermute | solution.py:177
  531.5 24.7 %collective-permute-start.63 = (bf16[3,384,256]{2,1,0:T(8,128)(2,1)S(1)}, bf16[3,384,256]{2,1,0:T(8,128)(2,1)S(1)}, u32[]{:S(2)}, u32[]{:S(2)}) collective-permute-start(bf16[3,384,256]{2,1,0:T(8,128)(2,1)S(1)} %fusion.67), channel_id=1, source_target_pairs={{8,0},{10,2},{12,4},{14,6},{16,8},{18,10},{20,12},{22,14},{24,16},... | collective-permute-start | bytes 1769480 | tf_op jit(solution)/shard_map/ppermute | solution.py:178
  533.0 31.4 %collective-permute-start.14 = (bf16[4,192,768]{2,1,0:T(8,128)(2,1)S(1)}, bf16[4,192,768]{2,1,0:T(8,128)(2,1)S(1)}, u32[]{:S(2)}, u32[]{:S(2)}) collective-permute-start(bf16[4,192,768]{2,1,0:T(8,128)(2,1)S(1)} %pad_maximum_fusion.9), channel_id=1, source_target_pairs={{0,4},{2,6},{4,0},{6,2},{8,12},{10,14},{12,8},{14,10},{16,20},{18,... | collective-permute-start | bytes 3538952 | tf_op jit(solution)/shard_map/ppermute | solution.py:184
  534.9 82.7 %collective-permute-start.13 = (bf16[4,192,768]{2,1,0:T(8,128)(2,1)S(1)}, bf16[4,192,768]{2,1,0:T(8,128)(2,1)S(1)}, u32[]{:S(2)}, u32[]{:S(2)}) collective-permute-start(bf16[4,192,768]{2,1,0:T(8,128)(2,1)S(1)} %pad_maximum_fusion.8), channel_id=1, source_target_pairs={{0,4},{2,6},{4,0},{6,2},{8,12},{10,14},{12,8},{14,10},{16,20},{18,... | collective-permute-start | bytes 3538952 | tf_op jit(solution)/shard_map/ppermute | solution.py:185
  543.2 22.9 %collective-permute-start.11 = (bf16[4,192,768]{2,1,0:T(8,128)(2,1)S(1)}, bf16[4,192,768]{2,1,0:T(8,128)(2,1)S(1)}, u32[]{:S(2)}, u32[]{:S(2)}) collective-permute-start(bf16[4,192,768]{2,1,0:T(8,128)(2,1)S(1)} %pad_maximum_fusion.7), channel_id=1, source_target_pairs={{0,2},{2,0},{4,6},{6,4},{8,10},{10,8},{12,14},{14,12},{16,18},{18,... | collective-permute-start | bytes 3538952 | tf_op jit(solution)/shard_map/ppermute | solution.py:184
  544.8 17.1 %collective-permute-start.29 = (bf16[288,768]{1,0:T(8,128)(2,1)S(1)}, bf16[288,768]{1,0:T(8,128)(2,1)S(1)}, u32[]{:S(2)}, u32[]{:S(2)}) collective-permute-start(bf16[288,768]{1,0:T(8,128)(2,1)S(1)} %get-tuple-element.79), channel_id=1, source_target_pairs={{0,8},{2,10},{4,12},{6,14},{8,16},{10,18},{12,20},{14,22},{1,9},{3... | collective-permute-start | bytes 1327112 | tf_op jit(solution)/shard_map/ppermute | solution.py:177
  561.9 13.1 %collective-permute-start.64 = (bf16[3,96,768]{2,1,0:T(8,128)(2,1)S(1)}, bf16[3,96,768]{2,1,0:T(8,128)(2,1)S(1)}, u32[]{:S(2)}, u32[]{:S(2)}) collective-permute-start(bf16[3,96,768]{2,1,0:T(8,128)(2,1)S(1)} %get-tuple-element.76), channel_id=1, source_target_pairs={{0,2},{2,0},{4,6},{6,4},{8,10},{10,8},{12,14},{14,12},{16,18},{18,... | collective-permute-start | bytes 1327112 | tf_op jit(solution)/shard_map/ppermute | solution.py:339
  562.6 36.3 %collective-permute-start.65 = (bf16[3,96,768]{2,1,0:T(8,128)(2,1)S(1)}, bf16[3,96,768]{2,1,0:T(8,128)(2,1)S(1)}, u32[]{:S(2)}, u32[]{:S(2)}) collective-permute-start(bf16[3,96,768]{2,1,0:T(8,128)(2,1)S(1)} %get-tuple-element.75), channel_id=1, source_target_pairs={{0,4},{2,6},{4,0},{6,2},{8,12},{10,14},{12,8},{14,10},{16,20},{18,... | collective-permute-start | bytes 1327112 | tf_op jit(solution)/shard_map/ppermute | solution.py:339
  564.4 36.0 %collective-permute-start.66 = (bf16[3,96,768]{2,1,0:T(8,128)(2,1)S(1)}, bf16[3,96,768]{2,1,0:T(8,128)(2,1)S(1)}, u32[]{:S(2)}, u32[]{:S(2)}) collective-permute-start(bf16[3,96,768]{2,1,0:T(8,128)(2,1)S(1)} %get-tuple-element.74), channel_id=1, source_target_pairs={{0,6},{2,4},{4,2},{6,0},{8,14},{10,12},{12,10},{14,8},{16,22},{18,... | collective-permute-start | bytes 1327112 | tf_op jit(solution)/shard_map/ppermute | solution.py:339
  566.0 63.4 %collective-permute-start.10 = (bf16[4,192,768]{2,1,0:T(8,128)(2,1)S(1)}, bf16[4,192,768]{2,1,0:T(8,128)(2,1)S(1)}, u32[]{:S(2)}, u32[]{:S(2)}) collective-permute-start(bf16[4,192,768]{2,1,0:T(8,128)(2,1)S(1)} %pad_maximum_fusion.6), channel_id=1, source_target_pairs={{0,2},{2,0},{4,6},{6,4},{8,10},{10,8},{12,14},{14,12},{16,18},{18,... | collective-permute-start | bytes 3538952 | tf_op jit(solution)/shard_map/ppermute | solution.py:185
  575.0 27.7 %collective-permute-start.30 = (bf16[288,768]{1,0:T(8,128)(2,1)S(1)}, bf16[288,768]{1,0:T(8,128)(2,1)S(1)}, u32[]{:S(2)}, u32[]{:S(2)}) collective-permute-start(bf16[288,768]{1,0:T(8,128)(2,1)S(1)} %get-tuple-element.77), channel_id=1, source_target_pairs={{0,8},{2,10},{4,12},{6,14},{8,16},{10,18},{12,20},{14,22},{16,24},... | collective-permute-start | bytes 1327112 | tf_op jit(solution)/shard_map/ppermute | solution.py:177
  598.9 15.4 %collective-permute-start.33 = (bf16[288,768]{1,0:T(8,128)(2,1)S(1)}, bf16[288,768]{1,0:T(8,128)(2,1)S(1)}, u32[]{:S(2)}, u32[]{:S(2)}) collective-permute-start(bf16[288,768]{1,0:T(8,128)(2,1)S(1)} %get-tuple-element.78), channel_id=1, source_target_pairs={{8,0},{10,2},{12,4},{14,6},{16,8},{18,10},{20,12},{22,14},{24,16},... | collective-permute-start | bytes 1327112 | tf_op jit(solution)/shard_map/ppermute | solution.py:178
  600.4 28.5 %collective-permute-start.15 = (bf16[4,192,768]{2,1,0:T(8,128)(2,1)S(1)}, bf16[4,192,768]{2,1,0:T(8,128)(2,1)S(1)}, u32[]{:S(2)}, u32[]{:S(2)}) collective-permute-start(bf16[4,192,768]{2,1,0:T(8,128)(2,1)S(1)} %add_convert_fusion.4), channel_id=1, source_target_pairs={{0,2},{2,0},{4,6},{6,4},{8,10},{10,8},{12,14},{14,12},{16,18},{18,... | collective-permute-start | bytes 3538952 | tf_op jit(solution)/shard_map/ppermute | solution.py:187
  602.7 51.5 %collective-permute-start.5 = (bf16[512,1536]{1,0:T(8,128)(2,1)S(1)}, bf16[512,1536]{1,0:T(8,128)(2,1)S(1)}, u32[]{:S(2)}, u32[]{:S(2)}) collective-permute-start(bf16[512,1536]{1,0:T(8,128)(2,1)S(1)} %fusion.13), channel_id=1, source_target_pairs={{0,1},{1,0},{2,3},{3,2},{4,5},{5,4},{6,7},{7,6},{8,9},{9,8},{10,11... | collective-permute-start | bytes 4718600 | tf_op jit(solution)/shard_map/ppermute | solution.py:149
  614.4 20.7 %collective-permute-start.12 = (bf16[4,192,768]{2,1,0:T(8,128)(2,1)S(1)}, bf16[4,192,768]{2,1,0:T(8,128)(2,1)S(1)}, u32[]{:S(2)}, u32[]{:S(2)}) collective-permute-start(bf16[4,192,768]{2,1,0:T(8,128)(2,1)S(1)} %add_convert_fusion.6), channel_id=1, source_target_pairs={{0,4},{2,6},{4,0},{6,2},{8,12},{10,14},{12,8},{14,10},{16,20},{18,... | collective-permute-start | bytes 3538952 | tf_op jit(solution)/shard_map/ppermute | solution.py:187
  637.1 22.6 %collective-permute-start.16 = (bf16[384,768]{1,0:T(8,128)(2,1)}, bf16[384,768]{1,0:T(8,128)(2,1)}, u32[]{:S(2)}, u32[]{:S(2)}) collective-permute-start(bf16[384,768]{1,0:T(8,128)(2,1)} %get-tuple-element.67), channel_id=1, source_target_pairs={{0,8},{2,10},{4,12},{6,14},{1,9},{3,11},{5,13},{7,15}} | collective-permute-start | bytes 1769480 | tf_op jit(solution)/shard_map/ppermute | solution.py:177
  655.9 12.7 %collective-permute-start.6 = (f32[6,1536]{1,0:T(8,128)S(1)}, f32[6,1536]{1,0:T(8,128)S(1)}, u32[]{:S(2)}, u32[]{:S(2)}) collective-permute-start(f32[6,1536]{1,0:T(8,128)S(1)} %stack.42), channel_id=1, source_target_pairs={{0,2},{2,0},{4,6},{6,4},{8,10},{10,8},{12,14},{14,12},{16,18},{18,... | collective-permute-start | bytes 110600 | tf_op jit(solution)/shard_map/ppermute | solution.py:359
  661.7 27.0 %collective-permute-start.17 = (bf16[384,768]{1,0:T(8,128)(2,1)S(1)}, bf16[384,768]{1,0:T(8,128)(2,1)S(1)}, u32[]{:S(2)}, u32[]{:S(2)}) collective-permute-start(bf16[384,768]{1,0:T(8,128)(2,1)S(1)} %get-tuple-element.65), channel_id=1, source_target_pairs={{0,8},{2,10},{4,12},{6,14},{8,16},{10,18},{12,20},{14,22},{1,9},{3... | collective-permute-start | bytes 1769480 | tf_op jit(solution)/shard_map/ppermute | solution.py:177
  666.1 22.6 %collective-permute-start.20 = (bf16[384,768]{1,0:T(8,128)(2,1)S(1)}, bf16[384,768]{1,0:T(8,128)(2,1)S(1)}, u32[]{:S(2)}, u32[]{:S(2)}) collective-permute-start(bf16[384,768]{1,0:T(8,128)(2,1)S(1)} %get-tuple-element.66), channel_id=1, source_target_pairs={{16,8},{18,10},{20,12},{22,14},{24,16},{26,18},{28,20},{30,22},{17... | collective-permute-start | bytes 1769480 | tf_op jit(solution)/shard_map/ppermute | solution.py:178
  672.7 11.3 %collective-permute-start.8 = (f32[6,1536]{1,0:T(8,128)S(1)}, f32[6,1536]{1,0:T(8,128)S(1)}, u32[]{:S(2)}, u32[]{:S(2)}) collective-permute-start(f32[6,1536]{1,0:T(8,128)S(1)} %add.529), channel_id=1, source_target_pairs={{0,8},{2,10},{4,12},{6,14},{8,0},{10,2},{12,4},{14,6},{16,24},{18,... | collective-permute-start | bytes 110600 | tf_op jit(solution)/shard_map/ppermute | solution.py:359
  684.1 11.3 %collective-permute-start.9 = (f32[6,1536]{1,0:T(8,128)S(1)}, f32[6,1536]{1,0:T(8,128)S(1)}, u32[]{:S(2)}, u32[]{:S(2)}) collective-permute-start(f32[6,1536]{1,0:T(8,128)S(1)} %add.530), channel_id=1, source_target_pairs={{0,16},{2,18},{4,20},{6,22},{8,24},{10,26},{12,28},{14,30},{16,0},... | collective-permute-start | bytes 110600 | tf_op jit(solution)/shard_map/ppermute | solution.py:359
  689.1 9.6 %collective-permute-start.18 = (bf16[384,768]{1,0:T(8,128)(2,1)S(1)}, bf16[384,768]{1,0:T(8,128)(2,1)S(1)}, u32[]{:S(2)}, u32[]{:S(2)}) collective-permute-start(bf16[384,768]{1,0:T(8,128)(2,1)S(1)} %get-tuple-element.63), channel_id=1, source_target_pairs={{0,8},{2,10},{4,12},{6,14},{8,16},{10,18},{12,20},{14,22},{16,24},... | collective-permute-start | bytes 1769480 | tf_op jit(solution)/shard_map/ppermute | solution.py:177
  691.4 11.8 %collective-permute-start.21 = (bf16[384,768]{1,0:T(8,128)(2,1)S(1)}, bf16[384,768]{1,0:T(8,128)(2,1)S(1)}, u32[]{:S(2)}, u32[]{:S(2)}) collective-permute-start(bf16[384,768]{1,0:T(8,128)(2,1)S(1)} %get-tuple-element.64), channel_id=1, source_target_pairs={{8,0},{10,2},{12,4},{14,6},{16,8},{18,10},{20,12},{22,14},{24,16},... | collective-permute-start | bytes 1769480 | tf_op jit(solution)/shard_map/ppermute | solution.py:178
  (164 other events, 1483.8 us)

commit v3 on v2

--- a/solution.py
+++ b/solution.py
@@ -1,3 +1,4 @@
+import functools
 import math
 
 import jax
@@ -9,6 +10,12 @@
 
 PROMPT = 128
 HEAD = 64
+PLANE = 4
+LEVELS = 4
+
+low = jnp.bfloat16
+f32 = jnp.float32
+sds = jax.ShapeDtypeStruct
 
 
 norm_eps = 1e-05
@@ -155,6 +162,26 @@
     return [(i, i ^ mask) for i in range(16)]
 
 
+def vector_sum(vectors):
+    if lax.axis_size("dp") == PLANE * LEVELS:
+        for mask in (1, 2, 4, 8):
+            vectors = vectors + lax.ppermute(vectors, "dp", pairs(mask))
+    else:
+        vectors = lax.psum(vectors, "dp")
+    share = vectors.shape[1] // (lax.axis_size("dp") * lax.axis_size("tensor"))
+    index = lax.axis_index("dp") * lax.axis_size("tensor") + lax.axis_index("tensor")
+    return lax.dynamic_slice_in_dim(vectors, index * share, share, 1)
+
+
+def generic_sum(rows_side, column_side):
+    return lax.psum_scatter(
+        product_over_rows(rows_side, column_side).astype(jnp.bfloat16),
+        "dp",
+        scatter_dimension=0,
+        tiled=True,
+    ).astype(jnp.float32)
+
+
 def add_low(*terms):
     total = terms[0].astype(jnp.float32)
     for term in terms[1:]:
@@ -162,25 +189,28 @@
     return total
 
 
-def z_scatter(own, z_index):
-    def block(offset):
-        return lax.dynamic_index_in_dim(own, jnp.clip(z_index + offset, 0, 3), 0, keepdims=False)
-
-    up = down = None
-    for step in range(1, 4):
-        up_perm = [(i, i + 4) for i in range(16) if i // 4 <= step - 1 and i // 4 < 3]
-        down_perm = [(i, i - 4) for i in range(16) if i // 4 >= 4 - step and i // 4 > 0]
-        up_send, down_send = block(4 - step), block(step - 4)
-        if up is not None:
-            up_send = add_low(up_send, up).astype(jnp.bfloat16)
-            down_send = add_low(down_send, down).astype(jnp.bfloat16)
-        up = lax.ppermute(up_send, "dp", up_perm)
-        down = lax.ppermute(down_send, "dp", down_perm)
-    return add_low(block(0), up, down)
+def z_halve(send, keep, level):
+    upper = level // 2
+    got = lax.ppermute(send, "dp", pairs(PLANE))
+
+    def half(values, index):
+        return lax.dynamic_index_in_dim(values, index, 0, keepdims=False)
+
+    passed = add_low(half(keep, 1 - upper), half(got, 1 - upper)).astype(low)
+    last = lax.ppermute(passed, "dp", pairs(2 * PLANE))
+    return add_low(half(keep, upper), half(got, upper), last)
+
+
+def z_scatter(own, level):
+    split = own.reshape(2, 2, *own.shape[1:])
+
+    def half(parity):
+        return lax.dynamic_index_in_dim(split, parity, 1, keepdims=False)
+
+    return z_halve(half(1 - level % 2), half(level % 2), level)
 
 
 def plane_scatter(parts, first):
-    low = jnp.bfloat16
     got_diag = lax.ppermute(parts[3], "dp", pairs(first))
     got_own = lax.ppermute(parts[first], "dp", pairs(first))
     passed = add_low(parts[3 - first], got_diag).astype(low)
@@ -188,20 +218,6 @@
     return add_low(parts[0], got_own, got_last).astype(low)
 
 
-def quarter_products(rows_side, column_side, mine):
-    turned = rows_side.T.reshape(4, 4, rows_side.shape[1] // 16, rows_side.shape[0])
-    out = []
-    for flip in range(4):
-        part = lax.dynamic_index_in_dim(turned, mine ^ flip, 1, keepdims=False)
-        product = product_plain(part.reshape(-1, part.shape[2]), column_side)
-        out.append(product.astype(jnp.bfloat16).reshape(4, -1, column_side.shape[1]))
-    return out
-
-
-def stacked(*products):
-    return [jnp.concatenate(part, axis=1) for part in zip(*products)]
-
-
 def plane_gather(own_half, mask_list=(1, 2, 3)):
     got = [lax.ppermute(own_half, "dp", pairs(mask)) for mask in mask_list]
     other = [lax.ppermute(part, "tensor", [(0, 1), (1, 0)]) for part in got]
@@ -211,7 +227,6 @@
 def ff_parts(gate, up, grad_mixed):
     sig = 1.0 / (1.0 + jnp.exp(-gate))
     act = gate * sig
-    low = jnp.bfloat16
     return (
         (act * up).astype(low),
         (grad_mixed * up * sig * (1.0 + gate * (1.0 - sig))).astype(low),
@@ -268,7 +283,7 @@
     )(normed, grad_out, w_gate, w_up, w_down)
 
 
-def share_kernel(_, in_ref, out_ref, gate_ref, up_ref, down_ref, grad_ref, acc):
+def share_kernel(info, in_ref, out_ref, gate_ref, up_ref, down_ref, send_ref, keep_ref, acc):
     step = pl.program_id(0)
     normed, grad_out = in_ref[...], out_ref[...]
     mixed, grad_gate, grad_up = ff_parts(
@@ -293,19 +308,20 @@
 
     @pl.when(step == pl.num_programs(0) - 1)
     def _():
-        rows = grad_ref.shape[2]
-        for block in range(grad_ref.shape[0]):
+        rows = send_ref.shape[2]
+        for pair in range(2):
             for index in range(3):
-                grad_ref[block, index] = acc[index, block * rows : (block + 1) * rows].astype(
-                    grad_ref.dtype
-                )
-
-
-def ff_share(normed, grad_out, w_gate, w_up, w_down, first_tile, tile):
+                for ref, parity in ((send_ref, 1 - info[1]), (keep_ref, info[1])):
+                    start = pl.multiple_of((2 * pair + parity) * rows, rows)
+                    ref[pair, index] = acc[index, pl.ds(start, rows), :].astype(ref.dtype)
+
+
+def ff_share(info, normed, grad_out, w_gate, w_up, w_down, tile):
     frames, width = normed.shape
     chunk = 512
-    rows = pl.BlockSpec((chunk, width), lambda j, first: (j, 0))
-    column = pl.BlockSpec((width, tile), lambda j, first: (0, first[0]))
+    rows = pl.BlockSpec((chunk, width), lambda j, info: (j, 0))
+    column = pl.BlockSpec((width, tile), lambda j, info: (0, info[0]))
+    half = (LEVELS // 2, 3, width // LEVELS, tile)
     return pl.pallas_call(
         share_kernel,
         grid_spec=pltpu.PrefetchScalarGridSpec(
@@ -316,19 +332,19 @@
                 rows,
                 column,
                 column,
-                pl.BlockSpec((tile, width), lambda j, first: (first[0], 0)),
+                pl.BlockSpec((tile, width), lambda j, info: (info[0], 0)),
             ],
-            out_specs=pl.BlockSpec((4, 3, width // 4, tile), lambda j, first: (0, 0, 0, 0)),
-            scratch_shapes=[pltpu.VMEM((3, width, tile), jnp.float32)],
+            out_specs=[pl.BlockSpec(half, lambda j, info: (0, 0, 0, 0))] * 2,
+            scratch_shapes=[pltpu.VMEM((3, width, tile), f32)],
         ),
-        out_shape=jax.ShapeDtypeStruct((4, 3, width // 4, tile), jnp.bfloat16),
+        out_shape=[sds(half, low)] * 2,
         compiler_params=pltpu.CompilerParams(vmem_limit_bytes=44 * 2**20),
         cost_estimate=pl.CostEstimate(
             flops=12 * frames * width * tile,
             bytes_accessed=4 * frames * width + 12 * width * tile,
             transcendentals=frames * tile,
         ),
-    )(first_tile.reshape(1), normed, grad_out, w_gate, w_up, w_down)
+    )(info, normed, grad_out, w_gate, w_up, w_down)
 
 
 def spread_units(mine, plane, parts=3):
@@ -344,27 +360,313 @@
     return jnp.concatenate(columns, axis=2).astype(jnp.float32)
 
 
-def generic_sum(rows_side, column_side):
-    return lax.psum_scatter(
-        product_over_rows(rows_side, column_side).astype(jnp.bfloat16),
-        "dp",
-        scatter_dimension=0,
-        tiled=True,
-    ).astype(jnp.float32)
-
-
-def vector_sum(vectors):
-    if lax.axis_size("dp") == 16:
-        for mask in (1, 2, 4, 8):
-            vectors = vectors + lax.ppermute(vectors, "dp", pairs(mask))
-    else:
-        vectors = lax.psum(vectors, "dp")
-    share = vectors.shape[1] // (lax.axis_size("dp") * lax.axis_size("tensor"))
-    index = lax.axis_index("dp") * lax.axis_size("tensor") + lax.axis_index("tensor")
-    return lax.dynamic_slice_in_dim(vectors, index * share, share, 1)
-
-
-def on_device(
+def turn(values, cos, lower, upper):
+    width = values.shape[1]
+    return (values * cos + pltpu.roll(values, width - 16, 1) * lower + pltpu.roll(values, 16, 1) * upper)
+
+def turn_back(values, cos, lower, upper):
+    width = values.shape[1]
+    return (values * cos + pltpu.roll(values * lower, 16, 1) + pltpu.roll(values * upper, width - 16, 1))
+
+def normed_rows(values, gain, shift):
+    average = jnp.mean(values, axis=-1, keepdims=True)
+    centered = values - average
+    variance = jnp.mean(centered * centered, axis=-1, keepdims=True)
+    return centered * lax.rsqrt(variance + norm_eps) * gain + shift
+
+def over_rows(rows, body, chunk=32):
+    @pl.loop(0, rows // chunk, unroll=min(4, rows // chunk))
+    def _(i):
+        body(pl.ds(pl.multiple_of(i * chunk, chunk), chunk))
+
+def attend(q, k, v, mask, lse_ref):
+    q_turned = (q * jnp.bfloat16(0.125)).T
+    v_turned = v.T
+    outs = []
+    for h in range(q.shape[1] // HEAD):
+        c = slice(h * HEAD, (h + 1) * HEAD)
+        s = product_plain(k[:, c], q_turned[c, :]) + mask
+        m = jnp.max(s, axis=0, keepdims=True)
+        e = jnp.exp(s - m)
+        total = jnp.sum(e, axis=0, keepdims=True)
+        o = product_plain(v_turned[c, :], e.astype(low)) * (1.0 / total)
+        outs.append(o)
+        lse_ref[h : h + 1, :] = m + jnp.log(total)
+    return jnp.concatenate(outs, axis=0).T.astype(low)
+
+
+def attend_back(q, k, v, g, mask, lse):
+    scaled = q * jnp.bfloat16(0.125)
+    q_turned = scaled.T
+    g_turned = g.T
+    k_turned = k.T
+    dq, dk, dv = [], [], []
+    for h in range(q.shape[1] // HEAD):
+        c = slice(h * HEAD, (h + 1) * HEAD)
+        p = jnp.exp(product_plain(k[:, c], q_turned[c, :]) + (mask - lse[h : h + 1, :]))
+        dp = product_plain(v[:, c], g_turned[c, :])
+        inner = jnp.sum(p * dp, axis=0, keepdims=True)
+        ds = (p * (dp - inner)).astype(low)
+        dq.append(product_plain(k_turned[c, :], ds))
+        dk.append(product_plain(ds, scaled[:, c]))
+        dv.append(product_plain(p.astype(low), g[:, c]))
+    return (
+        jnp.concatenate(dq, axis=0).T * 0.125,
+        jnp.concatenate(dk, axis=1),
+        jnp.concatenate(dv, axis=1),
+    )
+
+
+def self_mask(split, T):
+    r=lax.broadcasted_iota(jnp.int32,(T,T),0)>=split
+    c=lax.broadcasted_iota(jnp.int32,(T,T),1)>=split
+    return jnp.where(r==c,0.0,masked_score).astype(f32)
+
+def cross_mask(split, first, second, T, K):
+    r = lax.broadcasted_iota(jnp.int32, (K, T), 1) >= split
+    c = lax.broadcasted_iota(jnp.int32, (K, T), 0)
+    least = jnp.where(r, K // 2, 0)
+    most = jnp.where(r, K // 2 + second, first)
+    return jnp.where((c >= least) & (c < most), 0.0, masked_score).astype(f32)
+
+
+def self_kernel(info, hid, gain, shift, wq, wk, wv, wo, cos, lower, upper, in1, q, k, v, att, lse, part, acc, mask):
+    step=pl.program_id(0)
+    T=hid.shape[0]
+    @pl.when(step==0)
+    def _():
+        def rows(r):
+            in1[r,:]=normed_rows(hid[r,:],gain[...],shift[...]).astype(low)
+        over_rows(T,rows)
+        mask[...]=self_mask(info[0],T)
+    n=in1[...]
+    tabs=(cos[...],lower[...],upper[...])
+    q[...]=turn(product_plain(n,wq[...]),*tabs).astype(low)
+    k[...]=turn(product_plain(n,wk[...]),*tabs).astype(low)
+    v[...]=product_plain(n,wv[...]).astype(low)
+    a=attend(q[...],k[...],v[...],mask[...],lse)
+    att[...]=a
+    term=product_plain(a,wo[...])
+    @pl.when(step==0)
+    def _(): acc[...]=term
+    @pl.when(step!=0)
+    def _(): acc[...]+=term
+    @pl.when(step==pl.num_programs(0)-1)
+    def _(): part[...]=acc[...].astype(low)
+
+def specs(T,D,tile):
+    whole=pl.BlockSpec((T,D),lambda j,*_:(0,0))
+    vec=pl.BlockSpec((1,D),lambda j,*_:(0,0))
+    col=pl.BlockSpec((D,tile),lambda j,*_:(0,j))
+    row=pl.BlockSpec((tile,D),lambda j,*_:(j,0))
+    act=pl.BlockSpec((T,tile),lambda j,*_:(0,j))
+    tab=pl.BlockSpec((T,tile),lambda j,*_:(0,0))
+    lse=pl.BlockSpec((8,T),lambda j,*_:(j,0))
+    return whole,vec,col,row,act,tab,lse
+PARAMS=dict(compiler_params=pltpu.CompilerParams(vmem_limit_bytes=48*2**20))
+
+def self_forward(info,hid,gain,shift,wq,wk,wv,wo,tabs,tile=256):
+    T,D=hid.shape;C=wq.shape[1]
+    whole,vec,col,row,act,tab,lse=specs(T,D,tile)
+    return pl.pallas_call(self_kernel,grid_spec=pltpu.PrefetchScalarGridSpec(num_scalar_prefetch=1,grid=(C//tile,),
+        in_specs=[whole,vec,vec,col,col,col,row,tab,tab,tab],
+        out_specs=[whole,act,act,act,act,lse,whole],
+        scratch_shapes=[pltpu.VMEM((T,D),f32),pltpu.VMEM((T,T),f32)]),
+        out_shape=[sds((T,D),low)]+[sds((T,C),low)]*4+[sds((C//tile*8,T),f32),sds((T,D),low)],
+        cost_estimate=pl.CostEstimate(flops=2*T*C*(4*D+2*T*4),bytes_accessed=8*D*C+4*T*D+8*T*D,transcendentals=T*T*C//HEAD),
+        **PARAMS)(info,hid,gain,shift,wq,wk,wv,wo,*tabs)
+
+def cross_kernel(info, hid, mine, other, gain, shift, cq, ck, cv, co, res, in2, q, att, lse, part, acc, mask):
+    step=pl.program_id(0)
+    T=hid.shape[0]
+    @pl.when(step==0)
+    def _():
+        def rows(r):
+            x=hid[r,:]+(mine[r,:].astype(f32)+other[r,:].astype(f32))
+            res[r,:]=x
+            in2[r,:]=normed_rows(x,gain[...],shift[...]).astype(low)
+        over_rows(T,rows)
+        mask[...]=cross_mask(info[0],info[1],info[2],T,ck.shape[0])
+    q[...]=product_plain(in2[...],cq[...]).astype(low)
+    a=attend(q[...],ck[...],cv[...],mask[...],lse)
+    att[...]=a
+    term=product_plain(a,co[...])
+    @pl.when(step==0)
+    def _(): acc[...]=term
+    @pl.when(step!=0)
+    def _(): acc[...]+=term
+    @pl.when(step==pl.num_programs(0)-1)
+    def _(): part[...]=acc[...].astype(low)
+
+def cross_forward(info,hid,mine,other,gain,shift,cq,ck,cv,co,tile=256):
+    T,D=hid.shape;C=cq.shape[1];K=ck.shape[0]
+    whole,vec,col,row,act,tab,lse=specs(T,D,tile)
+    key=pl.BlockSpec((K,tile),lambda j,*_:(0,j))
+    return pl.pallas_call(cross_kernel,grid_spec=pltpu.PrefetchScalarGridSpec(num_scalar_prefetch=1,grid=(C//tile,),
+        in_specs=[whole,whole,whole,vec,vec,col,key,key,row],
+        out_specs=[whole,whole,act,act,lse,whole],
+        scratch_shapes=[pltpu.VMEM((T,D),f32),pltpu.VMEM((K,T),f32)]),
+        out_shape=[sds((T,D),f32),sds((T,D),low),sds((T,C),low),sds((T,C),low),sds((C//tile*8,T),f32),sds((T,D),low)],
+        cost_estimate=pl.CostEstimate(flops=2*T*C*(2*D+2*K*4),bytes_accessed=4*D*C+4*T*D+14*T*D,transcendentals=T*K*C//HEAD),
+        **PARAMS)(info,hid,mine,other,gain,shift,cq,ck,cv,co)
+
+def norm_kernel(hid,mine,other,gain,shift,res,out):
+    def rows(r):
+        x=hid[r,:]+(mine[r,:].astype(f32)+other[r,:].astype(f32))
+        res[r,:]=x
+        out[r,:]=normed_rows(x,gain[...],shift[...]).astype(low)
+    over_rows(hid.shape[0],rows)
+
+def norm_forward(hid,mine,other,gain,shift,block=128):
+    T,D=hid.shape
+    b=pl.BlockSpec((block,D),lambda j:(j,0)); vec=pl.BlockSpec((1,D),lambda j:(0,0))
+    return pl.pallas_call(norm_kernel,grid=(T//block,),in_specs=[b,b,b,vec,vec],out_specs=[b,b],
+        out_shape=[sds((T,D),f32),sds((T,D),low)],
+        cost_estimate=pl.CostEstimate(flops=10*T*D,bytes_accessed=14*T*D,transcendentals=T),**PARAMS)(hid,mine,other,gain,shift)
+
+def norm_back_rows(x,e,gain,above,sums,gain_acc,shift_acc):
+    average=jnp.mean(x,axis=-1,keepdims=True)
+    centered=x-average
+    variance=jnp.mean(centered*centered,axis=-1,keepdims=True)
+    inverse=lax.rsqrt(variance+norm_eps)
+    n=centered*inverse
+    en=e*n
+    w=e*gain
+    mean_w=jnp.mean(w,axis=-1,keepdims=True)
+    mean_wn=jnp.mean(en*gain,axis=-1,keepdims=True)
+    fold=lambda t: jnp.sum(t.reshape(t.shape[0]//8,8,t.shape[1]),axis=0)
+    gain_acc[...]+=fold(en)
+    shift_acc[...]+=fold(e)
+    return above+inverse*(w-mean_w-n*mean_wn)
+
+def norm_back_all(x,mine,other,above,gain,total,total_low,vec,gacc,sacc):
+    gacc[...]=jnp.zeros_like(gacc);sacc[...]=jnp.zeros_like(sacc)
+    def rows(r):
+        e=mine[r,:].astype(f32)+other[r,:].astype(f32)
+        t=norm_back_rows(x[r,:],e,gain[...],above[r,:],None,gacc,sacc)
+        total[r,:]=t
+        if total_low is not None: total_low[r,:]=t.astype(low)
+    over_rows(x.shape[0],rows)
+    vec[0:1,:]=jnp.sum(gacc[...],axis=0,keepdims=True)
+    vec[1:2,:]=jnp.sum(sacc[...],axis=0,keepdims=True)
+
+def cross_back_kernel(info, x, mine, other, above, gain, co, q, ck, cv, lse, cq, total, glow, vec, dq, dk, dv, part, acc, mask, gacc, sacc):
+    step=pl.program_id(0)
+    T=x.shape[0]
+    @pl.when(step==0)
+    def _():
+        norm_back_all(x,mine,other,above,gain,total,glow,vec,gacc,sacc)
+        mask[...]=cross_mask(info[0],info[1],info[2],T,ck.shape[0])
+    g=product_with_rows(glow[...],co[...]).astype(low)
+    a,b,c=attend_back(q[...],ck[...],cv[...],g,mask[...],lse[...])
+    a=a.astype(low)
+    dq[...]=a;dk[...]=b.astype(low);dv[...]=c.astype(low)
+    term=product_with_rows(a,cq[...])
+    @pl.when(step==0)
+    def _(): acc[...]=term
+    @pl.when(step!=0)
+    def _(): acc[...]+=term
+    @pl.when(step==pl.num_programs(0)-1)
+    def _(): part[...]=acc[...].astype(low)
+
+def cross_backward(info,x,mine,other,above,gain,co,q,ck,cv,lse_a,cq,tile=256):
+    T,D=x.shape;C=cq.shape[1];K=ck.shape[0]
+    whole,vec,col,row,act,tab,lse=specs(T,D,tile)
+    key=pl.BlockSpec((K,tile),lambda j,*_:(0,j))
+    two=pl.BlockSpec((2,D),lambda j,*_:(0,0))
+    return pl.pallas_call(cross_back_kernel,grid_spec=pltpu.PrefetchScalarGridSpec(num_scalar_prefetch=1,grid=(C//tile,),
+        in_specs=[whole,whole,whole,whole,vec,row,act,key,key,lse,col],
+        out_specs=[whole,whole,two,act,key,key,whole],
+        scratch_shapes=[pltpu.VMEM((T,D),f32),pltpu.VMEM((K,T),f32),pltpu.VMEM((8,D),f32),pltpu.VMEM((8,D),f32)]),
+        out_shape=[sds((T,D),f32),sds((T,D),low),sds((2,D),f32),sds((T,C),low),sds((K,C),low),sds((K,C),low),sds((T,D),low)],
+        cost_estimate=pl.CostEstimate(flops=2*T*C*(2*D+5*K*4),bytes_accessed=4*D*C+20*T*D,transcendentals=T*K*C//HEAD),
+        **PARAMS)(info,x,mine,other,above,gain,co,q,ck,cv,lse_a,cq)
+
+def self_back_kernel(info, x, mine, other, above, gain, wo, q, k, v, lse, wq, wk, wv, cos, lower, upper, total, glow, vec, dq, dk, dv, part, acc, mask, gacc, sacc):
+    step=pl.program_id(0)
+    T=x.shape[0]
+    @pl.when(step==0)
+    def _():
+        norm_back_all(x,mine,other,above,gain,total,glow,vec,gacc,sacc)
+        mask[...]=self_mask(info[0],T)
+    g=product_with_rows(glow[...],wo[...]).astype(low)
+    a,b,c=attend_back(q[...],k[...],v[...],g,mask[...],lse[...])
+    tabs=(cos[...],lower[...],upper[...])
+    a=turn_back(a,*tabs).astype(low);b=turn_back(b,*tabs).astype(low);c=c.astype(low)
+    dq[...]=a;dk[...]=b;dv[...]=c
+    term=product_with_rows(a,wq[...])+product_with_rows(b,wk[...])+product_with_rows(c,wv[...])
+    @pl.when(step==0)
+    def _(): acc[...]=term
+    @pl.when(step!=0)
+    def _(): acc[...]+=term
+    @pl.when(step==pl.num_programs(0)-1)
+    def _(): part[...]=acc[...].astype(low)
+
+def self_backward(info,x,mine,other,above,gain,wo,q,k,v,lse_a,wq,wk,wv,tabs,tile=256):
+    T,D=x.shape;C=wq.shape[1]
+    whole,vec,col,row,act,tab,lse=specs(T,D,tile)
+    two=pl.BlockSpec((2,D),lambda j,*_:(0,0))
+    return pl.pallas_call(self_back_kernel,grid_spec=pltpu.PrefetchScalarGridSpec(num_scalar_prefetch=1,grid=(C//tile,),
+        in_specs=[whole,whole,whole,whole,vec,row,act,act,act,lse,col,col,col,tab,tab,tab],
+        out_specs=[whole,whole,two,act,act,act,whole],
+        scratch_shapes=[pltpu.VMEM((T,D),f32),pltpu.VMEM((T,T),f32),pltpu.VMEM((8,D),f32),pltpu.VMEM((8,D),f32)]),
+        out_shape=[sds((T,D),f32),sds((T,D),low),sds((2,D),f32)]+[sds((T,C),low)]*3+[sds((T,D),low)],
+        cost_estimate=pl.CostEstimate(flops=2*T*C*(4*D+5*T*4),bytes_accessed=8*D*C+20*T*D,transcendentals=T*T*C//HEAD),
+        **PARAMS)(info,x,mine,other,above,gain,wo,q,k,v,lse_a,wq,wk,wv,*tabs)
+
+def last_kernel(x,mine,other,above,gain,total,vec,gacc,sacc):
+    step=pl.program_id(0)
+    @pl.when(step==0)
+    def _():
+        gacc[...]=jnp.zeros_like(gacc);sacc[...]=jnp.zeros_like(sacc)
+    def rows(r):
+        e=mine[r,:].astype(f32)+other[r,:].astype(f32)
+        total[r,:]=norm_back_rows(x[r,:],e,gain[...],above[r,:],None,gacc,sacc)
+    over_rows(x.shape[0],rows)
+    @pl.when(step==pl.num_programs(0)-1)
+    def _():
+        vec[0:1,:]=jnp.sum(gacc[...],axis=0,keepdims=True)
+        vec[1:2,:]=jnp.sum(sacc[...],axis=0,keepdims=True)
+
+def last_backward(x,mine,other,above,gain,block=128):
+    T,D=x.shape
+    b=pl.BlockSpec((block,D),lambda j:(j,0)); vec=pl.BlockSpec((1,D),lambda j:(0,0))
+    two=pl.BlockSpec((2,D),lambda j:(0,0))
+    return pl.pallas_call(last_kernel,grid=(T//block,),in_specs=[b,b,b,b,vec],out_specs=[b,two],
+        scratch_shapes=[pltpu.VMEM((8,D),f32),pltpu.VMEM((8,D),f32)],
+        out_shape=[sds((T,D),f32),sds((2,D),f32)],
+        cost_estimate=pl.CostEstimate(flops=20*T*D,bytes_accessed=16*T*D,transcendentals=T),**PARAMS)(x,mine,other,above,gain)
+
+def weight_kernel(plan, rows_a, info, *refs):
+    sides=refs[:rows_a];cols=refs[rows_a:rows_a+len(plan)];outs=refs[rows_a+len(plan):rows_a+len(plan)+8];turned=refs[rows_a+len(plan)+8:]
+    step=pl.program_id(0)
+    @pl.when(step==0)
+    def _():
+        for side,t in zip(sides,turned):
+            full=side[...].T
+            t[...]=full.reshape(t.shape)
+    plane=info[0]
+    for (which,half,first),col in zip(plan,cols):
+        t=turned[which];r=t.shape[2]
+        g=col[...]
+        for flip in range(4):
+            lhs=t[:,plane^flip].reshape(4*r,t.shape[3])
+            outs[half*4+flip][:,first:first+r,:]=product_plain(lhs,g).reshape(4,r,g.shape[1]).astype(low)
+
+def weight_products(plane,sides,plan,cols,rows_out,tile=256):
+    C=cols[0].shape[1]
+    in_specs=[pl.BlockSpec(s.shape,lambda j,*_:(0,0)) for s in sides]+[pl.BlockSpec((c.shape[0],tile),lambda j,*_:(0,j)) for c in cols]
+    outs=[pl.BlockSpec((4,rows_out,tile),lambda j,*_:(0,0,j))]*8
+    fl=sum(2*sides[w].shape[0]*sides[w].shape[1]*C for w,_,_ in plan)
+    return pl.pallas_call(functools.partial(weight_kernel,plan,len(sides)),grid_spec=pltpu.PrefetchScalarGridSpec(num_scalar_prefetch=1,grid=(C//tile,),
+        in_specs=in_specs,out_specs=outs,
+        scratch_shapes=[pltpu.VMEM((4,4,s.shape[1]//16,s.shape[0]),low) for s in sides]),
+        out_shape=[sds((4,rows_out,C),low)]*8,
+        cost_estimate=pl.CostEstimate(flops=fl,bytes_accessed=16*4*rows_out*C,transcendentals=0),
+        **PARAMS)(plane.reshape(1),*sides,*cols)
+
+
+def on_plane(
     hidden_in,
     out_grad,
     prompt_states,
@@ -388,19 +690,152 @@
     w_up,
     w_down,
 ):
-    low = jnp.bfloat16
-    known = lax.axis_size("dp") == 16 and lax.axis_size("tensor") == 2
-    frame_count = hidden_in.shape[0]
-    plane, level = lax.axis_index("dp") % 4, lax.axis_index("dp") // 4
-    grad_ff_out = out_grad.astype(low)
+    frames, width = hidden_in.shape
+    plane, level = lax.axis_index("dp") % PLANE, lax.axis_index("dp") // PLANE
+    info = jnp.concatenate([row_split, prompt_len])
+    positions = jnp.arange(frames, dtype=jnp.int32)
+    row_ids = (positions >= row_split[0]).astype(jnp.int32)
+    tables = rotary_tables((positions - row_ids * row_split[0]).astype(f32), 4 * HEAD)
+    gain_attn, bias_attn, gain_cross, bias_cross, gain_ff, bias_ff = (
+        vector[None] for vector in (gain_attn, bias_attn, gain_cross, bias_cross, gain_ff, bias_ff)
+    )
 
     def half_of(values):
         return lax.dynamic_slice_in_dim(
-            values, lax.axis_index("tensor") * (frame_count // 2), frame_count // 2, 0
+            values, lax.axis_index("tensor") * (frames // 2), frames // 2, 0
         )
 
-    if known:
-        frames_out = jnp.concatenate([grad_ff_out, *plane_gather(half_of(grad_ff_out))])
+    def swapped(part):
+        return lax.ppermute(part, "tensor", [(0, 1), (1, 0)])
+
+    context = prompt_states.reshape(2 * PROMPT, prompt_states.shape[2])
+    cross_key = product_plain(context, c_key).astype(low)
+    cross_value = product_plain(context, c_value).astype(low)
+    grad_ff_out = out_grad.astype(low)
+    input_one, query, key, value, attended_one, logsum_one, part = self_forward(
+        info, hidden_in, gain_attn, bias_attn, w_query, w_key, w_value, w_out, tables
+    )
+    frames_out = jnp.concatenate([grad_ff_out, *plane_gather(half_of(grad_ff_out))])
+    resid_one, input_two, cross_query, attended_two, logsum_two, part_two = cross_forward(
+        info, hidden_in, part, swapped(part), gain_cross, bias_cross, c_query, cross_key, cross_value, c_out
+    )
+    resid_two, input_three = norm_forward(resid_one, part_two, swapped(part_two), gain_ff, bias_ff)
+    frames_in = jnp.concatenate([input_three, *plane_gather(half_of(input_three))])
+    sum_part, back_part = ff_both(input_three, grad_ff_out, w_gate, w_up, w_down)
+    result = resid_two + add_low(sum_part, swapped(sum_part))
+
+    tile = 256
+    tiles = w_gate.shape[1] // (PLANE * tile)
+    shares = []
+    for index in range(tiles):
+        send, keep = ff_share(
+            jnp.stack([plane * tiles + index, level % 2]), frames_in, frames_out, w_gate, w_up, w_down, tile
+        )
+        shares.append(z_halve(send, keep, level))
+    spread = spread_units(jnp.concatenate(shares, axis=2), plane)
+    grad_w_down, grad_w_gate, grad_w_up = spread[0].T, spread[1], spread[2]
+
+    grad_two, grad_cross_out, vectors_ff, query_grad, key_grad, value_grad, part_back = cross_backward(
+        info,
+        resid_two,
+        back_part,
+        swapped(back_part),
+        out_grad,
+        gain_ff,
+        c_out,
+        cross_query,
+        cross_key,
+        cross_value,
+        logsum_two,
+        c_query,
+    )
+    r, c = width // 16, context.shape[1] // 16
+    parts = weight_products(
+        plane,
+        [grad_cross_out, input_two, context],
+        [(0, 0, 0), (2, 0, r), (1, 1, 0), (2, 1, r)],
+        [attended_two, key_grad, query_grad, value_grad],
+        r + c,
+    )
+    cross_sums = [
+        z_scatter(plane_scatter(parts[:4], 1), level),
+        z_scatter(plane_scatter(parts[4:], 2), level),
+    ]
+    grad_one, grad_self_out, vectors_cross, query_grad, key_grad, value_grad, part_last = self_backward(
+        info,
+        resid_one,
+        part_back,
+        swapped(part_back),
+        grad_two,
+        gain_cross,
+        w_out,
+        query,
+        key,
+        value,
+        logsum_one,
+        w_query,
+        w_key,
+        w_value,
+        tables,
+    )
+    parts = weight_products(
+        plane,
+        [grad_self_out, input_one],
+        [(0, 0, 0), (1, 0, r), (1, 1, 0), (1, 1, r)],
+        [attended_one, value_grad, query_grad, key_grad],
+        2 * r,
+    )
+    self_sums = [
+        z_scatter(plane_scatter(parts[:4], 1), level),
+        z_scatter(plane_scatter(parts[4:], 2), level),
+    ]
+    grad_hidden, vectors_attn = last_backward(
+        hidden_in, part_last, swapped(part_last), grad_one, gain_attn
+    )
+    vectors = vector_sum(jnp.concatenate([vectors_attn, vectors_cross, vectors_ff]))
+    return (
+        result,
+        grad_hidden,
+        *(vectors[index] for index in range(6)),
+        self_sums[1][:r],
+        self_sums[1][r:],
+        self_sums[0][r:],
+        self_sums[0][:r].T,
+        cross_sums[1][:r],
+        cross_sums[0][r:],
+        cross_sums[1][r:],
+        cross_sums[0][:r].T,
+        grad_w_gate,
+        grad_w_up,
+        grad_w_down,
+    )
+
+
+def on_any(
+    hidden_in,
+    out_grad,
+    prompt_states,
+    row_split,
+    prompt_len,
+    gain_attn,
+    bias_attn,
+    gain_cross,
+    bias_cross,
+    gain_ff,
+    bias_ff,
+    w_query,
+    w_key,
+    w_value,
+    w_out,
+    c_query,
+    c_key,
+    c_value,
+    c_out,
+    w_gate,
+    w_up,
+    w_down,
+):
+    frame_count = hidden_in.shape[0]
     positions = jnp.arange(frame_count, dtype=jnp.int32)
     split_here = row_split[0]
     row_ids = (positions >= split_here).astype(jnp.int32)
@@ -432,35 +867,30 @@
 
     normed, scaled_three, inverse_three = normalize(resid_two, gain_ff, bias_ff)
     input_three = normed.astype(low)
-    if known:
-        frames_in = jnp.concatenate([input_three, *plane_gather(half_of(input_three))])
-    sum_part, back_part = ff_both(input_three, grad_ff_out, w_gate, w_up, w_down)
-    result = resid_two + swap_sum(sum_part)
-    normed_grad_three = swap_sum(back_part)
-    if known:
-        units = w_gate.shape[1] // 4
-        tile = 256
-        shares = []
-        for part in range(units // tile):
-            own = ff_share(
-                frames_in, frames_out, w_gate, w_up, w_down, plane * (units // tile) + part, tile
-            )
-            shares.append(z_scatter(own, level))
-        spread = spread_units(jnp.concatenate(shares, axis=2), plane)
-        grad_w_down, grad_w_gate, grad_w_up = spread[0].T, spread[1], spread[2]
-    else:
-        gate_pre = product_plain(input_three, w_gate)
-        up_pre = product_plain(input_three, w_up)
-        grad_mixed = product_with_rows(grad_ff_out, w_down)
-        mixed, grad_gate, grad_up = ff_parts(gate_pre, up_pre, grad_mixed)
-        grad_w_down = generic_sum(grad_ff_out, mixed).T
-        grad_w_gate = generic_sum(input_three, grad_gate)
-        grad_w_up = generic_sum(input_three, grad_up)
+    gate_pre = product_plain(input_three, w_gate)
+    up_pre = product_plain(input_three, w_up)
+    sigmoid_gate = jax.nn.sigmoid(gate_pre)
+    mixed_low = (gate_pre * sigmoid_gate * up_pre).astype(low)
+    result = resid_two + swap_sum(product_plain(mixed_low, w_down))
+
+    grad_ff_out = out_grad.astype(low)
+    grad_w_down = generic_sum(grad_ff_out, mixed_low).T
+    grad_mixed = product_with_rows(grad_ff_out, w_down)
+    grad_gate = (
+        grad_mixed * up_pre * sigmoid_gate * (1.0 + gate_pre * (1.0 - sigmoid_gate))
+    ).astype(low)
+    grad_up = (grad_mixed * gate_pre * sigmoid_gate).astype(low)
+    grad_w_gate = generic_sum(input_three, grad_gate)
+    grad_w_up = generic_sum(input_three, grad_up)
+    normed_grad_three = swap_sum(
+        product_with_rows(grad_gate, w_gate) + product_with_rows(grad_up, w_up)
+    )
     back_three, grad_gain_ff, grad_bias_ff = normalize_back(
         normed_grad_three, scaled_three, inverse_three, gain_ff
     )
     grad_two = out_grad + back_three
     grad_cross_out = grad_two.astype(low)
+    grad_c_out = generic_sum(grad_cross_out, attended_two).T
     grad_attended_two = product_with_rows(grad_cross_out, c_out).astype(low)
     cross_query_grad, cross_key_grad, cross_value_grad = attend_backward(
         cross_query,
@@ -473,41 +903,16 @@
     cross_query_grad = cross_query_grad.astype(low)
     cross_key_grad = cross_key_grad.astype(low)
     cross_value_grad = cross_value_grad.astype(low)
-    if known:
-        context_part = quarter_products(
-            context_flat, jnp.concatenate([cross_key_grad, cross_value_grad], axis=1), plane
-        )
-        width = cross_key_grad.shape[1]
-        first = plane_scatter(
-            stacked(
-                quarter_products(grad_cross_out, attended_two, plane),
-                [part[..., :width] for part in context_part],
-            ),
-            1,
-        )
-        second = plane_scatter(
-            stacked(
-                quarter_products(input_two, cross_query_grad, plane),
-                [part[..., width:] for part in context_part],
-            ),
-            2,
-        )
-        sums = z_scatter(jnp.concatenate([first, second], axis=1), level)
-        r = input_two.shape[1] // 16
-        c = context_flat.shape[1] // 16
-        grad_c_out, grad_c_key = sums[:r].T, sums[r : r + c]
-        grad_c_query, grad_c_value = sums[r + c : 2 * r + c], sums[2 * r + c :]
-    else:
-        grad_c_out = generic_sum(grad_cross_out, attended_two).T
-        grad_c_query = generic_sum(input_two, cross_query_grad)
-        grad_c_key = generic_sum(context_flat, cross_key_grad)
-        grad_c_value = generic_sum(context_flat, cross_value_grad)
+    grad_c_query = generic_sum(input_two, cross_query_grad)
+    grad_c_key = generic_sum(context_flat, cross_key_grad)
+    grad_c_value = generic_sum(context_flat, cross_value_grad)
     normed_grad_two = swap_sum(product_with_rows(cross_query_grad, c_query))
     back_two, grad_gain_cross, grad_bias_cross = normalize_back(
         normed_grad_two, scaled_two, inverse_two, gain_cross
     )
     grad_one = grad_two + back_two
     grad_self_out = grad_one.astype(low)
+    grad_w_out = generic_sum(grad_self_out, attended_one).T
     grad_attended_one = product_with_rows(grad_self_out, w_out).astype(low)
     query_grad, key_grad, value_grad = attend_backward(
         query_one, heads_of(key_one), heads_of(value_one), self_ok, grad_attended_one, logsum_one
@@ -515,30 +920,9 @@
     query_grad = rotate_back(query_grad, tables).astype(low)
     key_grad = rotate_back(key_grad, tables).astype(low)
     value_grad = value_grad.astype(low)
-    if known:
-        first = plane_scatter(
-            stacked(
-                quarter_products(grad_self_out, attended_one, plane),
-                quarter_products(input_one, value_grad, plane),
-            ),
-            1,
-        )
-        second = plane_scatter(
-            stacked(
-                quarter_products(input_one, query_grad, plane),
-                quarter_products(input_one, key_grad, plane),
-            ),
-            2,
-        )
-        sums = z_scatter(jnp.concatenate([first, second], axis=1), level)
-        r = input_one.shape[1] // 16
-        grad_w_out, grad_w_value = sums[:r].T, sums[r : 2 * r]
-        grad_w_query, grad_w_key = sums[2 * r : 3 * r], sums[3 * r :]
-    else:
-        grad_w_out = generic_sum(grad_self_out, attended_one).T
-        grad_w_query = generic_sum(input_one, query_grad)
-        grad_w_key = generic_sum(input_one, key_grad)
-        grad_w_value = generic_sum(input_one, value_grad)
+    grad_w_query = generic_sum(input_one, query_grad)
+    grad_w_key = generic_sum(input_one, key_grad)
+    grad_w_value = generic_sum(input_one, value_grad)
     normed_grad_one = swap_sum(
         product_with_rows(query_grad, w_query)
         + product_with_rows(key_grad, w_key)
@@ -629,6 +1013,7 @@
         P("dp", "tensor"),
         P("tensor", "dp"),
     )
+    known = mesh.shape["dp"] == PLANE * LEVELS and mesh.shape["tensor"] == 2
     return jax.shard_map(
-        on_device, mesh=mesh, in_specs=in_specs, out_specs=out_specs, check_vma=False
-    )
+        on_plane if known else on_any, mesh=mesh, in_specs=in_specs, out_specs=out_specs, check_vma=False
+    )

time: 712 us -> 519 us (0.73)
  Pallas kernels: 80.2 us -> 205 us
  matrix products: 114 us -> 0.97 us
  starting transfers between devices: 151 us -> 47.5 us
  other arithmetic: 120 us -> 25.5 us
  local copies, waits for them, and re-layouts: 113 us -> 40.9 us
  waiting for transfers between devices: 123 us -> 187 us
    pallas_call x0 -> x8, Pallas kernels: none -> 120 us  [the longest x1 29.9 us: self_backward(): pl.pallas_call(self_back_kernel, grid_spec=pltpu.PrefetchScalarGridSpec(n...]
    ppermute x36 -> x20, starting transfers between devices: 108 us -> 18.5 us  [the longest x7 8.99 us: z_halve(): last = lax.ppermute(passed, 'dp', pairs(2 * PLANE))]
    dot_general x18 -> x0, matrix products: 68.7 us -> none  [the longest x6 27.5 us: product_with_rows(): lax.dot_general(left_side, right_side, (((1,), (1,)), ((), ())), preferre...]
    dot_general x36 -> x2, matrix products: 44.9 us -> 0.97 us  [product_plain(): return jnp.dot(left_side, right_side, preferred_element_type=jnp.float32)]
    convert_element_type x20 -> x8, other arithmetic: 44.4 us -> 5.53 us  [the longest x7 5.52 us: z_halve(): passed = add_low(half(keep, 1 - upper), half(got, 1 - upper)).astype(low)]
    ppermute x4, waiting for transfers between devices: 4.7 us -> 38.4 us  [vector_sum(): vectors = vectors + lax.ppermute(vectors, 'dp', pairs(mask))]
    ppermute x36 -> x20, waiting for transfers between devices: 43.8 us -> 71.1 us  [the longest x7 44.9 us: z_halve(): last = lax.ppermute(passed, 'dp', pairs(2 * PLANE))]
    ppermute x4, waiting for transfers between devices: 10.3 us -> 34.2 us  [plane_scatter(): got_diag = lax.ppermute(parts[3], 'dp', pairs(first))]
  transfers between devices with their start and end apart: 67 -> 51, of which waited for: 16 -> 20; matrix products, arithmetic and copies ran while one was open for 45% -> 8% of each run, Pallas kernels for 9% -> 35%
where the time goes in v3:
time: 519 us; the launch traced here: 509 us
  Pallas kernels  205 us (39%)
  waiting for transfers between devices  187 us (36%)
  starting transfers between devices  47.5 us (9%)
  local copies, waits for them, and re-layouts  40.9 us (8%)
  other arithmetic  25.5 us (5%)
    pallas_call x3, Pallas kernels, ff_share(): pl.pallas_call(share_kernel, grid_spec=pltpu.PrefetchScalarGridSpec(num_s...  49.6 us
    ppermute x7, waiting for transfers between devices, z_halve(): last = lax.ppermute(passed, 'dp', pairs(2 * PLANE))  44.9 us
    ppermute x4, waiting for transfers between devices, vector_sum(): vectors = vectors + lax.ppermute(vectors, 'dp', pairs(mask))  38.4 us
    pallas_call x1, Pallas kernels, ff_both(): pl.pallas_call(ff_kernel, grid=(units // tile,), in_specs=[whole, whole,...  35.1 us
    ppermute x4, waiting for transfers between devices, plane_scatter(): got_diag = lax.ppermute(parts[3], 'dp', pairs(first))  34.2 us
    unnamed x141, local copies, waits for them, and re-layouts  30.1 us
    pallas_call x1, Pallas kernels, self_backward(): pl.pallas_call(self_back_kernel, grid_spec=pltpu.PrefetchScalarGridSpec(n...  29.9 us
    ppermute x7, waiting for transfers between devices, z_halve(): got = lax.ppermute(send, 'dp', pairs(PLANE))  26.2 us
  transfers between devices with their start and end apart: 51, of which 20 were waited for; matrix products, arithmetic and copies ran while one was open for 8% of the time, Pallas kernels for 35%

profile of v3, /device:TPU:0, one launch (start us, length us, event | category | flops | bytes accessed | tf_op | source)
XLA Modules:
  0.0 508.8 jit_solution(12163927146489553037)
XLA Ops:
  3.6 2.0 fusion.3
  5.6 20.9 %shard_map.357 = (bf16[512,1536]{1,0:T(8,128)(2,1)}, bf16[512,768]{1,0:T(8,128)(2,1)S(1)}, bf16[512,768]{1,0:T(8,128)(2,1)S(1)}, bf16[512,768]{1,0:T(8,128)(2,1)...) custom-call(s32[3]{0:T(128)S(1)} %pad_add_fusion.info, f32[512,1536]{1,0:T(8,128)} %x.1, ...), custom_call_target="tpu_custom_call" | custom-call | flops 8053063680 | bytes 18874368 | tf_op jit(solution)/shard_map/pallas_call | solution.py:471
  31.1 3.3 constant_dynamic-update-slice_fusion.13
  35.4 2.5 collective-permute-start.36
  37.8 1.5 collective-permute-start.37
  41.8 14.7 %collective-permute-done.36 = bf16[256,1536]{1,0:T(8,128)(2,1)} collective-permute-done((bf16[256,1536]{1,0:T(8,128)(2,1)}, bf16[256,1536]{1,0:T(8,128)(2,1)}, u32[]{:S(2)}, u32[]{:S(2)}) %collective-permute-start.36) | collective-permute-done | bytes 786464 | tf_op jit(solution)/shard_map/ppermute | solution.py:222
  56.6 17.7 %shard_map.358 = (f32[512,1536]{1,0:T(8,128)}, bf16[512,1536]{1,0:T(8,128)(2,1)S(1)}, bf16[512,768]{1,0:T(8,128)(2,1)S(1)}, bf16[512,768]{1,0:T(8,128)(2,1)S(1)}...) custom-call(s32[3]{0:T(128)S(1)} %pad_add_fusion.info, f32[512,1536]{1,0:T(8,128)} %x.1, ...), custom_call_target="tpu_custom_call" | custom-call | flops 4026531840 | bytes 18874368 | tf_op jit(solution)/shard_map/pallas_call | solution.py:505
  74.3 1.2 copy-done.26
  79.1 2.1 constant_dynamic-update-slice_fusion.12
  81.7 2.1 constant_dynamic-update-slice_fusion.11
  83.8 2.1 constant_dynamic-update-slice_fusion.10
  85.8 2.1 constant_dynamic-update-slice_fusion.9
  89.8 5.1 %shard_map.359 = (f32[512,1536]{1,0:T(8,128)}, bf16[512,1536]{1,0:T(8,128)(2,1)S(1)}) custom-call(f32[512,1536]{1,0:T(8,128)} %get-tuple-element.75.hid.x, bf16[512,1536]{1,0:T(8,128)(2,1)} %get-tuple-element.76.mine, bf16[512,1536]{1,0:T(8,128)(2,1)} %collective-permute-done.1.other, f32[1,1536]{1,0:T(1,128)S(1)} %broadcast_in_dim.47.gain, ...), custom_call_target="tpu_custom_call" | custom-call | flops 7864320 | bytes 11010048 | tf_op jit(solution)/shard_map/pallas_call | solution.py:523
  95.0 2.0 collective-permute-start.30
  97.0 1.5 collective-permute-start.31
  98.5 35.1 %shard_map.360 = (bf16[512,1536]{1,0:T(8,128)(2,1)S(1)}, bf16[512,1536]{1,0:T(8,128)(2,1)S(1)}) custom-call(bf16[512,1536]{1,0:T(8,128)(2,1)S(1)} %get-tuple-element.78.in_ref, bf16[512,1536]{1,0:T(8,128)(2,1)S(1)} %get-tuple-element.130.out_ref, bf16[1536,3072]{1,0:T(8,128)(2,1)} %gate_ref.7, bf16[1536,3072]{1,0:T(8,128)(2,1)} %up_ref.7, ...), custom_call_target="tpu_custom_call" | custom-call | flops 28991029248 | bytes 34603008 | tf_op jit(solution)/shard_map/pallas_call | solution.py:270
  136.0 5.6 %collective-permute-done.34 = bf16[256,1536]{1,0:T(8,128)(2,1)S(1)} collective-permute-done((bf16[256,1536]{1,0:T(8,128)(2,1)S(1)}, bf16[256,1536]{1,0:T(8,128)(2,1)S(1)}, u32[]{:S(2)}, u32[]{:S(2)}) %collective-permute-start.34) | collective-permute-done | bytes 786464 | tf_op jit(solution)/shard_map/ppermute | solution.py:223
  142.8 16.7 %shard_map.366 = (bf16[2,3,384,256]{3,2,1,0:T(8,128)(2,1)}, bf16[2,3,384,256]{3,2,1,0:T(8,128)(2,1)S(1)}) custom-call(s32[2]{0:T(128)S(1)} %get-tuple-element.157.info, bf16[2048,1536]{1,0:T(8,128)(2,1)S(1)} %constant_dynamic-update-slice_fusion.in_ref, bf16[2048,1536]{1,0:T(8,128)(2,1)} %constant_dynamic-update-slice_fusion.7.out_ref, ...), custom_call_target="tpu_custom_call" | custom-call | flops 9663676416 | bytes 17301504 | tf_op jit(solution)/shard_map/pallas_call | solution.py:325
  159.5 2.0 collective-permute-start.42
  161.5 16.8 %shard_map.367 = (bf16[2,3,384,256]{3,2,1,0:T(8,128)(2,1)}, bf16[2,3,384,256]{3,2,1,0:T(8,128)(2,1)S(1)}) custom-call(s32[2]{0:T(128)S(1)} %copy-done.18, bf16[2048,1536]{1,0:T(8,128)(2,1)S(1)} %constant_dynamic-update-slice_fusion.in_ref, bf16[2048,1536]{1,0:T(8,128)(2,1)} %constant_dynamic-update-slice_fusion.7.out_ref, bf16[1536,3072]{1,0:T(8,128)(2,1)} %gate_ref.7, ...), custom_call_target="tpu_custom_call" | custom-call | flops 9663676416 | bytes 17301504 | tf_op jit(solution)/shard_map/pallas_call | solution.py:325
  178.4 1.2 copy-done.62
  179.6 21.8 %shard_map.361 = (f32[512,1536]{1,0:T(8,128)}, bf16[512,1536]{1,0:T(8,128)(2,1)S(1)}, f32[2,1536]{1,0:T(2,128)S(1)}, bf16[512,768]{1,0:T(8,128)(2,1)S(1)}, bf16[...) custom-call(s32[3]{0:T(128)S(1)} %copy-done.24, ...), custom_call_target="tpu_custom_call" | custom-call | flops 6442450944 | bytes 20447232 | tf_op jit(solution)/shard_map/pallas_call | solution.py:577
  208.1 8.0 %shard_map.365 = (bf16[4,144,768]{2,1,0:T(8,128)(2,1)S(1)}, bf16[4,144,768]{2,1,0:T(8,128)(2,1)S(1)}, bf16[4,144,768]{2,1,0:T(8,128)(2,1)S(1)}, bf16[4,144,768]{...) custom-call(s32[1]{0:T(128)} %bitcast.8.info, ...), custom_call_target="tpu_custom_call" | custom-call | flops 3019898880 | bytes 7077888 | tf_op jit(solution)/shard_map/pallas_call | solution.py:661
  217.9 1.9 collective-permute-start.26
  219.9 16.2 %shard_map.368 = (bf16[2,3,384,256]{3,2,1,0:T(8,128)(2,1)S(1)}, bf16[2,3,384,256]{3,2,1,0:T(8,128)(2,1)S(1)}) custom-call(s32[2]{0:T(128)S(1)} %copy-done.19, bf16[2048,1536]{1,0:T(8,128)(2,1)S(1)} %constant_dynamic-update-slice_fusion.in_ref, bf16[2048,1536]{1,0:T(8,128)(2,1)} %constant_dynamic-update-slice_fusion.7.out_ref, bf16[1536,3072]{1,0:T(8,128)(2,1)} %gate_ref.7, ...), custom_call_target="tpu_custom_call" | custom-call | flops 9663676416 | bytes 17301504 | tf_op jit(solution)/shard_map/pallas_call | solution.py:325
  236.0 1.6 collective-permute-start.46
  237.7 1.5 collective-permute-start.21
  239.6 3.7 add_add_fusion
  244.4 14.1 %collective-permute-done.21 = bf16[4,144,768]{2,1,0:T(8,128)(2,1)S(1)} collective-permute-done((bf16[4,144,768]{2,1,0:T(8,128)(2,1)}, bf16[4,144,768]{2,1,0:T(8,128)(2,1)S(1)}, u32[]{:S(2)}, u32[]{:S(2)}) %collective-permute-start.21) | collective-permute-done | bytes 884768 | tf_op jit(solution)/shard_map/ppermute | solution.py:214
  260.1 1.5 collective-permute-start.20
  261.7 2.1 fusion.5
  263.7 2.6 collective-permute-start.43
  266.4 2.2 fusion.6
  269.9 2.6 collective-permute-start.47
  272.6 29.9 %shard_map.362 = (f32[512,1536]{1,0:T(8,128)}, bf16[512,1536]{1,0:T(8,128)(2,1)}, f32[2,1536]{1,0:T(2,128)S(1)}, bf16[512,768]{1,0:T(8,128)(2,1)S(1)}, bf16[512,...) custom-call(s32[3]{0:T(128)S(1)} %copy-done.25, ...), custom_call_target="tpu_custom_call" | custom-call | flops 12884901888 | bytes 25165824 | tf_op jit(solution)/shard_map/pallas_call | solution.py:609
  302.5 10.3 %shard_map.364 = (bf16[4,192,768]{2,1,0:T(8,128)(2,1)S(1)}, bf16[4,192,768]{2,1,0:T(8,128)(2,1)S(1)}, bf16[4,192,768]{2,1,0:T(8,128)(2,1)}, bf16[4,192,768]{2,1,...) custom-call(s32[1]{0:T(128)} %bitcast.8.info, ...), custom_call_target="tpu_custom_call" | custom-call | flops 4831838208 | bytes 9437184 | tf_op jit(solution)/shard_map/pallas_call | solution.py:661
  312.8 3.3 collective-permute-done.43
  316.1 1.5 collective-permute-start.27
  317.7 1.5 fusion.2
  319.2 9.5 %collective-permute-done.45 = bf16[3,384,256]{2,1,0:T(8,128)(2,1)S(1)} collective-permute-done((bf16[3,384,256]{2,1,0:T(8,128)(2,1)}, bf16[3,384,256]{2,1,0:T(8,128)(2,1)S(1)}, u32[]{:S(2)}, u32[]{:S(2)}) %collective-permute-start.45) | collective-permute-done | bytes 589856 | tf_op jit(solution)/shard_map/ppermute | solution.py:200
  329.6 1.4 fusion.1
  331.0 9.8 %collective-permute-done.47 = bf16[3,384,256]{2,1,0:T(8,128)(2,1)S(1)} collective-permute-done((bf16[3,384,256]{2,1,0:T(8,128)(2,1)}, bf16[3,384,256]{2,1,0:T(8,128)(2,1)S(1)}, u32[]{:S(2)}, u32[]{:S(2)}) %collective-permute-start.47) | collective-permute-done | bytes 589856 | tf_op jit(solution)/shard_map/ppermute | solution.py:200
  341.3 1.5 collective-permute-start.48
  343.4 1.5 collective-permute-start.50
  346.2 1.4 collective-permute-start.16
  347.6 3.7 collective-permute-done.22
  352.1 8.6 %collective-permute-done.48 = bf16[3,96,768]{2,1,0:T(8,128)(2,1)S(1)} collective-permute-done((bf16[3,96,768]{2,1,0:T(8,128)(2,1)S(1)}, bf16[3,96,768]{2,1,0:T(8,128)(2,1)S(1)}, u32[]{:S(2)}, u32[]{:S(2)}) %collective-permute-start.48) | collective-permute-done | bytes 442400 | tf_op jit(solution)/shard_map/ppermute | solution.py:355
  362.8 8.4 %collective-permute-done.50 = bf16[3,96,768]{2,1,0:T(8,128)(2,1)S(1)} collective-permute-done((bf16[3,96,768]{2,1,0:T(8,128)(2,1)S(1)}, bf16[3,96,768]{2,1,0:T(8,128)(2,1)S(1)}, u32[]{:S(2)}, u32[]{:S(2)}) %collective-permute-start.50) | collective-permute-done | bytes 442400 | tf_op jit(solution)/shard_map/ppermute | solution.py:355
  372.1 1.2 copy-done.2
  373.9 1.9 slice_bitcast_fusion
  375.7 19.8 %collective-permute-done.16 = bf16[4,192,768]{2,1,0:T(8,128)(2,1)S(1)} collective-permute-done((bf16[4,192,768]{2,1,0:T(8,128)(2,1)S(1)}, bf16[4,192,768]{2,1,0:T(8,128)(2,1)S(1)}, u32[]{:S(2)}, u32[]{:S(2)}) %collective-permute-start.16) | collective-permute-done | bytes 1179680 | tf_op jit(solution)/shard_map/ppermute | solution.py:214
  396.3 1.2 collective-permute-start.17
  397.5 6.2 %shard_map.363 = (f32[512,1536]{1,0:T(8,128)}, f32[2,1536]{1,0:T(2,128)S(1)}) custom-call(f32[512,1536]{1,0:T(8,128)} %x.1, bf16[512,1536]{1,0:T(8,128)(2,1)S(1)} %copy-done.2, bf16[512,1536]{1,0:T(8,128)(2,1)S(1)} %collective-permute-done.5.other, f32[512,1536]{1,0:T(8,128)} %get-tuple-element.90.above, f32[1,1536]{1,0:T(1,128)S(1)} %broadcast_in_dim.38.gain), custom_call_target="tpu_custom_call" | custom-call | flops 15728640 | bytes 12582912 | tf_op jit(solution)/shard_map/pallas_call | solution.py:635
  405.1 3.3 collective-permute-start.29
  408.4 11.6 %collective-permute-done.6 = f32[6,1536]{1,0:T(8,128)S(1)} collective-permute-done((f32[6,1536]{1,0:T(8,128)S(1)}, f32[6,1536]{1,0:T(8,128)S(1)}, u32[]{:S(2)}, u32[]{:S(2)}) %collective-permute-start.6) | collective-permute-done | bytes 36896 | tf_op jit(solution)/shard_map/ppermute | solution.py:168
  420.0 1.7 collective-permute-start.12
  422.0 22.8 %collective-permute-done.7 = f32[6,1536]{1,0:T(8,128)S(1)} collective-permute-done((f32[6,1536]{1,0:T(8,128)S(1)}, f32[6,1536]{1,0:T(8,128)S(1)}, u32[]{:S(2)}, u32[]{:S(2)}) %collective-permute-start.7) | collective-permute-done | bytes 36896 | tf_op jit(solution)/shard_map/ppermute | solution.py:168
  444.9 9.6 %collective-permute-done.24 = bf16[144,768]{1,0:T(8,128)(2,1)S(1)} collective-permute-done((bf16[144,768]{1,0:T(8,128)(2,1)S(1)}, bf16[144,768]{1,0:T(8,128)(2,1)S(1)}, u32[]{:S(2)}, u32[]{:S(2)}) %collective-permute-start.24) | collective-permute-done | bytes 221216 | tf_op jit(solution)/shard_map/ppermute | solution.py:200
  454.6 4.0 collective-permute-done.8
  459.8 2.1 collective-permute-start.18
  462.5 1.2 collective-permute-start.13
  466.5 13.2 %collective-permute-done.18 = bf16[2,192,768]{2,1,0:T(8,128)(2,1)S(1)} collective-permute-done((bf16[2,192,768]{2,1,0:T(8,128)(2,1)S(1)}, bf16[2,192,768]{2,1,0:T(8,128)(2,1)S(1)}, u32[]{:S(2)}, u32[]{:S(2)}) %collective-permute-start.18) | collective-permute-done | bytes 589856 | tf_op jit(solution)/shard_map/ppermute | solution.py:194
  480.4 13.0 %collective-permute-done.13 = bf16[2,192,768]{2,1,0:T(8,128)(2,1)S(1)} collective-permute-done((bf16[2,192,768]{2,1,0:T(8,128)(2,1)S(1)}, bf16[2,192,768]{2,1,0:T(8,128)(2,1)S(1)}, u32[]{:S(2)}, u32[]{:S(2)}) %collective-permute-start.13) | collective-permute-done | bytes 589856 | tf_op jit(solution)/shard_map/ppermute | solution.py:194
  494.6 12.7 %collective-permute-done.14 = bf16[192,768]{1,0:T(8,128)(2,1)S(1)} collective-permute-done((bf16[192,768]{1,0:T(8,128)(2,1)S(1)}, bf16[192,768]{1,0:T(8,128)(2,1)S(1)}, u32[]{:S(2)}, u32[]{:S(2)}) %collective-permute-start.14) | collective-permute-done | bytes 294944 | tf_op jit(solution)/shard_map/ppermute | solution.py:200
  (257 shorter events, 50.4 us)
Async XLA Ops:
  0.7 38.7 %copy-start = (bf16[768,768]{1,0:T(8,128)(2,1)S(1)}, bf16[768,768]{1,0:T(8,128)(2,1)}, u32[]{:S(2)}) copy-start(bf16[768,768]{1,0:T(8,128)(2,1)} %param.39) | copy-start | bytes 3538948
  2.2 54.4 %copy-start.23 = (s32[3]{0:T(128)}, s32[3]{0:T(128)S(1)}, u32[]{:S(2)}) copy-start(s32[3]{0:T(128)S(1)} %pad_add_fusion.info) | copy-start | bytes 40
  5.6 20.9 %copy-start.8 = (f32[512,256]{1,0:T(8,128)}, f32[512,256]{1,0:T(8,128)S(1)}, u32[]{:S(2)}) copy-start(f32[512,256]{1,0:T(8,128)S(1)} %get-tuple-element.152.upper) | copy-start | bytes 1572868
  5.6 20.9 %copy-start.10 = (f32[512,256]{1,0:T(8,128)}, f32[512,256]{1,0:T(8,128)S(1)}, u32[]{:S(2)}) copy-start(f32[512,256]{1,0:T(8,128)S(1)} %get-tuple-element.153.lower) | copy-start | bytes 1572868
  30.7 25.9 %collective-permute-start = (bf16[512,1536]{1,0:T(8,128)(2,1)}, bf16[512,1536]{1,0:T(8,128)(2,1)}, u32[]{:S(2)}, u32[]{:S(2)}) collective-permute-start(bf16[512,1536]{1,0:T(8,128)(2,1)} %get-tuple-element.74.mine), channel_id=1, source_target_pairs={{0,1},{1,0},{2,3},{3,2},{4,5},{5,4},{6,7},{7,6},{8,9},{9,8},{10,11... | collective-permute-start | bytes 4718600 | tf_op jit(solution)/shard_map/ppermute | solution.py:709
  35.4 21.2 %collective-permute-start.36 = (bf16[256,1536]{1,0:T(8,128)(2,1)}, bf16[256,1536]{1,0:T(8,128)(2,1)}, u32[]{:S(2)}, u32[]{:S(2)}) collective-permute-start(bf16[256,1536]{1,0:T(8,128)(2,1)} %constant_dynamic-slice_fusion.1), channel_id=1, source_target_pairs={{0,2},{2,0},{4,6},{6,4},{8,10},{10,8},{12,14},{14,12},{16,18},{18,... | collective-permute-start | bytes 2359304 | tf_op jit(solution)/shard_map/ppermute | solution.py:222
  37.8 41.1 %collective-permute-start.37 = (bf16[256,1536]{1,0:T(8,128)(2,1)}, bf16[256,1536]{1,0:T(8,128)(2,1)}, u32[]{:S(2)}, u32[]{:S(2)}) collective-permute-start(bf16[256,1536]{1,0:T(8,128)(2,1)} %constant_dynamic-slice_fusion.1), channel_id=1, source_target_pairs={{0,4},{2,6},{4,0},{6,2},{8,12},{10,14},{12,8},{14,10},{16,20},{18,... | collective-permute-start | bytes 2359304 | tf_op jit(solution)/shard_map/ppermute | solution.py:222
  39.4 41.8 %collective-permute-start.38 = (bf16[256,1536]{1,0:T(8,128)(2,1)}, bf16[256,1536]{1,0:T(8,128)(2,1)}, u32[]{:S(2)}, u32[]{:S(2)}) collective-permute-start(bf16[256,1536]{1,0:T(8,128)(2,1)} %constant_dynamic-slice_fusion.1), channel_id=1, source_target_pairs={{0,6},{2,4},{4,2},{6,0},{8,14},{10,12},{12,10},{14,8},{16,22},{18,... | collective-permute-start | bytes 2359304 | tf_op jit(solution)/shard_map/ppermute | solution.py:222
  41.1 33.1 %copy-start.14 = (bf16[256,768]{1,0:T(8,128)(2,1)}, bf16[256,768]{1,0:T(8,128)(2,1)S(1)}, u32[]{:S(2)}) copy-start(bf16[256,768]{1,0:T(8,128)(2,1)S(1)} %convolution_convert_fusion.1.ck) | copy-start | bytes 1179652
  41.8 32.5 %copy-start.16 = (f32[1,1536]{1,0:T(1,128)}, f32[1,1536]{1,0:T(1,128)S(1)}, u32[]{:S(2)}) copy-start(f32[1,1536]{1,0:T(1,128)S(1)} %broadcast_in_dim.45.gain) | copy-start | bytes 18436
  41.8 37.1 %copy-start.60 = (f32[1536]{0:T(1024)S(1)}, f32[1536]{0:T(1024)}, u32[]{:S(2)}) copy-start(f32[1536]{0:T(1024)} %param.31) | copy-start | bytes 18436
  41.8 37.1 %copy-start.61 = (f32[1536]{0:T(1024)S(1)}, f32[1536]{0:T(1024)}, u32[]{:S(2)}) copy-start(f32[1536]{0:T(1024)} %param.32) | copy-start | bytes 18436
  56.5 29.3 %collective-permute-start.39 = (bf16[256,1536]{1,0:T(8,128)(2,1)}, bf16[256,1536]{1,0:T(8,128)(2,1)}, u32[]{:S(2)}, u32[]{:S(2)}) collective-permute-start(bf16[256,1536]{1,0:T(8,128)(2,1)} %collective-permute-done.36), channel_id=1, source_target_pairs={{0,1},{1,0},{2,3},{3,2},{4,5},{5,4},{6,7},{7,6},{8,9},{9,8},{10,11... | collective-permute-start | bytes 2359304 | tf_op jit(solution)/shard_map/ppermute | solution.py:223
  77.8 12.0 %collective-permute-start.1 = (bf16[512,1536]{1,0:T(8,128)(2,1)}, bf16[512,1536]{1,0:T(8,128)(2,1)}, u32[]{:S(2)}, u32[]{:S(2)}) collective-permute-start(bf16[512,1536]{1,0:T(8,128)(2,1)} %get-tuple-element.76.mine), channel_id=1, source_target_pairs={{0,1},{1,0},{2,3},{3,2},{4,5},{5,4},{6,7},{7,6},{8,9},{9,8},{10,11... | collective-permute-start | bytes 4718600 | tf_op jit(solution)/shard_map/ppermute | solution.py:709
  79.0 8.9 %collective-permute-start.40 = (bf16[256,1536]{1,0:T(8,128)(2,1)}, bf16[256,1536]{1,0:T(8,128)(2,1)S(1)}, u32[]{:S(2)}, u32[]{:S(2)}) collective-permute-start(bf16[256,1536]{1,0:T(8,128)(2,1)} %collective-permute-done.37), channel_id=1, source_target_pairs={{0,1},{1,0},{2,3},{3,2},{4,5},{5,4},{6,7},{7,6},{8,9},{9,8},{10,11... | collective-permute-start | bytes 2359304 | tf_op jit(solution)/shard_map/ppermute | solution.py:223
  81.2 7.7 %collective-permute-start.41 = (bf16[256,1536]{1,0:T(8,128)(2,1)}, bf16[256,1536]{1,0:T(8,128)(2,1)S(1)}, u32[]{:S(2)}, u32[]{:S(2)}) collective-permute-start(bf16[256,1536]{1,0:T(8,128)(2,1)} %collective-permute-done.38), channel_id=1, source_target_pairs={{0,1},{1,0},{2,3},{3,2},{4,5},{5,4},{6,7},{7,6},{8,9},{9,8},{10,11... | collective-permute-start | bytes 2359304 | tf_op jit(solution)/shard_map/ppermute | solution.py:223
  95.0 38.6 %collective-permute-start.30 = (bf16[256,1536]{1,0:T(8,128)(2,1)S(1)}, bf16[256,1536]{1,0:T(8,128)(2,1)S(1)}, u32[]{:S(2)}, u32[]{:S(2)}) collective-permute-start(bf16[256,1536]{1,0:T(8,128)(2,1)S(1)} %constant_dynamic-slice_fusion.2), channel_id=1, source_target_pairs={{0,2},{2,0},{4,6},{6,4},{8,10},{10,8},{12,14},{14,12},{16,18},{18,... | collective-permute-start | bytes 2359304 | tf_op jit(solution)/shard_map/ppermute | solution.py:222
  97.0 37.5 %collective-permute-start.31 = (bf16[256,1536]{1,0:T(8,128)(2,1)S(1)}, bf16[256,1536]{1,0:T(8,128)(2,1)S(1)}, u32[]{:S(2)}, u32[]{:S(2)}) collective-permute-start(bf16[256,1536]{1,0:T(8,128)(2,1)S(1)} %constant_dynamic-slice_fusion.2), channel_id=1, source_target_pairs={{0,4},{2,6},{4,0},{6,2},{8,12},{10,14},{12,8},{14,10},{16,20},{18,... | collective-permute-start | bytes 2359304 | tf_op jit(solution)/shard_map/ppermute | solution.py:222
  98.5 36.4 %collective-permute-start.32 = (bf16[256,1536]{1,0:T(8,128)(2,1)S(1)}, bf16[256,1536]{1,0:T(8,128)(2,1)S(1)}, u32[]{:S(2)}, u32[]{:S(2)}) collective-permute-start(bf16[256,1536]{1,0:T(8,128)(2,1)S(1)} %constant_dynamic-slice_fusion.2), channel_id=1, source_target_pairs={{0,6},{2,4},{4,2},{6,0},{8,14},{10,12},{12,10},{14,8},{16,22},{18,... | collective-permute-start | bytes 2359304 | tf_op jit(solution)/shard_map/ppermute | solution.py:222
  133.6 2.4 collective-permute-start.33
  133.8 44.6 %collective-permute-start.3 = (bf16[512,1536]{1,0:T(8,128)(2,1)S(1)}, bf16[512,1536]{1,0:T(8,128)(2,1)S(1)}, u32[]{:S(2)}, u32[]{:S(2)}) collective-permute-start(bf16[512,1536]{1,0:T(8,128)(2,1)S(1)} %get-tuple-element.80.mine), channel_id=1, source_target_pairs={{0,1},{1,0},{2,3},{3,2},{4,5},{5,4},{6,7},{7,6},{8,9},{9,8},{10,11... | collective-permute-start | bytes 4718600 | tf_op jit(solution)/shard_map/ppermute | solution.py:709
  134.4 103.3 %collective-permute-start.2 = (bf16[512,1536]{1,0:T(8,128)(2,1)S(1)}, bf16[512,1536]{1,0:T(8,128)(2,1)}, u32[]{:S(2)}, u32[]{:S(2)}) collective-permute-start(bf16[512,1536]{1,0:T(8,128)(2,1)S(1)} %get-tuple-element.79), channel_id=1, source_target_pairs={{0,1},{1,0},{2,3},{3,2},{4,5},{5,4},{6,7},{7,6},{8,9},{9,8},{10,11... | collective-permute-start | bytes 4718600 | tf_op jit(solution)/shard_map/ppermute | solution.py:709
  134.5 7.1 %collective-permute-start.34 = (bf16[256,1536]{1,0:T(8,128)(2,1)S(1)}, bf16[256,1536]{1,0:T(8,128)(2,1)S(1)}, u32[]{:S(2)}, u32[]{:S(2)}) collective-permute-start(bf16[256,1536]{1,0:T(8,128)(2,1)S(1)} %collective-permute-done.31), channel_id=1, source_target_pairs={{0,1},{1,0},{2,3},{3,2},{4,5},{5,4},{6,7},{7,6},{8,9},{9,8},{10,11... | collective-permute-start | bytes 2359304 | tf_op jit(solution)/shard_map/ppermute | solution.py:223
  135.0 7.8 %collective-permute-start.35 = (bf16[256,1536]{1,0:T(8,128)(2,1)S(1)}, bf16[256,1536]{1,0:T(8,128)(2,1)S(1)}, u32[]{:S(2)}, u32[]{:S(2)}) collective-permute-start(bf16[256,1536]{1,0:T(8,128)(2,1)S(1)} %collective-permute-done.32), channel_id=1, source_target_pairs={{0,1},{1,0},{2,3},{3,2},{4,5},{5,4},{6,7},{7,6},{8,9},{9,8},{10,11... | collective-permute-start | bytes 2359304 | tf_op jit(solution)/shard_map/ppermute | solution.py:223
  159.5 100.7 %collective-permute-start.42 = (bf16[2,3,384,256]{3,2,1,0:T(8,128)(2,1)}, bf16[2,3,384,256]{3,2,1,0:T(8,128)(2,1)}, u32[]{:S(2)}, u32[]{:S(2)}) collective-permute-start(bf16[2,3,384,256]{3,2,1,0:T(8,128)(2,1)} %get-tuple-element.124), channel_id=1, source_target_pairs={{0,8},{2,10},{4,12},{6,14},{8,0},{10,2},{12,4},{14,6},{16,24},{18,... | collective-permute-start | bytes 3538952 | tf_op jit(solution)/shard_map/ppermute | solution.py:194
  178.3 85.4 %collective-permute-start.44 = (bf16[2,3,384,256]{3,2,1,0:T(8,128)(2,1)}, bf16[2,3,384,256]{3,2,1,0:T(8,128)(2,1)}, u32[]{:S(2)}, u32[]{:S(2)}) collective-permute-start(bf16[2,3,384,256]{3,2,1,0:T(8,128)(2,1)} %get-tuple-element.126), channel_id=1, source_target_pairs={{0,8},{2,10},{4,12},{6,14},{8,0},{10,2},{12,4},{14,6},{16,24},{18,... | collective-permute-start | bytes 3538952 | tf_op jit(solution)/shard_map/ppermute | solution.py:194
  179.6 25.3 %copy-start.28 = (bf16[512,768]{1,0:T(8,128)(2,1)S(1)}, bf16[512,768]{1,0:T(8,128)(2,1)}, u32[]{:S(2)}) copy-start(bf16[512,768]{1,0:T(8,128)(2,1)} %copy-done.27) | copy-start | bytes 2359300
  217.9 21.6 %collective-permute-start.26 = (bf16[4,144,768]{2,1,0:T(8,128)(2,1)}, bf16[4,144,768]{2,1,0:T(8,128)(2,1)S(1)}, u32[]{:S(2)}, u32[]{:S(2)}) collective-permute-start(bf16[4,144,768]{2,1,0:T(8,128)(2,1)} %get-tuple-element.122), channel_id=1, source_target_pairs={{0,2},{2,0},{4,6},{6,4},{8,10},{10,8},{12,14},{14,12},{16,18},{18,... | collective-permute-start | bytes 2654216 | tf_op jit(solution)/shard_map/ppermute | solution.py:214
  236.0 32.9 %copy-start.4 = (bf16[2,3,384,256]{3,2,1,0:T(8,128)(2,1)}, bf16[2,3,384,256]{3,2,1,0:T(8,128)(2,1)S(1)}, u32[]{:S(2)}) copy-start(bf16[2,3,384,256]{3,2,1,0:T(8,128)(2,1)S(1)} %get-tuple-element.127) | copy-start | bytes 3538948
  236.0 32.6 %collective-permute-start.46 = (bf16[2,3,384,256]{3,2,1,0:T(8,128)(2,1)S(1)}, bf16[2,3,384,256]{3,2,1,0:T(8,128)(2,1)S(1)}, u32[]{:S(2)}, u32[]{:S(2)}) collective-permute-start(bf16[2,3,384,256]{3,2,1,0:T(8,128)(2,1)S(1)} %get-tuple-element.128), channel_id=1, source_target_pairs={{0,8},{2,10},{4,12},{6,14},{8,0},{10,2},{12,4},{14,6},{16,24},{18,... | collective-permute-start | bytes 3538952 | tf_op jit(solution)/shard_map/ppermute | solution.py:194
  237.7 20.8 %collective-permute-start.21 = (bf16[4,144,768]{2,1,0:T(8,128)(2,1)}, bf16[4,144,768]{2,1,0:T(8,128)(2,1)S(1)}, u32[]{:S(2)}, u32[]{:S(2)}) collective-permute-start(bf16[4,144,768]{2,1,0:T(8,128)(2,1)} %get-tuple-element.118), channel_id=1, source_target_pairs={{0,4},{2,6},{4,0},{6,2},{8,12},{10,14},{12,8},{14,10},{16,20},{18,... | collective-permute-start | bytes 2654216 | tf_op jit(solution)/shard_map/ppermute | solution.py:214
  239.6 30.4 %collective-permute-start.4 = (bf16[512,1536]{1,0:T(8,128)(2,1)}, bf16[512,1536]{1,0:T(8,128)(2,1)S(1)}, u32[]{:S(2)}, u32[]{:S(2)}) collective-permute-start(bf16[512,1536]{1,0:T(8,128)(2,1)} %get-tuple-element.83.mine), channel_id=1, source_target_pairs={{0,1},{1,0},{2,3},{3,2},{4,5},{5,4},{6,7},{7,6},{8,9},{9,8},{10,11... | collective-permute-start | bytes 4718600 | tf_op jit(solution)/shard_map/ppermute | solution.py:709
  258.5 84.3 %collective-permute-start.25 = (bf16[4,144,768]{2,1,0:T(8,128)(2,1)S(1)}, bf16[4,144,768]{2,1,0:T(8,128)(2,1)S(1)}, u32[]{:S(2)}, u32[]{:S(2)}) collective-permute-start(bf16[4,144,768]{2,1,0:T(8,128)(2,1)S(1)} %copy-done.22), channel_id=1, source_target_pairs={{0,2},{2,0},{4,6},{6,4},{8,10},{10,8},{12,14},{14,12},{16,18},{18,... | collective-permute-start | bytes 2654216 | tf_op jit(solution)/shard_map/ppermute | solution.py:215
  260.1 85.1 %collective-permute-start.20 = (bf16[4,144,768]{2,1,0:T(8,128)(2,1)}, bf16[4,144,768]{2,1,0:T(8,128)(2,1)S(1)}, u32[]{:S(2)}, u32[]{:S(2)}) collective-permute-start(bf16[4,144,768]{2,1,0:T(8,128)(2,1)} %get-tuple-element.116), channel_id=1, source_target_pairs={{0,4},{2,6},{4,0},{6,2},{8,12},{10,14},{12,8},{14,10},{16,20},{18,... | collective-permute-start | bytes 2654216 | tf_op jit(solution)/shard_map/ppermute | solution.py:215
  263.7 52.4 %collective-permute-start.43 = (bf16[3,384,256]{2,1,0:T(8,128)(2,1)}, bf16[3,384,256]{2,1,0:T(8,128)(2,1)}, u32[]{:S(2)}, u32[]{:S(2)}) collective-permute-start(bf16[3,384,256]{2,1,0:T(8,128)(2,1)} %fusion.5), channel_id=1, source_target_pairs={{0,16},{2,18},{4,20},{6,22},{8,24},{10,26},{12,28},{14,30},{16,0},... | collective-permute-start | bytes 1769480 | tf_op jit(solution)/shard_map/ppermute | solution.py:200
  268.6 60.1 %collective-permute-start.45 = (bf16[3,384,256]{2,1,0:T(8,128)(2,1)}, bf16[3,384,256]{2,1,0:T(8,128)(2,1)S(1)}, u32[]{:S(2)}, u32[]{:S(2)}) collective-permute-start(bf16[3,384,256]{2,1,0:T(8,128)(2,1)} %fusion.6), channel_id=1, source_target_pairs={{0,16},{2,18},{4,20},{6,22},{8,24},{10,26},{12,28},{14,30},{16,0},... | collective-permute-start | bytes 1769480 | tf_op jit(solution)/shard_map/ppermute | solution.py:200
  269.9 70.9 %collective-permute-start.47 = (bf16[3,384,256]{2,1,0:T(8,128)(2,1)}, bf16[3,384,256]{2,1,0:T(8,128)(2,1)S(1)}, u32[]{:S(2)}, u32[]{:S(2)}) collective-permute-start(bf16[3,384,256]{2,1,0:T(8,128)(2,1)} %fusion.7), channel_id=1, source_target_pairs={{0,16},{2,18},{4,20},{6,22},{8,24},{10,26},{12,28},{14,30},{16,0},... | collective-permute-start | bytes 1769480 | tf_op jit(solution)/shard_map/ppermute | solution.py:200
  272.6 29.9 %copy-start.39 = (bf16[512,768]{1,0:T(8,128)(2,1)S(1)}, bf16[512,768]{1,0:T(8,128)(2,1)}, u32[]{:S(2)}) copy-start(bf16[512,768]{1,0:T(8,128)(2,1)} %copy-done.38) | copy-start | bytes 2359300
  316.1 27.3 %collective-permute-start.27 = (bf16[4,144,768]{2,1,0:T(8,128)(2,1)S(1)}, bf16[4,144,768]{2,1,0:T(8,128)(2,1)S(1)}, u32[]{:S(2)}, u32[]{:S(2)}) collective-permute-start(bf16[4,144,768]{2,1,0:T(8,128)(2,1)S(1)} %copy-done.56), channel_id=1, source_target_pairs={{0,4},{2,6},{4,0},{6,2},{8,12},{10,14},{12,8},{14,10},{16,20},{18,... | collective-permute-start | bytes 2654216 | tf_op jit(solution)/shard_map/ppermute | solution.py:217
  319.2 21.6 %copy-start.5 = (bf16[2,3,384,256]{3,2,1,0:T(8,128)(2,1)S(1)}, bf16[2,3,384,256]{3,2,1,0:T(8,128)(2,1)}, u32[]{:S(2)}) copy-start(bf16[2,3,384,256]{3,2,1,0:T(8,128)(2,1)} %copy-done.4) | copy-start | bytes 3538948
  328.7 22.6 %collective-permute-start.22 = (bf16[4,144,768]{2,1,0:T(8,128)(2,1)S(1)}, bf16[4,144,768]{2,1,0:T(8,128)(2,1)S(1)}, u32[]{:S(2)}, u32[]{:S(2)}) collective-permute-start(bf16[4,144,768]{2,1,0:T(8,128)(2,1)S(1)} %copy-done.55), channel_id=1, source_target_pairs={{0,2},{2,0},{4,6},{6,4},{8,10},{10,8},{12,14},{14,12},{16,18},{18,... | collective-permute-start | bytes 2654216 | tf_op jit(solution)/shard_map/ppermute | solution.py:217
  341.3 19.4 %collective-permute-start.48 = (bf16[3,96,768]{2,1,0:T(8,128)(2,1)S(1)}, bf16[3,96,768]{2,1,0:T(8,128)(2,1)S(1)}, u32[]{:S(2)}, u32[]{:S(2)}) collective-permute-start(bf16[3,96,768]{2,1,0:T(8,128)(2,1)S(1)} %get-tuple-element.141), channel_id=1, source_target_pairs={{0,2},{2,0},{4,6},{6,4},{8,10},{10,8},{12,14},{14,12},{16,18},{18,... | collective-permute-start | bytes 1327112 | tf_op jit(solution)/shard_map/ppermute | solution.py:355
  342.8 18.9 %collective-permute-start.49 = (bf16[3,96,768]{2,1,0:T(8,128)(2,1)S(1)}, bf16[3,96,768]{2,1,0:T(8,128)(2,1)S(1)}, u32[]{:S(2)}, u32[]{:S(2)}) collective-permute-start(bf16[3,96,768]{2,1,0:T(8,128)(2,1)S(1)} %get-tuple-element.140), channel_id=1, source_target_pairs={{0,4},{2,6},{4,0},{6,2},{8,12},{10,14},{12,8},{14,10},{16,20},{18,... | collective-permute-start | bytes 1327112 | tf_op jit(solution)/shard_map/ppermute | solution.py:355
  343.4 27.8 %collective-permute-start.50 = (bf16[3,96,768]{2,1,0:T(8,128)(2,1)S(1)}, bf16[3,96,768]{2,1,0:T(8,128)(2,1)S(1)}, u32[]{:S(2)}, u32[]{:S(2)}) collective-permute-start(bf16[3,96,768]{2,1,0:T(8,128)(2,1)S(1)} %get-tuple-element.139), channel_id=1, source_target_pairs={{0,6},{2,4},{4,2},{6,0},{8,14},{10,12},{12,10},{14,8},{16,22},{18,... | collective-permute-start | bytes 1327112 | tf_op jit(solution)/shard_map/ppermute | solution.py:355
  346.2 49.4 %collective-permute-start.16 = (bf16[4,192,768]{2,1,0:T(8,128)(2,1)S(1)}, bf16[4,192,768]{2,1,0:T(8,128)(2,1)S(1)}, u32[]{:S(2)}, u32[]{:S(2)}) collective-permute-start(bf16[4,192,768]{2,1,0:T(8,128)(2,1)S(1)} %copy-done.64), channel_id=1, source_target_pairs={{0,2},{2,0},{4,6},{6,4},{8,10},{10,8},{12,14},{14,12},{16,18},{18,... | collective-permute-start | bytes 3538952 | tf_op jit(solution)/shard_map/ppermute | solution.py:214
  351.3 20.8 %collective-permute-start.28 = (bf16[2,144,768]{2,1,0:T(8,128)(2,1)S(1)}, bf16[2,144,768]{2,1,0:T(8,128)(2,1)S(1)}, u32[]{:S(2)}, u32[]{:S(2)}) collective-permute-start(bf16[2,144,768]{2,1,0:T(8,128)(2,1)S(1)} %dynamic-slice_bitcast_fusion.10), channel_id=1, source_target_pairs={{0,8},{2,10},{4,12},{6,14},{8,0},{10,2},{12,4},{14,6},{16,24},{18,... | collective-permute-start | bytes 1327112 | tf_op jit(solution)/shard_map/ppermute | solution.py:194
  360.7 98.5 %collective-permute-start.15 = (bf16[4,192,768]{2,1,0:T(8,128)(2,1)S(1)}, bf16[4,192,768]{2,1,0:T(8,128)(2,1)S(1)}, u32[]{:S(2)}, u32[]{:S(2)}) collective-permute-start(bf16[4,192,768]{2,1,0:T(8,128)(2,1)S(1)} %get-tuple-element.106), channel_id=1, source_target_pairs={{0,2},{2,0},{4,6},{6,4},{8,10},{10,8},{12,14},{14,12},{16,18},{18,... | collective-permute-start | bytes 3538952 | tf_op jit(solution)/shard_map/ppermute | solution.py:215
  361.7 42.1 %collective-permute-start.11 = (bf16[4,192,768]{2,1,0:T(8,128)(2,1)}, bf16[4,192,768]{2,1,0:T(8,128)(2,1)S(1)}, u32[]{:S(2)}, u32[]{:S(2)}) collective-permute-start(bf16[4,192,768]{2,1,0:T(8,128)(2,1)} %get-tuple-element.104), channel_id=1, source_target_pairs={{0,4},{2,6},{4,0},{6,2},{8,12},{10,14},{12,8},{14,10},{16,20},{18,... | collective-permute-start | bytes 3538952 | tf_op jit(solution)/shard_map/ppermute | solution.py:214
  371.2 90.7 %collective-permute-start.10 = (bf16[4,192,768]{2,1,0:T(8,128)(2,1)}, bf16[4,192,768]{2,1,0:T(8,128)(2,1)S(1)}, u32[]{:S(2)}, u32[]{:S(2)}) collective-permute-start(bf16[4,192,768]{2,1,0:T(8,128)(2,1)} %get-tuple-element.102), channel_id=1, source_target_pairs={{0,4},{2,6},{4,0},{6,2},{8,12},{10,14},{12,8},{14,10},{16,20},{18,... | collective-permute-start | bytes 3538952 | tf_op jit(solution)/shard_map/ppermute | solution.py:215
  373.4 22.9 %collective-permute-start.5 = (bf16[512,1536]{1,0:T(8,128)(2,1)S(1)}, bf16[512,1536]{1,0:T(8,128)(2,1)S(1)}, u32[]{:S(2)}, u32[]{:S(2)}) collective-permute-start(bf16[512,1536]{1,0:T(8,128)(2,1)S(1)} %copy-done.2), channel_id=1, source_target_pairs={{0,1},{1,0},{2,3},{3,2},{4,5},{5,4},{6,7},{7,6},{8,9},{9,8},{10,11... | collective-permute-start | bytes 4718600 | tf_op jit(solution)/shard_map/ppermute | solution.py:709
  373.8 22.1 %copy-start.51 = (bf16[4,192,768]{2,1,0:T(8,128)(2,1)S(1)}, bf16[4,192,768]{2,1,0:T(8,128)(2,1)}, u32[]{:S(2)}) copy-start(bf16[4,192,768]{2,1,0:T(8,128)(2,1)} %get-tuple-element.107) | copy-start | bytes 3538948
  395.5 9.5 %collective-permute-start.23 = (bf16[2,144,768]{2,1,0:T(8,128)(2,1)S(1)}, bf16[2,144,768]{2,1,0:T(8,128)(2,1)S(1)}, u32[]{:S(2)}, u32[]{:S(2)}) collective-permute-start(bf16[2,144,768]{2,1,0:T(8,128)(2,1)S(1)} %dynamic-slice_bitcast_fusion.11), channel_id=1, source_target_pairs={{0,8},{2,10},{4,12},{6,14},{8,0},{10,2},{12,4},{14,6},{16,24},{18,... | collective-permute-start | bytes 1327112 | tf_op jit(solution)/shard_map/ppermute | solution.py:194
  396.3 63.0 %collective-permute-start.17 = (bf16[4,192,768]{2,1,0:T(8,128)(2,1)S(1)}, bf16[4,192,768]{2,1,0:T(8,128)(2,1)S(1)}, u32[]{:S(2)}, u32[]{:S(2)}) collective-permute-start(bf16[4,192,768]{2,1,0:T(8,128)(2,1)S(1)} %add_convert_fusion.1), channel_id=1, source_target_pairs={{0,4},{2,6},{4,0},{6,2},{8,12},{10,14},{12,8},{14,10},{16,20},{18,... | collective-permute-start | bytes 3538952 | tf_op jit(solution)/shard_map/ppermute | solution.py:217
  403.8 16.2 %collective-permute-start.6 = (f32[6,1536]{1,0:T(8,128)S(1)}, f32[6,1536]{1,0:T(8,128)S(1)}, u32[]{:S(2)}, u32[]{:S(2)}) collective-permute-start(f32[6,1536]{1,0:T(8,128)S(1)} %pad_maximum_fusion.2), channel_id=1, source_target_pairs={{0,2},{2,0},{4,6},{6,4},{8,10},{10,8},{12,14},{14,12},{16,18},{18,... | collective-permute-start | bytes 110600 | tf_op jit(solution)/shard_map/ppermute | solution.py:168
  405.1 16.7 %collective-permute-start.29 = (bf16[144,768]{1,0:T(8,128)(2,1)S(1)}, bf16[144,768]{1,0:T(8,128)(2,1)S(1)}, u32[]{:S(2)}, u32[]{:S(2)}) collective-permute-start(bf16[144,768]{1,0:T(8,128)(2,1)S(1)} %fusion.14), channel_id=1, source_target_pairs={{0,16},{2,18},{4,20},{6,22},{8,24},{10,26},{12,28},{14,30},{16,0},... | collective-permute-start | bytes 663560 | tf_op jit(solution)/shard_map/ppermute | solution.py:200
  420.0 41.9 %collective-permute-start.12 = (bf16[4,192,768]{2,1,0:T(8,128)(2,1)S(1)}, bf16[4,192,768]{2,1,0:T(8,128)(2,1)S(1)}, u32[]{:S(2)}, u32[]{:S(2)}) collective-permute-start(bf16[4,192,768]{2,1,0:T(8,128)(2,1)S(1)} %add_convert_fusion.3), channel_id=1, source_target_pairs={{0,2},{2,0},{4,6},{6,4},{8,10},{10,8},{12,14},{14,12},{16,18},{18,... | collective-permute-start | bytes 3538952 | tf_op jit(solution)/shard_map/ppermute | solution.py:217
  421.8 23.0 %collective-permute-start.7 = (f32[6,1536]{1,0:T(8,128)S(1)}, f32[6,1536]{1,0:T(8,128)S(1)}, u32[]{:S(2)}, u32[]{:S(2)}) collective-permute-start(f32[6,1536]{1,0:T(8,128)S(1)} %fusion.23), channel_id=1, source_target_pairs={{0,4},{2,6},{4,0},{6,2},{8,12},{10,14},{12,8},{14,10},{16,20},{18,... | collective-permute-start | bytes 110600 | tf_op jit(solution)/shard_map/ppermute | solution.py:168
  444.8 9.7 %collective-permute-start.24 = (bf16[144,768]{1,0:T(8,128)(2,1)S(1)}, bf16[144,768]{1,0:T(8,128)(2,1)S(1)}, u32[]{:S(2)}, u32[]{:S(2)}) collective-permute-start(bf16[144,768]{1,0:T(8,128)(2,1)S(1)} %fusion.16), channel_id=1, source_target_pairs={{0,16},{2,18},{4,20},{6,22},{8,24},{10,26},{12,28},{14,30},{16,0},... | collective-permute-start | bytes 663560 | tf_op jit(solution)/shard_map/ppermute | solution.py:200
  454.5 4.1 collective-permute-start.8
  458.6 7.9 %collective-permute-start.9 = (f32[6,1536]{1,0:T(8,128)S(1)}, f32[6,1536]{1,0:T(8,128)S(1)}, u32[]{:S(2)}, u32[]{:S(2)}) collective-permute-start(f32[6,1536]{1,0:T(8,128)S(1)} %add.295), channel_id=1, source_target_pairs={{0,16},{2,18},{4,20},{6,22},{8,24},{10,26},{12,28},{14,30},{16,0},... | collective-permute-start | bytes 110600 | tf_op jit(solution)/shard_map/ppermute | solution.py:168
  459.8 19.9 %collective-permute-start.18 = (bf16[2,192,768]{2,1,0:T(8,128)(2,1)S(1)}, bf16[2,192,768]{2,1,0:T(8,128)(2,1)S(1)}, u32[]{:S(2)}, u32[]{:S(2)}) collective-permute-start(bf16[2,192,768]{2,1,0:T(8,128)(2,1)S(1)} %dynamic-slice_bitcast_fusion), channel_id=1, source_target_pairs={{0,8},{2,10},{4,12},{6,14},{8,0},{10,2},{12,4},{14,6},{16,24},{18,... | collective-permute-start | bytes 1769480 | tf_op jit(solution)/shard_map/ppermute | solution.py:194
  462.5 31.0 %collective-permute-start.13 = (bf16[2,192,768]{2,1,0:T(8,128)(2,1)S(1)}, bf16[2,192,768]{2,1,0:T(8,128)(2,1)S(1)}, u32[]{:S(2)}, u32[]{:S(2)}) collective-permute-start(bf16[2,192,768]{2,1,0:T(8,128)(2,1)S(1)} %dynamic-slice_bitcast_fusion.1), channel_id=1, source_target_pairs={{0,8},{2,10},{4,12},{6,14},{8,0},{10,2},{12,4},{14,6},{16,24},{18,... | collective-permute-start | bytes 1769480 | tf_op jit(solution)/shard_map/ppermute | solution.py:194
  479.8 13.8 %collective-permute-start.19 = (bf16[192,768]{1,0:T(8,128)(2,1)S(1)}, bf16[192,768]{1,0:T(8,128)(2,1)S(1)}, u32[]{:S(2)}, u32[]{:S(2)}) collective-permute-start(bf16[192,768]{1,0:T(8,128)(2,1)S(1)} %fusion.8), channel_id=1, source_target_pairs={{0,16},{2,18},{4,20},{6,22},{8,24},{10,26},{12,28},{14,30},{16,0},... | collective-permute-start | bytes 884744 | tf_op jit(solution)/shard_map/ppermute | solution.py:200
  493.5 13.8 %collective-permute-start.14 = (bf16[192,768]{1,0:T(8,128)(2,1)S(1)}, bf16[192,768]{1,0:T(8,128)(2,1)S(1)}, u32[]{:S(2)}, u32[]{:S(2)}) collective-permute-start(bf16[192,768]{1,0:T(8,128)(2,1)S(1)} %fusion.10), channel_id=1, source_target_pairs={{0,16},{2,18},{4,20},{6,22},{8,24},{10,26},{12,28},{14,30},{16,0},... | collective-permute-start | bytes 884744 | tf_op jit(solution)/shard_map/ppermute | solution.py:200
  (52 other events, 324.1 us)

commit v4 on v1

--- a/solution.py
+++ b/solution.py
@@ -1,12 +1,21 @@
+import functools
 import math
 
 import jax
 import jax.numpy as jnp
 from jax import lax
+from jax.experimental import pallas as pl
+from jax.experimental.pallas import tpu as pltpu
 from jax.sharding import PartitionSpec as P
 
 PROMPT = 128
 HEAD = 64
+PLANE = 4
+LEVELS = 4
+
+low = jnp.bfloat16
+f32 = jnp.float32
+sds = jax.ShapeDtypeStruct
 
 
 norm_eps = 1e-05
@@ -153,78 +162,8 @@
     return [(i, i ^ mask) for i in range(16)]
 
 
-def quarters(rows_side, mine):
-    blocks = rows_side.reshape(4, 4, rows_side.shape[0] // 16, rows_side.shape[1])
-    out = []
-    for flip in range(4):
-        part = lax.dynamic_index_in_dim(blocks, mine ^ flip, 1, keepdims=False)
-        out.append(part.reshape(rows_side.shape[0] // 4, rows_side.shape[1]))
-    return out
-
-
-def add_low(*terms):
-    total = terms[0].astype(jnp.float32)
-    for term in terms[1:]:
-        total = total + term.astype(jnp.float32)
-    return total
-
-
-def z_scatter(own, z_index):
-    def block(offset):
-        return lax.dynamic_index_in_dim(own, jnp.clip(z_index + offset, 0, 3), 0, keepdims=False)
-
-    up = down = None
-    for step in range(1, 4):
-        up_perm = [(i, i + 4) for i in range(16) if i // 4 <= step - 1 and i // 4 < 3]
-        down_perm = [(i, i - 4) for i in range(16) if i // 4 >= 4 - step and i // 4 > 0]
-        up_send, down_send = block(4 - step), block(step - 4)
-        if up is not None:
-            up_send = add_low(up_send, up).astype(jnp.bfloat16)
-            down_send = add_low(down_send, down).astype(jnp.bfloat16)
-        up = lax.ppermute(up_send, "dp", up_perm)
-        down = lax.ppermute(down_send, "dp", down_perm)
-    return add_low(block(0), up, down)
-
-
-def plane_scatter(parts):
-    own, to_x, to_y, to_d = parts
-    half = own.shape[1] // 2
-    low = jnp.bfloat16
-    pieces = []
-    for first, second, cut in ((1, 2, slice(0, half)), (2, 1, slice(half, 2 * half))):
-        to_first = to_x if first == 1 else to_y
-        to_second = to_y if first == 1 else to_x
-        got_diag = lax.ppermute(to_d[:, cut], "dp", pairs(first))
-        got_own = lax.ppermute(to_first[:, cut], "dp", pairs(first))
-        passed = add_low(to_second[:, cut], got_diag).astype(low)
-        got_last = lax.ppermute(passed, "dp", pairs(second))
-        pieces.append(add_low(own[:, cut], got_own, got_last).astype(low))
-    return jnp.concatenate(pieces, axis=1)
-
-
-def weight_sum(rows_side, column_side, turned=False):
-    if lax.axis_size("dp") == 16 and lax.axis_size("tensor") == 2:
-        index = lax.axis_index("dp")
-        turned_rows = rows_side.T
-        parts = [
-            product_plain(part, column_side).astype(jnp.bfloat16)
-            for part in quarters(turned_rows, index % 4)
-        ]
-        own = plane_scatter(parts)
-        own = own.reshape(4, own.shape[0] // 4, own.shape[1])
-        total = z_scatter(own, index // 4)
-    else:
-        total = lax.psum_scatter(
-            product_over_rows(rows_side, column_side).astype(jnp.bfloat16),
-            "dp",
-            scatter_dimension=0,
-            tiled=True,
-        ).astype(jnp.float32)
-    return total.T if turned else total
-
-
 def vector_sum(vectors):
-    if lax.axis_size("dp") == 16:
+    if lax.axis_size("dp") == PLANE * LEVELS:
         for mask in (1, 2, 4, 8):
             vectors = vectors + lax.ppermute(vectors, "dp", pairs(mask))
     else:
@@ -234,7 +173,687 @@
     return lax.dynamic_slice_in_dim(vectors, index * share, share, 1)
 
 
-def on_device(
+def generic_sum(rows_side, column_side):
+    return lax.psum_scatter(
+        product_over_rows(rows_side, column_side).astype(jnp.bfloat16),
+        "dp",
+        scatter_dimension=0,
+        tiled=True,
+    ).astype(jnp.float32)
+
+
+def add_low(*terms):
+    total = terms[0].astype(jnp.float32)
+    for term in terms[1:]:
+        total = total + term.astype(jnp.float32)
+    return total
+
+
+def ff_parts(gate, up, grad_mixed):
+    sig = 1.0 / (1.0 + jnp.exp(-gate))
+    act = gate * sig
+    return (
+        (act * up).astype(low),
+        (grad_mixed * up * sig * (1.0 + gate * (1.0 - sig))).astype(low),
+        (grad_mixed * act).astype(low),
+    )
+
+
+def turn(values, cos, lower, upper):
+    width = values.shape[1]
+    return (values * cos + pltpu.roll(values, width - 16, 1) * lower + pltpu.roll(values, 16, 1) * upper)
+
+def turn_back(values, cos, lower, upper):
+    width = values.shape[1]
+    return (values * cos + pltpu.roll(values * lower, 16, 1) + pltpu.roll(values * upper, width - 16, 1))
+
+def normed_rows(values, gain, shift):
+    average = jnp.mean(values, axis=-1, keepdims=True)
+    centered = values - average
+    variance = jnp.mean(centered * centered, axis=-1, keepdims=True)
+    return centered * lax.rsqrt(variance + norm_eps) * gain + shift
+
+def over_rows(rows, body, chunk=32):
+    @pl.loop(0, rows // chunk, unroll=min(4, rows // chunk))
+    def _(i):
+        body(pl.ds(pl.multiple_of(i * chunk, chunk), chunk))
+
+def attend(q, k, v, mask, lse_ref):
+    q_turned = (q * jnp.bfloat16(0.125)).T
+    v_turned = v.T
+    outs = []
+    for h in range(q.shape[1] // HEAD):
+        c = slice(h * HEAD, (h + 1) * HEAD)
+        s = product_plain(k[:, c], q_turned[c, :]) + mask
+        m = jnp.max(s, axis=0, keepdims=True)
+        e = jnp.exp(s - m)
+        total = jnp.sum(e, axis=0, keepdims=True)
+        o = product_plain(v_turned[c, :], e.astype(low)) * (1.0 / total)
+        outs.append(o)
+        lse_ref[h : h + 1, :] = m + jnp.log(total)
+    return jnp.concatenate(outs, axis=0).T.astype(low)
+
+
+def attend_back(q, k, v, g, mask, lse):
+    scaled = q * jnp.bfloat16(0.125)
+    q_turned = scaled.T
+    g_turned = g.T
+    k_turned = k.T
+    dq, dk, dv = [], [], []
+    for h in range(q.shape[1] // HEAD):
+        c = slice(h * HEAD, (h + 1) * HEAD)
+        p = jnp.exp(product_plain(k[:, c], q_turned[c, :]) + (mask - lse[h : h + 1, :]))
+        dp = product_plain(v[:, c], g_turned[c, :])
+        inner = jnp.sum(p * dp, axis=0, keepdims=True)
+        ds = (p * (dp - inner)).astype(low)
+        dq.append(product_plain(k_turned[c, :], ds))
+        dk.append(product_plain(ds, scaled[:, c]))
+        dv.append(product_plain(p.astype(low), g[:, c]))
+    return (
+        jnp.concatenate(dq, axis=0).T * 0.125,
+        jnp.concatenate(dk, axis=1),
+        jnp.concatenate(dv, axis=1),
+    )
+
+
+def self_mask(split, T):
+    r=lax.broadcasted_iota(jnp.int32,(T,T),0)>=split
+    c=lax.broadcasted_iota(jnp.int32,(T,T),1)>=split
+    return jnp.where(r==c,0.0,masked_score).astype(f32)
+
+def cross_mask(split, first, second, T, K):
+    r = lax.broadcasted_iota(jnp.int32, (K, T), 1) >= split
+    c = lax.broadcasted_iota(jnp.int32, (K, T), 0)
+    least = jnp.where(r, K // 2, 0)
+    most = jnp.where(r, K // 2 + second, first)
+    return jnp.where((c >= least) & (c < most), 0.0, masked_score).astype(f32)
+
+
+def norm_back_rows(x,e,gain,above,gain_acc,shift_acc):
+    average=jnp.mean(x,axis=-1,keepdims=True)
+    centered=x-average
+    variance=jnp.mean(centered*centered,axis=-1,keepdims=True)
+    inverse=lax.rsqrt(variance+norm_eps)
+    n=centered*inverse
+    en=e*n
+    w=e*gain
+    mean_w=jnp.mean(w,axis=-1,keepdims=True)
+    mean_wn=jnp.mean(en*gain,axis=-1,keepdims=True)
+    fold=lambda t: jnp.sum(t.reshape(t.shape[0]//8,8,t.shape[1]),axis=0)
+    gain_acc[...]+=fold(en)
+    shift_acc[...]+=fold(e)
+    return above+inverse*(w-mean_w-n*mean_wn)
+
+def norm_back_all(x,mine,other,above,gain,total,total_low,vec,gacc,sacc):
+    gacc[...]=jnp.zeros_like(gacc);sacc[...]=jnp.zeros_like(sacc)
+    def rows(r):
+        e=mine[r,:].astype(f32)+other[r,:].astype(f32)
+        t=norm_back_rows(x[r,:],e,gain[...],above[r,:],gacc,sacc)
+        total[r,:]=t
+        if total_low is not None: total_low[r,:]=t.astype(low)
+    over_rows(x.shape[0],rows)
+    vec[0:1,:]=jnp.sum(gacc[...],axis=0,keepdims=True)
+    vec[1:2,:]=jnp.sum(sacc[...],axis=0,keepdims=True)
+
+
+def ordered(kernel, token, args, in_specs, out_specs, out_shape, grid, flops, scratch=(), info=None, copied=0):
+    if info is None:
+        info = jnp.zeros((1,), jnp.int32)
+    inputs, outputs = len(args), len(out_shape)
+
+    def body(info_ref, *refs):
+        token_ref = refs[inputs + 1 + outputs]
+
+        @pl.when(functools.reduce(jnp.logical_and, [pl.program_id(i) == 0 for i in range(len(grid))]))
+        def _():
+            token_ref[...] = jnp.zeros_like(token_ref)
+
+        kernel(
+            info_ref,
+            *refs[:inputs],
+            *refs[inputs + 1 : inputs + 1 + outputs],
+            *refs[inputs + 2 + outputs :],
+        )
+
+    moved = sum(math.prod(a.shape) * a.dtype.itemsize for a in (*args, *out_shape))
+    *results, token = pl.pallas_call(
+        body,
+        grid_spec=pltpu.PrefetchScalarGridSpec(
+            num_scalar_prefetch=1,
+            grid=grid,
+            in_specs=[*in_specs, pl.BlockSpec(memory_space=pl.ANY)],
+            out_specs=[*out_specs, pl.BlockSpec((8, 128), lambda *_: (0, 0))],
+            scratch_shapes=list(scratch),
+        ),
+        out_shape=[*out_shape, sds((8, 128), f32)],
+        compiler_params=pltpu.CompilerParams(vmem_limit_bytes=48 * 2**20),
+        cost_estimate=pl.CostEstimate(flops=flops, bytes_accessed=moved, transcendentals=0),
+    )(info, *args, token)
+    return (*results, token)
+
+
+def specs(frames, width, tile):
+    whole = pl.BlockSpec((frames, width), lambda j, *_: (0, 0))
+    vector = pl.BlockSpec((1, width), lambda j, *_: (0, 0))
+    column = pl.BlockSpec((width, tile), lambda j, *_: (0, j))
+    row = pl.BlockSpec((tile, width), lambda j, *_: (j, 0))
+    act = pl.BlockSpec((frames, tile), lambda j, *_: (0, j))
+    table = pl.BlockSpec((frames, tile), lambda j, *_: (0, 0))
+    logsum = pl.BlockSpec((8, frames), lambda j, *_: (j, 0))
+    return whole, vector, column, row, act, table, logsum
+
+
+def added(acc, term, result):
+    step = pl.program_id(0)
+
+    @pl.when(step == 0)
+    def _():
+        acc[...] = term
+
+    @pl.when(step != 0)
+    def _():
+        acc[...] += term
+
+    @pl.when(step == pl.num_programs(0) - 1)
+    def _():
+        result[...] = acc[...].astype(result.dtype)
+
+
+def self_kernel(info, hid, gain, shift, wq, wk, wv, wo, cos, lower, upper, normed, q, k, v, att, logsum, part, acc, mask):
+    frames = hid.shape[0]
+
+    @pl.when(pl.program_id(0) == 0)
+    def _():
+        def rows(r):
+            normed[r, :] = normed_rows(hid[r, :], gain[...], shift[...]).astype(low)
+
+        over_rows(frames, rows)
+        mask[...] = self_mask(info[0], frames)
+
+    n = normed[...]
+    tables = (cos[...], lower[...], upper[...])
+    q[...] = turn(product_plain(n, wq[...]), *tables).astype(low)
+    k[...] = turn(product_plain(n, wk[...]), *tables).astype(low)
+    v[...] = product_plain(n, wv[...]).astype(low)
+    attended = attend(q[...], k[...], v[...], mask[...], logsum)
+    att[...] = attended
+    added(acc, product_plain(attended, wo[...]), part)
+
+
+def self_forward(token, info, hid, gain, shift, wq, wk, wv, wo, tables, tile=4 * HEAD):
+    frames, width = hid.shape
+    columns = wq.shape[1]
+    whole, vector, column, row, act, table, logsum = specs(frames, width, tile)
+    return ordered(
+        self_kernel,
+        token,
+        (hid, gain, shift, wq, wk, wv, wo, *tables),
+        [whole, vector, vector, column, column, column, row, table, table, table],
+        [whole, act, act, act, act, logsum, whole],
+        [sds((frames, width), low)]
+        + [sds((frames, columns), low)] * 4
+        + [sds((columns // tile * 8, frames), f32), sds((frames, width), low)],
+        (columns // tile,),
+        2 * frames * columns * (4 * width + 8 * frames),
+        [pltpu.VMEM((frames, width), f32), pltpu.VMEM((frames, frames), f32)],
+        info,
+    )
+
+
+def cross_kernel(info, hid, mine, other, gain, shift, cq, ck, cv, co, total, normed, q, att, logsum, part, acc, mask):
+    frames = hid.shape[0]
+
+    @pl.when(pl.program_id(0) == 0)
+    def _():
+        def rows(r):
+            x = hid[r, :] + (mine[r, :].astype(f32) + other[r, :].astype(f32))
+            total[r, :] = x
+            normed[r, :] = normed_rows(x, gain[...], shift[...]).astype(low)
+
+        over_rows(frames, rows)
+        mask[...] = cross_mask(info[0], info[1], info[2], frames, ck.shape[0])
+
+    q[...] = product_plain(normed[...], cq[...]).astype(low)
+    attended = attend(q[...], ck[...], cv[...], mask[...], logsum)
+    att[...] = attended
+    added(acc, product_plain(attended, co[...]), part)
+
+
+def cross_forward(token, info, hid, mine, other, gain, shift, cq, ck, cv, co, tile=4 * HEAD):
+    frames, width = hid.shape
+    columns, keys = cq.shape[1], ck.shape[0]
+    whole, vector, column, row, act, table, logsum = specs(frames, width, tile)
+    key = pl.BlockSpec((keys, tile), lambda j, *_: (0, j))
+    return ordered(
+        cross_kernel,
+        token,
+        (hid, mine, other, gain, shift, cq, ck, cv, co),
+        [whole, whole, whole, vector, vector, column, key, key, row],
+        [whole, whole, act, act, logsum, whole],
+        [
+            sds((frames, width), f32),
+            sds((frames, width), low),
+            sds((frames, columns), low),
+            sds((frames, columns), low),
+            sds((columns // tile * 8, frames), f32),
+            sds((frames, width), low),
+        ],
+        (columns // tile,),
+        2 * frames * columns * (2 * width + 8 * keys),
+        [pltpu.VMEM((frames, width), f32), pltpu.VMEM((keys, frames), f32)],
+        info,
+    )
+
+
+def norm_kernel(_, hid, mine, other, gain, shift, total, normed):
+    def rows(r):
+        x = hid[r, :] + (mine[r, :].astype(f32) + other[r, :].astype(f32))
+        total[r, :] = x
+        normed[r, :] = normed_rows(x, gain[...], shift[...]).astype(low)
+
+    over_rows(hid.shape[0], rows)
+
+
+def norm_forward(token, hid, mine, other, gain, shift, block=128):
+    frames, width = hid.shape
+    rows = pl.BlockSpec((block, width), lambda j, *_: (j, 0))
+    vector = pl.BlockSpec((1, width), lambda j, *_: (0, 0))
+    return ordered(
+        norm_kernel,
+        token,
+        (hid, mine, other, gain, shift),
+        [rows, rows, rows, vector, vector],
+        [rows, rows],
+        [sds((frames, width), f32), sds((frames, width), low)],
+        (frames // block,),
+        10 * frames * width,
+    )
+
+
+def cross_back_kernel(info, x, mine, other, above, gain, co, q, ck, cv, logsum, cq, total, total_low, vectors, dq, dk, dv, part, acc, mask, gain_acc, shift_acc):
+    @pl.when(pl.program_id(0) == 0)
+    def _():
+        norm_back_all(x, mine, other, above, gain, total, total_low, vectors, gain_acc, shift_acc)
+        mask[...] = cross_mask(info[0], info[1], info[2], x.shape[0], ck.shape[0])
+
+    g = product_with_rows(total_low[...], co[...]).astype(low)
+    a, b, c = attend_back(q[...], ck[...], cv[...], g, mask[...], logsum[...])
+    a = a.astype(low)
+    dq[...] = a
+    dk[...] = b.astype(low)
+    dv[...] = c.astype(low)
+    added(acc, product_with_rows(a, cq[...]), part)
+
+
+def cross_backward(token, info, x, mine, other, above, gain, co, q, ck, cv, logsums, cq, tile=4 * HEAD):
+    frames, width = x.shape
+    columns, keys = cq.shape[1], ck.shape[0]
+    whole, vector, column, row, act, table, logsum = specs(frames, width, tile)
+    key = pl.BlockSpec((keys, tile), lambda j, *_: (0, j))
+    two = pl.BlockSpec((2, width), lambda j, *_: (0, 0))
+    return ordered(
+        cross_back_kernel,
+        token,
+        (x, mine, other, above, gain, co, q, ck, cv, logsums, cq),
+        [whole, whole, whole, whole, vector, row, act, key, key, logsum, column],
+        [whole, whole, two, act, key, key, whole],
+        [
+            sds((frames, width), f32),
+            sds((frames, width), low),
+            sds((2, width), f32),
+            sds((frames, columns), low),
+            sds((keys, columns), low),
+            sds((keys, columns), low),
+            sds((frames, width), low),
+        ],
+        (columns // tile,),
+        2 * frames * columns * (2 * width + 20 * keys),
+        [
+            pltpu.VMEM((frames, width), f32),
+            pltpu.VMEM((keys, frames), f32),
+            pltpu.VMEM((8, width), f32),
+            pltpu.VMEM((8, width), f32),
+        ],
+        info,
+    )
+
+
+def self_back_kernel(info, x, mine, other, above, gain, wo, q, k, v, logsum, wq, wk, wv, cos, lower, upper, total, total_low, vectors, grads, part, acc, mask, gain_acc, shift_acc):
+    frames = x.shape[0]
+
+    @pl.when(pl.program_id(0) == 0)
+    def _():
+        norm_back_all(x, mine, other, above, gain, total, total_low, vectors, gain_acc, shift_acc)
+        mask[...] = self_mask(info[0], frames)
+
+    g = product_with_rows(total_low[...], wo[...]).astype(low)
+    a, b, c = attend_back(q[...], k[...], v[...], g, mask[...], logsum[...])
+    tables = (cos[...], lower[...], upper[...])
+    a = turn_back(a, *tables).astype(low)
+    b = turn_back(b, *tables).astype(low)
+    c = c.astype(low)
+    for index, values in enumerate((a, b, c)):
+        turned = values.T
+        for quarter in range(PLANE):
+            grads[quarter, index] = turned[quarter * HEAD : (quarter + 1) * HEAD]
+    added(
+        acc,
+        product_with_rows(a, wq[...]) + product_with_rows(b, wk[...]) + product_with_rows(c, wv[...]),
+        part,
+    )
+
+
+def self_backward(token, info, x, mine, other, above, gain, wo, q, k, v, logsums, wq, wk, wv, tables, tile=4 * HEAD):
+    frames, width = x.shape
+    columns = wq.shape[1]
+    whole, vector, column, row, act, table, logsum = specs(frames, width, tile)
+    two = pl.BlockSpec((2, width), lambda j, *_: (0, 0))
+    heads = pl.BlockSpec((PLANE, 3, HEAD, frames), lambda j, *_: (0, 0, j, 0))
+    return ordered(
+        self_back_kernel,
+        token,
+        (x, mine, other, above, gain, wo, q, k, v, logsums, wq, wk, wv, *tables),
+        [whole, whole, whole, whole, vector, row, act, act, act, logsum, column, column, column, table, table, table],
+        [whole, whole, two, heads, whole],
+        [
+            sds((frames, width), f32),
+            sds((frames, width), low),
+            sds((2, width), f32),
+            sds((PLANE, 3, columns // PLANE, frames), low),
+            sds((frames, width), low),
+        ],
+        (columns // tile,),
+        2 * frames * columns * (4 * width + 20 * frames),
+        [
+            pltpu.VMEM((frames, width), f32),
+            pltpu.VMEM((frames, frames), f32),
+            pltpu.VMEM((8, width), f32),
+            pltpu.VMEM((8, width), f32),
+        ],
+        info,
+    )
+
+
+def last_kernel(_, x, mine, other, above, gain, total, vectors, gain_acc, shift_acc):
+    step = pl.program_id(0)
+
+    @pl.when(step == 0)
+    def _():
+        gain_acc[...] = jnp.zeros_like(gain_acc)
+        shift_acc[...] = jnp.zeros_like(shift_acc)
+
+    def rows(r):
+        e = mine[r, :].astype(f32) + other[r, :].astype(f32)
+        total[r, :] = norm_back_rows(x[r, :], e, gain[...], above[r, :], gain_acc, shift_acc)
+
+    over_rows(x.shape[0], rows)
+
+    @pl.when(step == pl.num_programs(0) - 1)
+    def _():
+        vectors[0:1, :] = jnp.sum(gain_acc[...], axis=0, keepdims=True)
+        vectors[1:2, :] = jnp.sum(shift_acc[...], axis=0, keepdims=True)
+
+
+def last_backward(token, x, mine, other, above, gain, block=128):
+    frames, width = x.shape
+    rows = pl.BlockSpec((block, width), lambda j, *_: (j, 0))
+    vector = pl.BlockSpec((1, width), lambda j, *_: (0, 0))
+    two = pl.BlockSpec((2, width), lambda j, *_: (0, 0))
+    return ordered(
+        last_kernel,
+        token,
+        (x, mine, other, above, gain),
+        [rows, rows, rows, rows, vector],
+        [rows, two],
+        [sds((frames, width), f32), sds((2, width), f32)],
+        (frames // block,),
+        20 * frames * width,
+        [pltpu.VMEM((8, width), f32), pltpu.VMEM((8, width), f32)],
+    )
+
+
+def pack_kernel(_, values, copies):
+    copies[...] = values[...]
+
+
+def packed(token, values, half):
+    frames, width = values.shape
+    return ordered(
+        pack_kernel,
+        token,
+        (values,),
+        [pl.BlockSpec((frames // 2, width), lambda j, info: (info[0], 0))],
+        [pl.BlockSpec((frames // 2, width), lambda j, info: (j, 0))],
+        [sds((PLANE * frames // 2, width), low)],
+        (PLANE,),
+        0,
+        info=half,
+    )
+
+
+def ff_kernel(_, in_ref, out_ref, gate_ref, up_ref, down_ref, sum_ref, back_ref, sum_acc, back_acc):
+    normed = in_ref[...]
+    mixed, grad_gate, grad_up = ff_parts(
+        product_plain(normed, gate_ref[...]),
+        product_plain(normed, up_ref[...]),
+        product_with_rows(out_ref[...], down_ref[...]),
+    )
+    added(sum_acc, product_plain(mixed, down_ref[...]), sum_ref)
+    added(
+        back_acc,
+        product_with_rows(grad_gate, gate_ref[...]) + product_with_rows(grad_up, up_ref[...]),
+        back_ref,
+    )
+
+
+def ff_both(token, normed, grad_out, w_gate, w_up, w_down, tile=512):
+    frames, width = normed.shape
+    units = w_gate.shape[1]
+    whole, _, column, row, *_ = specs(frames, width, tile)
+    return ordered(
+        ff_kernel,
+        token,
+        (normed, grad_out, w_gate, w_up, w_down),
+        [whole, whole, column, column, row],
+        [whole, whole],
+        [sds((frames, width), low)] * 2,
+        (units // tile,),
+        12 * frames * width * units,
+        [pltpu.VMEM((frames, width), f32)] * 2,
+    )
+
+
+def share_kernel(info, in_mine, in_other, out_mine, out_other, gate_ref, up_ref, down_ref, send_ref, keep_ref, acc):
+    step = pl.program_id(0)
+    normed = jnp.concatenate([in_mine[...], in_other[...]], axis=0)
+    grad_out = jnp.concatenate([out_mine[...], out_other[...]], axis=0)
+    mixed, grad_gate, grad_up = ff_parts(
+        product_plain(normed, gate_ref[...]),
+        product_plain(normed, up_ref[...]),
+        product_with_rows(grad_out, down_ref[...]),
+    )
+    fresh = (
+        product_over_rows(grad_out, mixed),
+        product_over_rows(normed, grad_gate),
+        product_over_rows(normed, grad_up),
+    )
+    for index, term in enumerate(fresh):
+
+        @pl.when(step == 0)
+        def _():
+            acc[index] = term
+
+        @pl.when(step != 0)
+        def _():
+            acc[index] += term
+
+    @pl.when(step == pl.num_programs(0) - 1)
+    def _():
+        rows = send_ref.shape[1] // 3
+        for pair in range(2):
+            for index in range(3):
+                for ref, parity in ((send_ref, 1 - info[1]), (keep_ref, info[1])):
+                    start = pl.multiple_of((2 * pair + parity) * rows, rows)
+                    ref[pair, index * rows : (index + 1) * rows] = acc[
+                        index, pl.ds(start, rows), :
+                    ].astype(ref.dtype)
+
+
+def ff_share(token, info, normed, grad_out, w_gate, w_up, w_down, tile):
+    frames, width = normed[0].shape
+    chunk = frames // PLANE
+    rows = pl.BlockSpec((chunk, width), lambda j, info: (j, 0))
+    column = pl.BlockSpec((width, tile), lambda j, info: (0, info[0]))
+    half = (LEVELS // 2, 3 * width // LEVELS, tile)
+    return ordered(
+        share_kernel,
+        token,
+        (*normed, *grad_out, w_gate, w_up, w_down),
+        [rows] * 4 + [column, column, pl.BlockSpec((tile, width), lambda j, info: (info[0], 0))],
+        [pl.BlockSpec(half, lambda j, info: (0, 0, 0))] * 2,
+        [sds(half, low)] * 2,
+        (PLANE,),
+        24 * frames * width * tile,
+        [pltpu.VMEM((3, width, tile), f32)],
+        info,
+    )
+
+
+def weight_kernel(plan, sides_count, _, *refs):
+    sides, columns = refs[:sides_count], refs[sides_count : sides_count + len(plan)]
+    out = refs[sides_count + len(plan)]
+    turned = refs[sides_count + len(plan) + 1 :]
+
+    @pl.when(pl.program_id(0) == 0)
+    def _():
+        for side, ref in zip(sides, turned):
+            ref[...] = side[...].T
+
+    for (which, first), column in zip(plan, columns):
+        product = product_plain(turned[which][...], column[...]).astype(low)
+        rows = product.shape[0] // (PLANE * LEVELS)
+        product = product.reshape(LEVELS, PLANE, rows, product.shape[1])
+        for owner in range(PLANE):
+            out[owner, :, first : first + rows, :] = product[:, owner]
+
+
+def weight_products(token, sides, plan, columns, tile=256):
+    width = columns[0].shape[1]
+    rows = sum(sides[which].shape[1] for which, _ in plan) // (PLANE * LEVELS)
+    return ordered(
+        functools.partial(weight_kernel, plan, len(sides)),
+        token,
+        (*sides, *columns),
+        [pl.BlockSpec(side.shape, lambda j, *_: (0, 0)) for side in sides]
+        + [pl.BlockSpec((column.shape[0], tile), lambda j, *_: (0, j)) for column in columns],
+        [pl.BlockSpec((PLANE, LEVELS, rows, tile), lambda j, *_: (0, 0, 0, j))],
+        [sds((PLANE, LEVELS, rows, width), low)],
+        (width // tile,),
+        sum(2 * sides[w].shape[0] * sides[w].shape[1] * width for w, _ in plan),
+        [pltpu.VMEM((side.shape[1], side.shape[0]), low) for side in sides],
+    )
+
+
+def plane_sum_kernel(info, got, send, keep):
+    for ref, parity in ((send, 1 - info[0]), (keep, info[0])):
+        total = got[0, 0, parity].astype(f32)
+        for source in range(1, PLANE):
+            total = total + got[source, 0, parity].astype(f32)
+        ref[0] = total.astype(low)
+
+
+def plane_sum(token, got, parity):
+    rows, width = got.shape[2:]
+    out = pl.BlockSpec((1, rows, width), lambda j, *_: (j, 0, 0))
+    return ordered(
+        plane_sum_kernel,
+        token,
+        (got.reshape(PLANE, 2, 2, rows, width),),
+        [pl.BlockSpec((PLANE, 1, 2, rows, width), lambda j, *_: (0, j, 0, 0, 0))],
+        [out, out],
+        [sds((2, rows, width), low)] * 2,
+        (2,),
+        0,
+        info=parity,
+    )
+
+
+def level_sum_kernel(_, keep_pass, got_pass, keep_own, got_own, passed, own):
+    passed[...] = (keep_pass[0].astype(f32) + got_pass[0].astype(f32)).astype(low)
+    own[...] = keep_own[0].astype(f32) + got_own[0].astype(f32)
+
+
+def level_sum(token, keep, got, upper):
+    rows, width = keep.shape[1:]
+    block = rows // 2 if rows % 32 == 0 else rows
+    off = pl.BlockSpec((1, block, width), lambda j, info: (1 - info[0], j, 0))
+    own = pl.BlockSpec((1, block, width), lambda j, info: (info[0], j, 0))
+    out = pl.BlockSpec((block, width), lambda j, info: (j, 0))
+    return ordered(
+        level_sum_kernel,
+        token,
+        (keep, got, keep, got),
+        [off, off, own, own],
+        [out, out],
+        [sds((rows, width), low), sds((rows, width), f32)],
+        (rows // block,),
+        0,
+        info=upper,
+    )
+
+
+def head_kernel(info, grads_mine, grads_other, in_mine, in_other, send, keep, acc):
+    step = pl.program_id(0)
+    rows = acc.shape[0]
+    term = product_plain(grads_mine[0].reshape(rows, -1), in_mine[...]) + product_plain(
+        grads_other[0].reshape(rows, -1), in_other[...]
+    )
+
+    @pl.when(step == 0)
+    def _():
+        acc[...] = term
+
+    @pl.when(step != 0)
+    def _():
+        acc[...] += term
+
+    @pl.when(step == pl.num_programs(0) - 1)
+    def _():
+        width = send.shape[2]
+        for level in range(LEVELS):
+            for ref, parity in ((send, 1 - info[1]), (keep, info[1])):
+
+                @pl.when(parity == level % 2)
+                def _():
+                    ref[level // 2] = acc[:, level * width : (level + 1) * width].astype(low)
+
+
+def head_products(token, info, grads, normed):
+    _, three, features, frames = grads.shape
+    width = normed[0].shape[1]
+    chunk = normed[0].shape[0] // PLANE
+    rows = pl.BlockSpec((chunk, width), lambda j, info: (j, 0))
+    half = (LEVELS // 2, three * features, width // LEVELS)
+    return ordered(
+        head_kernel,
+        token,
+        (grads, grads, *normed),
+        [
+            pl.BlockSpec((1, three, features, chunk), lambda j, info: (j, 0, 0, info[0])),
+            pl.BlockSpec((1, three, features, chunk), lambda j, info: (j, 0, 0, 1 - info[0])),
+            rows,
+            rows,
+        ],
+        [pl.BlockSpec(half, lambda j, info: (0, 0, 0))] * 2,
+        [sds(half, low)] * 2,
+        (PLANE,),
+        2 * three * features * PLANE * frames * width,
+        [pltpu.VMEM((three * features, width), f32)],
+        info,
+    )
+
+
+def on_plane(
     hidden_in,
     out_grad,
     prompt_states,
@@ -258,7 +877,204 @@
     w_up,
     w_down,
 ):
-    low = jnp.bfloat16
+    frames, width = hidden_in.shape
+    plane, level = lax.axis_index("dp") % PLANE, lax.axis_index("dp") // PLANE
+    info = jnp.concatenate([row_split, prompt_len])
+    positions = jnp.arange(frames, dtype=jnp.int32)
+    row_ids = (positions >= row_split[0]).astype(jnp.int32)
+    tables = rotary_tables((positions - row_ids * row_split[0]).astype(f32), 4 * HEAD)
+    gain_attn, bias_attn, gain_cross, bias_cross, gain_ff, bias_ff = (
+        vector[None] for vector in (gain_attn, bias_attn, gain_cross, bias_cross, gain_ff, bias_ff)
+    )
+
+    zero = jnp.zeros((1,), jnp.int32)
+    half = zero + lax.axis_index("tensor")
+    parity, upper = zero + level % 2, zero + level // 2
+    chips = [[PLANE * z + p for p in range(PLANE)] for z in range(LEVELS)]
+
+    def swapped(part):
+        return lax.ppermute(part, "tensor", [(0, 1), (1, 0)])
+
+    def in_plane(values):
+        shape = values.shape
+        return lax.all_to_all(
+            values, "dp", 0, 0, axis_index_groups=chips, tiled=True
+        ).reshape(shape)
+
+    def level_swap(values, mask):
+        return lax.ppermute(values, "dp", pairs(mask))
+
+    token = jnp.zeros((8, 128), f32)
+    context = prompt_states.reshape(2 * PROMPT, prompt_states.shape[2])
+    cross_key = product_plain(context, c_key).astype(low)
+    cross_value = product_plain(context, c_value).astype(low)
+    grad_ff_out = out_grad.astype(low)
+    copies, token = packed(token, grad_ff_out, half)
+    frames_out = in_plane(copies)
+    frames_out = (frames_out, swapped(frames_out))
+    input_one, query, key, value, attended_one, logsum_one, part, token = self_forward(
+        token, info, hidden_in, gain_attn, bias_attn, w_query, w_key, w_value, w_out, tables
+    )
+    resid_one, input_two, cross_query, attended_two, logsum_two, part, token = cross_forward(
+        token,
+        info,
+        hidden_in,
+        part,
+        swapped(part),
+        gain_cross,
+        bias_cross,
+        c_query,
+        cross_key,
+        cross_value,
+        c_out,
+    )
+    resid_two, input_three, token = norm_forward(
+        token, resid_one, part, swapped(part), gain_ff, bias_ff
+    )
+    copies, token = packed(token, input_three, half)
+    frames_in = in_plane(copies)
+    frames_in = (frames_in, swapped(frames_in))
+    sum_part, back_part, token = ff_both(token, input_three, grad_ff_out, w_gate, w_up, w_down)
+    result = resid_two + add_low(sum_part, swapped(sum_part))
+    grad_two, grad_cross_out, vectors_ff, query_grad, key_grad, value_grad, part, token = cross_backward(
+        token,
+        info,
+        resid_two,
+        back_part,
+        swapped(back_part),
+        out_grad,
+        gain_ff,
+        c_out,
+        cross_query,
+        cross_key,
+        cross_value,
+        logsum_two,
+        c_query,
+    )
+    back_swapped = swapped(part)
+
+    tile = 256
+    tiles = w_gate.shape[1] // (PLANE * tile)
+
+    def share(token, index):
+        number = jnp.concatenate([zero + plane * tiles + index, parity])
+        return ff_share(token, number, frames_in, frames_out, w_gate, w_up, w_down, tile)
+
+    send_a, keep_a, token = share(token, 0)
+    got_a = level_swap(send_a, PLANE)
+    copies, token = packed(token, input_one, half)
+    frames_one = in_plane(copies)
+    frames_one = (frames_one, swapped(frames_one))
+    r, c = width // 16, context.shape[1] // 16
+    products, token = weight_products(
+        token,
+        [grad_cross_out, input_two, context],
+        [(0, 0), (1, r), (2, 2 * r), (2, 2 * r + c)],
+        [attended_two, query_grad, key_grad, value_grad],
+    )
+    got_cross = in_plane(products)
+    send_b, keep_b, token = share(token, 1)
+    got_b = level_swap(send_b, PLANE)
+    pass_a, own_a, token = level_sum(token, keep_a, got_a, upper)
+    last_a = level_swap(pass_a, 2 * PLANE)
+    grad_one, grad_self_out, vectors_cross, grads, part, token = self_backward(
+        token,
+        info,
+        resid_one,
+        part,
+        back_swapped,
+        grad_two,
+        gain_cross,
+        w_out,
+        query,
+        key,
+        value,
+        logsum_one,
+        w_query,
+        w_key,
+        w_value,
+        tables,
+    )
+    got_heads = in_plane(grads)
+    part_swapped = swapped(part)
+    pass_b, own_b, token = level_sum(token, keep_b, got_b, upper)
+    last_b = level_swap(pass_b, 2 * PLANE)
+    send_c, keep_c, token = share(token, 2)
+    got_c = level_swap(send_c, PLANE)
+    products, token = weight_products(token, [grad_self_out], [(0, 0)], [attended_one])
+    got_out = in_plane(products)
+    grad_hidden, vectors_attn, token = last_backward(
+        token, hidden_in, part, part_swapped, grad_one, gain_attn
+    )
+    vectors = vector_sum(jnp.concatenate([vectors_attn, vectors_cross, vectors_ff]))
+    send_x, keep_x, token = plane_sum(token, got_cross, parity)
+    got_x = level_swap(send_x, PLANE)
+    pass_c, own_c, token = level_sum(token, keep_c, got_c, upper)
+    last_c = level_swap(pass_c, 2 * PLANE)
+    send_h, keep_h, token = head_products(
+        token, jnp.concatenate([half, parity]), got_heads, frames_one
+    )
+    got_h = level_swap(send_h, PLANE)
+    pass_x, own_x, token = level_sum(token, keep_x, got_x, upper)
+    last_x = level_swap(pass_x, 2 * PLANE)
+    send_o, keep_o, token = plane_sum(token, got_out, parity)
+    got_o = level_swap(send_o, PLANE)
+    pass_h, own_h, token = level_sum(token, keep_h, got_h, upper)
+    last_h = level_swap(pass_h, 2 * PLANE)
+    pass_o, own_o, token = level_sum(token, keep_o, got_o, upper)
+    last_o = level_swap(pass_o, 2 * PLANE)
+
+    units = jnp.stack([add_low(own_a, last_a), add_low(own_b, last_b), add_low(own_c, last_c)])
+    units = units.astype(low).reshape(tiles, 3, PLANE, r, tile).transpose(2, 1, 3, 0, 4)
+    units = in_plane(units.reshape(PLANE, 3, r, tiles * tile))
+    units = units.transpose(1, 2, 0, 3).reshape(3, r, w_gate.shape[1]).astype(f32)
+    cross = add_low(own_x, last_x)
+    heads = add_low(own_h, last_h).astype(low).T
+    heads = in_plane(heads.reshape(PLANE, r, heads.shape[1]))
+    heads = heads.reshape(PLANE, r, 3, w_query.shape[1] // (PLANE * HEAD), HEAD)
+    heads = heads.transpose(2, 1, 3, 0, 4).reshape(3, r, w_query.shape[1]).astype(f32)
+    return (
+        result,
+        grad_hidden,
+        *(vectors[index] for index in range(6)),
+        heads[0],
+        heads[1],
+        heads[2],
+        add_low(own_o, last_o).T,
+        cross[r : 2 * r],
+        cross[2 * r : 2 * r + c],
+        cross[2 * r + c :],
+        cross[:r].T,
+        units[1],
+        units[2],
+        units[0].T,
+    )
+
+
+def on_any(
+    hidden_in,
+    out_grad,
+    prompt_states,
+    row_split,
+    prompt_len,
+    gain_attn,
+    bias_attn,
+    gain_cross,
+    bias_cross,
+    gain_ff,
+    bias_ff,
+    w_query,
+    w_key,
+    w_value,
+    w_out,
+    c_query,
+    c_key,
+    c_value,
+    c_out,
+    w_gate,
+    w_up,
+    w_down,
+):
     frame_count = hidden_in.shape[0]
     positions = jnp.arange(frame_count, dtype=jnp.int32)
     split_here = row_split[0]
@@ -298,14 +1114,14 @@
     result = resid_two + swap_sum(product_plain(mixed_low, w_down))
 
     grad_ff_out = out_grad.astype(low)
-    grad_w_down = weight_sum(grad_ff_out, mixed_low, True)
+    grad_w_down = generic_sum(grad_ff_out, mixed_low).T
     grad_mixed = product_with_rows(grad_ff_out, w_down)
     grad_gate = (
         grad_mixed * up_pre * sigmoid_gate * (1.0 + gate_pre * (1.0 - sigmoid_gate))
     ).astype(low)
     grad_up = (grad_mixed * gate_pre * sigmoid_gate).astype(low)
-    grad_w_gate = weight_sum(input_three, grad_gate)
-    grad_w_up = weight_sum(input_three, grad_up)
+    grad_w_gate = generic_sum(input_three, grad_gate)
+    grad_w_up = generic_sum(input_three, grad_up)
     normed_grad_three = swap_sum(
         product_with_rows(grad_gate, w_gate) + product_with_rows(grad_up, w_up)
     )
@@ -314,7 +1130,7 @@
     )
     grad_two = out_grad + back_three
     grad_cross_out = grad_two.astype(low)
-    grad_c_out = weight_sum(grad_cross_out, attended_two, True)
+    grad_c_out = generic_sum(grad_cross_out, attended_two).T
     grad_attended_two = product_with_rows(grad_cross_out, c_out).astype(low)
     cross_query_grad, cross_key_grad, cross_value_grad = attend_backward(
         cross_query,
@@ -327,16 +1143,16 @@
     cross_query_grad = cross_query_grad.astype(low)
     cross_key_grad = cross_key_grad.astype(low)
     cross_value_grad = cross_value_grad.astype(low)
-    grad_c_query = weight_sum(input_two, cross_query_grad)
-    grad_c_key = weight_sum(context_flat, cross_key_grad)
-    grad_c_value = weight_sum(context_flat, cross_value_grad)
+    grad_c_query = generic_sum(input_two, cross_query_grad)
+    grad_c_key = generic_sum(context_flat, cross_key_grad)
+    grad_c_value = generic_sum(context_flat, cross_value_grad)
     normed_grad_two = swap_sum(product_with_rows(cross_query_grad, c_query))
     back_two, grad_gain_cross, grad_bias_cross = normalize_back(
         normed_grad_two, scaled_two, inverse_two, gain_cross
     )
     grad_one = grad_two + back_two
     grad_self_out = grad_one.astype(low)
-    grad_w_out = weight_sum(grad_self_out, attended_one, True)
+    grad_w_out = generic_sum(grad_self_out, attended_one).T
     grad_attended_one = product_with_rows(grad_self_out, w_out).astype(low)
     query_grad, key_grad, value_grad = attend_backward(
         query_one, heads_of(key_one), heads_of(value_one), self_ok, grad_attended_one, logsum_one
@@ -344,9 +1160,9 @@
     query_grad = rotate_back(query_grad, tables).astype(low)
     key_grad = rotate_back(key_grad, tables).astype(low)
     value_grad = value_grad.astype(low)
-    grad_w_query = weight_sum(input_one, query_grad)
-    grad_w_key = weight_sum(input_one, key_grad)
-    grad_w_value = weight_sum(input_one, value_grad)
+    grad_w_query = generic_sum(input_one, query_grad)
+    grad_w_key = generic_sum(input_one, key_grad)
+    grad_w_value = generic_sum(input_one, value_grad)
     normed_grad_one = swap_sum(
         product_with_rows(query_grad, w_query)
         + product_with_rows(key_grad, w_key)
@@ -437,6 +1253,7 @@
         P("dp", "tensor"),
         P("tensor", "dp"),
     )
+    known = mesh.shape["dp"] == PLANE * LEVELS and mesh.shape["tensor"] == 2
     return jax.shard_map(
-        on_device, mesh=mesh, in_specs=in_specs, out_specs=out_specs, check_vma=False
-    )
+        on_plane if known else on_any, mesh=mesh, in_specs=in_specs, out_specs=out_specs, check_vma=False
+    )

time: 1020 us -> 583 us (0.57)
  starting transfers between devices: 284 us -> 54.4 us
  Pallas kernels: 0 us -> 222 us
  matrix products: 204 us -> 0.96 us
  waiting for transfers between devices: 290 us -> 167 us
  other arithmetic: 131 us -> 25.7 us
  blocking collectives: 0 us -> 33 us
  local copies, waits for them, and re-layouts: 97.8 us -> 69.1 us
    ppermute x138 -> x21, starting transfers between devices: 276 us -> 18 us  [the longest x12 15.9 us: level_swap(): return lax.ppermute(values, 'dp', pairs(mask))]
    ppermute x138 -> x21, waiting for transfers between devices: 285 us -> 57.1 us  [the longest x12 50.7 us: level_swap(): return lax.ppermute(values, 'dp', pairs(mask))]
    pallas_call x0 -> x24, Pallas kernels: none -> 222 us  [ordered(): pl.pallas_call(body, grid_spec=pltpu.PrefetchScalarGridSpec(num_scalar_pr...]
    dot_general x55 -> x2, matrix products: 108 us -> 0.96 us  [product_plain(): return jnp.dot(left_side, right_side, preferred_element_type=jnp.float32)]
    dot_general x21 -> x0, matrix products: 96.3 us -> none  [the longest x9 52.7 us: product_with_rows(): lax.dot_general(left_side, right_side, (((1,), (1,)), ((), ())), preferre...]
    all_to_all x0 -> x7, waiting for transfers between devices: none -> 61.7 us  [in_plane(): lax.all_to_all(values, 'dp', 0, 0, axis_index_groups=chips, tiled=True)]
    convert_element_type x73 -> x3, other arithmetic: 54.8 us -> 3.88 us  [the longest x1 2.06 us: on_plane(): grad_ff_out = out_grad.astype(low)]
    ppermute x4, waiting for transfers between devices: 5.03 us -> 48.3 us  [vector_sum(): vectors = vectors + lax.ppermute(vectors, 'dp', pairs(mask))]
  transfers between devices with their start and end apart: 142 -> 32, of which waited for: 63 -> 13; matrix products, arithmetic and copies ran while one was open for 25% -> 6% of each run, Pallas kernels for 0% -> 35%
where the time goes in v4:
time: 583 us; the launch traced here: 575 us
  Pallas kernels  222 us (38%)
  waiting for transfers between devices  167 us (29%)
  local copies, waits for them, and re-layouts  69.1 us (12%)
  starting transfers between devices  54.4 us (9%)
  blocking collectives  33 us (6%)
  other arithmetic  25.7 us (4%)
    pallas_call x24, Pallas kernels, ordered(): pl.pallas_call(body, grid_spec=pltpu.PrefetchScalarGridSpec(num_scalar_pr...  222 us
    all_to_all x7, waiting for transfers between devices, in_plane(): lax.all_to_all(values, 'dp', 0, 0, axis_index_groups=chips, tiled=True)  61.7 us
    unnamed x202, local copies, waits for them, and re-layouts  50.9 us
    ppermute x12, waiting for transfers between devices, level_swap(): return lax.ppermute(values, 'dp', pairs(mask))  50.7 us
    ppermute x4, waiting for transfers between devices, vector_sum(): vectors = vectors + lax.ppermute(vectors, 'dp', pairs(mask))  48.3 us
    all_to_all x1, blocking collectives, in_plane(): lax.all_to_all(values, 'dp', 0, 0, axis_index_groups=chips, tiled=True)  33 us
    all_to_all x7, starting transfers between devices, in_plane(): lax.all_to_all(values, 'dp', 0, 0, axis_index_groups=chips, tiled=True)  31.8 us
    ppermute x12, starting transfers between devices, level_swap(): return lax.ppermute(values, 'dp', pairs(mask))  15.9 us
  transfers between devices with their start and end apart: 32, of which 13 were waited for; matrix products, arithmetic and copies ran while one was open for 6% of the time, Pallas kernels for 35%

profile of v4, /device:TPU:0, one launch (start us, length us, event | category | flops | bytes accessed | tf_op | source)
XLA Modules:
  0.0 575.0 jit_solution(16058411151727635032)
XLA Ops:
  3.6 2.1 convert_element_type.72.refs_0_.refs_1_
  6.0 2.0 fusion
  8.0 21.0 %shard_map.358 = (bf16[512,1536]{1,0:T(8,128)(2,1)}, bf16[512,768]{1,0:T(8,128)(2,1)S(1)}, bf16[512,768]{1,0:T(8,128)(2,1)S(1)}, bf16[512,768]{1,0:T(8,128)(2,1)...) custom-call(s32[3]{0:T(128)S(1)} %pad_add_fusion.info_ref, ...), custom_call_target="tpu_custom_call" | custom-call | flops 8053063680 | bytes 20508672 | tf_op jit(solution)/shard_map/pallas_call | solution.py:319
  33.7 5.1 all-to-all-start.1
  40.6 17.1 %shard_map.359 = (f32[512,1536]{1,0:T(8,128)}, bf16[512,1536]{1,0:T(8,128)(2,1)S(1)}, bf16[512,768]{1,0:T(8,128)(2,1)S(1)}, bf16[512,768]{1,0:T(8,128)(2,1)S(1)}...) custom-call(s32[3]{0:T(128)S(1)} %pad_add_fusion.info_ref, f32[512,1536]{1,0:T(8,128)} %refs_0_.5, ...), custom_call_target="tpu_custom_call" | custom-call | flops 4026531840 | bytes 19722240 | tf_op jit(solution)/shard_map/pallas_call | solution.py:319
  60.1 3.1 collective-permute-done.1.refs_2_
  63.2 4.6 shard_map.360
  68.1 1.7 copy-done.11
  71.0 5.6 all-to-all-done.1
  76.6 4.0 all-to-all-start
  80.6 36.3 %all-to-all-done = bf16[4,256,1536]{2,1,0:T(8,128)(2,1)S(1)} async-done(((bf16[4,256,1536]{2,1,0:T(8,128)(2,1)}), bf16[4,256,1536]{2,1,0:T(8,128)(2,1)S(1)}, u32[]{:S(2)}, u32[]{:S(2)}) %all-to-all-start) | async-done | bytes 3145760 | tf_op jit(solution)/shard_map/all_to_all | solution.py:900
  117.0 1.4 copy-done.19
  118.4 41.1 %shard_map.362 = (bf16[512,1536]{1,0:T(8,128)(2,1)S(1)}, bf16[512,1536]{1,0:T(8,128)(2,1)}, f32[8,128]{1,0:T(8,128)S(1)}) custom-call(s32[1]{0:T(128)} %constant.81.clone.1.info_ref, bf16[512,1536]{1,0:T(8,128)(2,1)S(1)} %copy-done.19, bf16[512,1536]{1,0:T(8,128)(2,1)} %copy-done.2, bf16[1536,3072]{1,0:T(8,128)(2,1)} %refs_4_.9, ...), custom_call_target="tpu_custom_call" | custom-call | flops 28991029248 | bytes 34603008 | tf_op jit(solution)/shard_map/pallas_call | solution.py:319
  161.9 3.2 collective-permute-done.3.refs_2_
  171.1 21.7 %shard_map.363 = (f32[512,1536]{1,0:T(8,128)}, bf16[512,1536]{1,0:T(8,128)(2,1)S(1)}, f32[2,1536]{1,0:T(2,128)S(1)}, bf16[512,768]{1,0:T(8,128)(2,1)S(1)}, bf16[...) custom-call(s32[3]{0:T(128)S(1)} %copy-done.57, ...), custom_call_target="tpu_custom_call" | custom-call | flops 6442450944 | bytes 23660544 | tf_op jit(solution)/shard_map/pallas_call | solution.py:319
  196.7 17.7 %shard_map.364 = (bf16[2,1152,256]{2,1,0:T(8,128)(2,1)}, bf16[2,1152,256]{2,1,0:T(8,128)(2,1)S(1)}, f32[8,128]{1,0:T(8,128)S(1)}) custom-call(s32[2]{0:T(128)S(1)} %pad_add_fusion.1.info_ref, bf16[1024,1536]{1,0:T(8,128)(2,1)S(1)} %bitcast.63, bf16[1024,1536]{1,0:T(8,128)(2,1)} %collective-permute-done.5.refs_1_, bf16[1024,1536]{1,0:T(8,128)(2,1)} %bitcast.9.refs_2_, ...), custom_call_target="tpu_custom_call" | custom-call | flops 9663676416 | bytes 43253760 | tf_op jit(solution)/shard_map/pallas_call | solution.py:319
  215.3 1.6 collective-permute-start.7
  217.8 1.6 copy-done.10
  219.4 4.6 all-to-all-start.3
  224.8 1.4 copy-done.65
  227.3 1.4 copy-done.71
  231.8 6.6 %shard_map.366 = (bf16[4,4,288,768]{3,2,1,0:T(8,128)(2,1)}, f32[8,128]{1,0:T(8,128)S(1)}) custom-call(s32[1]{0:T(128)} %constant.81.clone.1.info_ref, bf16[512,1536]{1,0:T(8,128)(2,1)S(1)} %copy-done.71, bf16[512,1536]{1,0:T(8,128)(2,1)S(1)} %copy-done.65, bf16[256,768]{1,0:T(8,128)(2,1)S(1)} %bitcast.72, bf16[512,768]{1,0:T(8,128)(2,1)S(1)} %copy-done.67, ...), custom_call_target="tpu_custom_call" | custom-call | flops 3019898880 | bytes 12976128 | tf_op jit(solution)/shard_map/pallas_call | solution.py:319
  238.4 16.2 %shard_map.367 = (bf16[2,1152,256]{2,1,0:T(8,128)(2,1)S(1)}, bf16[2,1152,256]{2,1,0:T(8,128)(2,1)S(1)}, f32[8,128]{1,0:T(8,128)S(1)}) custom-call(s32[2]{0:T(128)S(1)} %pad_add_fusion.2.info_ref, bf16[1024,1536]{1,0:T(8,128)(2,1)S(1)} %bitcast.64, bf16[1024,1536]{1,0:T(8,128)(2,1)} %collective-permute-done.5.refs_1_, bf16[1024,1536]{1,0:T(8,128)(2,1)} %bitcast.9.refs_2_, ...), custom_call_target="tpu_custom_call" | custom-call | flops 9663676416 | bytes 43253760 | tf_op jit(solution)/shard_map/pallas_call | solution.py:319
  255.7 2.5 shard_map.368
  259.4 29.3 %shard_map.369 = (f32[512,1536]{1,0:T(8,128)}, bf16[512,1536]{1,0:T(8,128)(2,1)S(1)}, f32[2,1536]{1,0:T(2,128)S(1)}, bf16[4,3,192,512]{3,2,1,0:T(8,128)(2,1)}, b...) custom-call(s32[3]{0:T(128)S(1)} %copy-done.58, f32[512,1536]{1,0:T(8,128)} %get-tuple-element.105.refs_0_, ...), custom_call_target="tpu_custom_call" | custom-call | flops 12884901888 | bytes 31524864 | tf_op jit(solution)/shard_map/pallas_call | solution.py:319
  290.5 33.0 %all_to_all.58.refs_0_.refs_1_ = bf16[4,3,192,512]{3,2,1,0:T(8,128)(2,1)} all-to-all(bf16[4,3,192,512]{3,2,1,0:T(8,128)(2,1)} %get-tuple-element.154), channel_id=1, replica_groups={{0,2,4,6},{8,10,12,14},{16,18,20,22},{24,26,28,30},{1,3,5,7},{9,11,13,1..., dimensions={0} | all-to-all | bytes 4718592 | tf_op jit(solution)/shard_map/all_to_all | solution.py:900
  323.5 5.4 all-to-all-start.4
  329.9 25.5 %collective-permute-done.9.refs_1_.refs_3_ = bf16[2,1152,256]{2,1,0:T(8,128)(2,1)S(1)} collective-permute-done((bf16[2,1152,256]{2,1,0:T(8,128)(2,1)}, bf16[2,1152,256]{2,1,0:T(8,128)(2,1)S(1)}, u32[]{:S(2)}, u32[]{:S(2)}) %collective-permute-start.9) | collective-permute-done | bytes 1179680 | tf_op jit(solution)/shard_map/ppermute | solution.py:905
  355.4 1.3 copy-done.6
  357.0 17.9 %shard_map.371 = (bf16[2,1152,256]{2,1,0:T(8,128)(2,1)}, bf16[2,1152,256]{2,1,0:T(8,128)(2,1)S(1)}, f32[8,128]{1,0:T(8,128)S(1)}) custom-call(s32[2]{0:T(128)S(1)} %pad_add_fusion.3.info_ref, bf16[1024,1536]{1,0:T(8,128)(2,1)S(1)} %bitcast.65, bf16[1024,1536]{1,0:T(8,128)(2,1)} %collective-permute-done.5.refs_1_, bf16[1024,1536]{1,0:T(8,128)(2,1)} %bitcast.9.refs_2_, ...), custom_call_target="tpu_custom_call" | custom-call | flops 9663676416 | bytes 43253760 | tf_op jit(solution)/shard_map/pallas_call | solution.py:319
  376.4 2.4 shard_map.372
  378.9 1.4 copy-done.13
  380.3 6.2 %shard_map.373 = (f32[512,1536]{1,0:T(8,128)}, f32[2,1536]{1,0:T(2,128)S(1)}, f32[8,128]{1,0:T(8,128)S(1)}) custom-call(s32[1]{0:T(128)} %constant.81.clone.1.info_ref, f32[512,1536]{1,0:T(8,128)} %refs_0_.5, bf16[512,1536]{1,0:T(8,128)(2,1)S(1)} %copy-done.16, bf16[512,1536]{1,0:T(8,128)(2,1)S(1)} %collective-permute-done.8.refs_2_, ...), custom_call_target="tpu_custom_call" | custom-call | flops 15728640 | bytes 12601344 | tf_op jit(solution)/shard_map/pallas_call | solution.py:319
  387.1 1.6 collective-permute-start.10
  389.3 2.6 collective-permute-start.22
  391.9 14.6 %all-to-all-done.4 = bf16[4,4,288,768]{3,2,1,0:T(8,128)(2,1)} async-done(((bf16[4,4,288,768]{3,2,1,0:T(8,128)(2,1)}), bf16[4,4,288,768]{3,2,1,0:T(8,128)(2,1)}, u32[]{:S(2)}, u32[]{:S(2)}) %all-to-all-start.4) | async-done | bytes 7077920 | tf_op jit(solution)/shard_map/all_to_all | solution.py:900
  406.5 3.8 all-to-all-start.5
  410.4 2.7 collective-permute-start.23
  413.9 3.6 shard_map.374
  417.6 2.1 collective-permute-start.11
  422.1 9.1 %shard_map.376 = (bf16[2,576,384]{2,1,0:T(8,128)(2,1)}, bf16[2,576,384]{2,1,0:T(8,128)(2,1)S(1)}, f32[8,128]{1,0:T(8,128)S(1)}) custom-call(s32[2]{0:T(128)S(1)} %copy-done.59, bf16[4,3,192,512]{3,2,1,0:T(8,128)(2,1)S(1)} %copy-done.12, bf16[4,3,192,512]{3,2,1,0:T(8,128)(2,1)S(1)} %copy-done.12, bf16[1024,1536]{1,0:T(8,128)(2,1)} %bitcast.17.refs_2_, ...), custom_call_target="tpu_custom_call" | custom-call | flops 3623878656 | bytes 12779520 | tf_op jit(solution)/shard_map/pallas_call | solution.py:319
  431.2 1.6 collective-permute-start.16
  432.8 3.8 add_add_fusion
  436.6 1.3 collective-permute-done.11
  438.5 2.1 add_convert_fusion.2
  440.6 32.8 %collective-permute-done.12 = f32[6,1536]{1,0:T(8,128)S(1)} collective-permute-done((f32[6,1536]{1,0:T(8,128)S(1)}, f32[6,1536]{1,0:T(8,128)S(1)}, u32[]{:S(2)}, u32[]{:S(2)}) %collective-permute-start.12) | collective-permute-done | bytes 36896 | tf_op jit(solution)/shard_map/ppermute | solution.py:168
  474.5 2.4 collective-permute-start.24
  480.1 1.5 shard_map.379
  482.2 1.2 add_convert_fusion.1
  484.5 2.0 copy.56
  486.5 14.2 %collective-permute-done.13 = f32[6,1536]{1,0:T(8,128)} collective-permute-done((f32[6,1536]{1,0:T(8,128)}, f32[6,1536]{1,0:T(8,128)}, u32[]{:S(2)}, u32[]{:S(2)}) %collective-permute-start.13) | collective-permute-done | bytes 36896 | tf_op jit(solution)/shard_map/ppermute | solution.py:168
  501.4 19.2 %collective-permute-done.18 = bf16[576,384]{1,0:T(8,128)(2,1)S(1)} collective-permute-done((bf16[576,384]{1,0:T(8,128)(2,1)S(1)}, bf16[576,384]{1,0:T(8,128)(2,1)S(1)}, u32[]{:S(2)}, u32[]{:S(2)}) %collective-permute-start.18) | collective-permute-done | bytes 442400 | tf_op jit(solution)/shard_map/ppermute | solution.py:905
  521.7 4.1 all-to-all-start.6
  525.9 1.3 add_convert_fusion
  528.4 2.7 collective-permute-start.21
  531.1 5.0 maximum_bitcast_fusion
  536.1 5.6 reshape.123
  541.7 4.8 all-to-all-start.7
  548.0 3.2 collective-permute-done.21
  553.1 2.7 collective-permute-done.20
  557.4 1.3 copy.51
  561.5 5.1 all-to-all-done.7
  566.6 1.8 convert_bitcast_fusion
  569.4 1.2 copy.66
  (278 shorter events, 65.2 us)
Async XLA Ops:
  0.7 38.1 %copy-start = (bf16[768,768]{1,0:T(8,128)(2,1)S(1)}, bf16[768,768]{1,0:T(8,128)(2,1)}, u32[]{:S(2)}) copy-start(bf16[768,768]{1,0:T(8,128)(2,1)} %param.39) | copy-start | bytes 3538948
  2.2 38.4 %copy-start.56 = (s32[3]{0:T(128)}, s32[3]{0:T(128)S(1)}, u32[]{:S(2)}) copy-start(s32[3]{0:T(128)S(1)} %pad_add_fusion.info_ref) | copy-start | bytes 40
  2.9 5.1 copy-start.42
  8.0 21.0 %copy-start.29 = (f32[512,256]{1,0:T(8,128)}, f32[512,256]{1,0:T(8,128)S(1)}, u32[]{:S(2)}) copy-start(f32[512,256]{1,0:T(8,128)S(1)} %get-tuple-element.239.refs_9_.refs_15_) | copy-start | bytes 1572868
  8.0 21.0 %copy-start.31 = (f32[512,256]{1,0:T(8,128)}, f32[512,256]{1,0:T(8,128)S(1)}, u32[]{:S(2)}) copy-start(f32[512,256]{1,0:T(8,128)S(1)} %get-tuple-element.240.refs_8_.refs_14_) | copy-start | bytes 1572868
  8.0 21.0 %copy-start.33 = (f32[512,256]{1,0:T(8,128)}, f32[512,256]{1,0:T(8,128)S(1)}, u32[]{:S(2)}) copy-start(f32[512,256]{1,0:T(8,128)S(1)} %get-tuple-element.241.refs_7_.refs_13_) | copy-start | bytes 1572868
  33.2 7.3 %collective-permute-start = (bf16[512,1536]{1,0:T(8,128)(2,1)}, bf16[512,1536]{1,0:T(8,128)(2,1)}, u32[]{:S(2)}, u32[]{:S(2)}) collective-permute-start(bf16[512,1536]{1,0:T(8,128)(2,1)} %get-tuple-element.103.refs_1_), channel_id=1, source_target_pairs={{0,1},{1,0},{2,3},{3,2},{4,5},{5,4},{6,7},{7,6},{8,9},{9,8},{10,11... | collective-permute-start | bytes 4718600 | tf_op jit(solution)/shard_map/ppermute | solution.py:896
  33.7 5.1 copy-start.20
  33.7 42.9 %all-to-all-start.1 = ((bf16[4,256,1536]{2,1,0:T(8,128)(2,1)}), bf16[4,256,1536]{2,1,0:T(8,128)(2,1)}, u32[]{:S(2)}, u32[]{:S(2)}) async-start(bf16[4,256,1536]{2,1,0:T(8,128)(2,1)} %bitcast.67), calls=%async_computation.1 | async-start | bytes 6291456 | tf_op jit(solution)/shard_map/all_to_all | solution.py:900
  39.5 18.3 %copy-start.35 = (bf16[256,768]{1,0:T(8,128)(2,1)}, bf16[256,768]{1,0:T(8,128)(2,1)S(1)}, u32[]{:S(2)}) copy-start(bf16[256,768]{1,0:T(8,128)(2,1)S(1)} %convolution_convert_fusion.refs_7_.refs_8_) | copy-start | bytes 1179652
  39.5 18.2 %copy-start.46 = (f32[1,1536]{1,0:T(1,128)}, f32[1,1536]{1,0:T(1,128)S(1)}, u32[]{:S(2)}) copy-start(f32[1,1536]{1,0:T(1,128)S(1)} %broadcast_in_dim.49.refs_3_.refs_4_) | copy-start | bytes 18436
  40.6 17.2 %copy-start.37 = (bf16[256,768]{1,0:T(8,128)(2,1)}, bf16[256,768]{1,0:T(8,128)(2,1)S(1)}, u32[]{:S(2)}) copy-start(bf16[256,768]{1,0:T(8,128)(2,1)S(1)} %convolution_convert_fusion.1.refs_6_.refs_7_) | copy-start | bytes 1179652
  40.6 19.4 %copy-start.96 = (f32[1536]{0:T(1024)S(1)}, f32[1536]{0:T(1024)}, u32[]{:S(2)}) copy-start(f32[1536]{0:T(1024)} %param.31) | copy-start | bytes 18436
  40.6 19.4 %copy-start.97 = (f32[1536]{0:T(1024)S(1)}, f32[1536]{0:T(1024)}, u32[]{:S(2)}) copy-start(f32[1536]{0:T(1024)} %param.32) | copy-start | bytes 18436
  59.8 8.0 %copy-start.68 = (bf16[512,768]{1,0:T(8,128)(2,1)}, bf16[512,768]{1,0:T(8,128)(2,1)S(1)}, u32[]{:S(2)}) copy-start(bf16[512,768]{1,0:T(8,128)(2,1)S(1)} %get-tuple-element.114.refs_6_) | copy-start | bytes 2359300
  59.8 8.0 %copy-start.78 = (f32[24,512]{1,0:T(8,128)}, f32[24,512]{1,0:T(8,128)S(1)}, u32[]{:S(2)}) copy-start(f32[24,512]{1,0:T(8,128)S(1)} %get-tuple-element.115.refs_9_) | copy-start | bytes 147460
  59.8 3.4 collective-permute-start.1
  60.0 7.7 %copy-start.44 = (f32[1,1536]{1,0:T(1,128)}, f32[1,1536]{1,0:T(1,128)S(1)}, u32[]{:S(2)}) copy-start(f32[1,1536]{1,0:T(1,128)S(1)} %broadcast_in_dim.51.refs_3_.refs_4_) | copy-start | bytes 18436
  76.6 40.4 %all-to-all-start = ((bf16[4,256,1536]{2,1,0:T(8,128)(2,1)}), bf16[4,256,1536]{2,1,0:T(8,128)(2,1)S(1)}, u32[]{:S(2)}, u32[]{:S(2)}) async-start(bf16[4,256,1536]{2,1,0:T(8,128)(2,1)} %bitcast.69), calls=%async_computation | async-start | bytes 6291456 | tf_op jit(solution)/shard_map/all_to_all | solution.py:900
  80.5 116.1 %collective-permute-start.6 = (bf16[1024,1536]{1,0:T(8,128)(2,1)}, bf16[1024,1536]{1,0:T(8,128)(2,1)}, u32[]{:S(2)}, u32[]{:S(2)}) collective-permute-start(bf16[1024,1536]{1,0:T(8,128)(2,1)} %bitcast.9.refs_2_), channel_id=1, source_target_pairs={{0,1},{1,0},{2,3},{3,2},{4,5},{5,4},{6,7},{7,6},{8,9},{9,8},{10,11... | collective-permute-start | bytes 9437192 | tf_op jit(solution)/shard_map/ppermute | solution.py:896
  117.0 79.7 %collective-permute-start.5 = (bf16[1024,1536]{1,0:T(8,128)(2,1)S(1)}, bf16[1024,1536]{1,0:T(8,128)(2,1)}, u32[]{:S(2)}, u32[]{:S(2)}) collective-permute-start(bf16[1024,1536]{1,0:T(8,128)(2,1)S(1)} %bitcast.62), channel_id=1, source_target_pairs={{0,1},{1,0},{2,3},{3,2},{4,5},{5,4},{6,7},{7,6},{8,9},{9,8},{10,11... | collective-permute-start | bytes 9437192 | tf_op jit(solution)/shard_map/ppermute | solution.py:896
  161.2 3.9 collective-permute-start.3
  196.3 63.0 %collective-permute-start.4 = (bf16[512,1536]{1,0:T(8,128)(2,1)}, bf16[512,1536]{1,0:T(8,128)(2,1)}, u32[]{:S(2)}, u32[]{:S(2)}) collective-permute-start(bf16[512,1536]{1,0:T(8,128)(2,1)} %get-tuple-element.117.refs_1_), channel_id=1, source_target_pairs={{0,1},{1,0},{2,3},{3,2},{4,5},{5,4},{6,7},{7,6},{8,9},{9,8},{10,11... | collective-permute-start | bytes 4718600 | tf_op jit(solution)/shard_map/ppermute | solution.py:896
  196.7 20.3 %copy-start.17 = (bf16[512,1536]{1,0:T(8,128)(2,1)S(1)}, bf16[512,1536]{1,0:T(8,128)(2,1)}, u32[]{:S(2)}) copy-start(bf16[512,1536]{1,0:T(8,128)(2,1)} %get-tuple-element.134.refs_0_) | copy-start | bytes 4718596
  215.3 40.3 %collective-permute-start.7 = (bf16[2,1152,256]{2,1,0:T(8,128)(2,1)}, bf16[2,1152,256]{2,1,0:T(8,128)(2,1)}, u32[]{:S(2)}, u32[]{:S(2)}) collective-permute-start(bf16[2,1152,256]{2,1,0:T(8,128)(2,1)} %get-tuple-element.127), channel_id=1, source_target_pairs={{0,8},{2,10},{4,12},{6,14},{8,0},{10,2},{12,4},{14,6},{16,24},{18,... | collective-permute-start | bytes 3538952 | tf_op jit(solution)/shard_map/ppermute | solution.py:905
  219.4 71.0 %all-to-all-start.3 = ((bf16[4,256,1536]{2,1,0:T(8,128)(2,1)}), bf16[4,256,1536]{2,1,0:T(8,128)(2,1)}, u32[]{:S(2)}, u32[]{:S(2)}) async-start(bf16[4,256,1536]{2,1,0:T(8,128)(2,1)} %bitcast.68), calls=%async_computation.3 | async-start | bytes 6291456 | tf_op jit(solution)/shard_map/all_to_all | solution.py:900
  238.4 17.2 %copy-start.8 = (bf16[2,1152,256]{2,1,0:T(8,128)(2,1)S(1)}, bf16[2,1152,256]{2,1,0:T(8,128)(2,1)}, u32[]{:S(2)}) copy-start(bf16[2,1152,256]{2,1,0:T(8,128)(2,1)} %copy-done.7) | copy-start | bytes 3538948
  255.6 3.7 copy-start.30
  323.5 83.1 %all-to-all-start.4 = ((bf16[4,4,288,768]{3,2,1,0:T(8,128)(2,1)}), bf16[4,4,288,768]{3,2,1,0:T(8,128)(2,1)}, u32[]{:S(2)}, u32[]{:S(2)}) async-start(bf16[4,4,288,768]{3,2,1,0:T(8,128)(2,1)} %get-tuple-element.158), calls=%async_computation.4 | async-start | bytes 14155776 | tf_op jit(solution)/shard_map/all_to_all | solution.py:900
  328.8 26.6 %collective-permute-start.9 = (bf16[2,1152,256]{2,1,0:T(8,128)(2,1)}, bf16[2,1152,256]{2,1,0:T(8,128)(2,1)S(1)}, u32[]{:S(2)}, u32[]{:S(2)}) collective-permute-start(bf16[2,1152,256]{2,1,0:T(8,128)(2,1)} %copy-done.48), channel_id=1, source_target_pairs={{0,8},{2,10},{4,12},{6,14},{8,0},{10,2},{12,4},{14,6},{16,24},{18,... | collective-permute-start | bytes 3538952 | tf_op jit(solution)/shard_map/ppermute | solution.py:905
  329.3 92.3 %collective-permute-start.14 = (bf16[1024,1536]{1,0:T(8,128)(2,1)}, bf16[1024,1536]{1,0:T(8,128)(2,1)}, u32[]{:S(2)}, u32[]{:S(2)}) collective-permute-start(bf16[1024,1536]{1,0:T(8,128)(2,1)} %bitcast.17.refs_2_), channel_id=1, source_target_pairs={{0,1},{1,0},{2,3},{3,2},{4,5},{5,4},{6,7},{7,6},{8,9},{9,8},{10,11... | collective-permute-start | bytes 9437192 | tf_op jit(solution)/shard_map/ppermute | solution.py:896
  329.3 50.9 %collective-permute-start.8 = (bf16[512,1536]{1,0:T(8,128)(2,1)}, bf16[512,1536]{1,0:T(8,128)(2,1)S(1)}, u32[]{:S(2)}, u32[]{:S(2)}) collective-permute-start(bf16[512,1536]{1,0:T(8,128)(2,1)} %get-tuple-element.140.refs_1_), channel_id=1, source_target_pairs={{0,1},{1,0},{2,3},{3,2},{4,5},{5,4},{6,7},{7,6},{8,9},{9,8},{10,11... | collective-permute-start | bytes 4718600 | tf_op jit(solution)/shard_map/ppermute | solution.py:896
  329.9 101.3 %collective-permute-start.2 = (bf16[512,1536]{1,0:T(8,128)(2,1)}, bf16[512,1536]{1,0:T(8,128)(2,1)}, u32[]{:S(2)}, u32[]{:S(2)}) collective-permute-start(bf16[512,1536]{1,0:T(8,128)(2,1)} %copy-done.14), channel_id=1, source_target_pairs={{0,1},{1,0},{2,3},{3,2},{4,5},{5,4},{6,7},{7,6},{8,9},{9,8},{10,11... | collective-permute-start | bytes 4718600 | tf_op jit(solution)/shard_map/ppermute | solution.py:896
  357.0 18.0 %copy-start.23 = (f32[1152,256]{1,0:T(8,128)}, f32[1152,256]{1,0:T(8,128)S(1)}, u32[]{:S(2)}) copy-start(f32[1152,256]{1,0:T(8,128)S(1)} %get-tuple-element.181) | copy-start | bytes 3538948
  357.0 18.0 %copy-start.49 = (bf16[1152,256]{1,0:T(8,128)(2,1)}, bf16[1152,256]{1,0:T(8,128)(2,1)S(1)}, u32[]{:S(2)}) copy-start(bf16[1152,256]{1,0:T(8,128)(2,1)S(1)} %get-tuple-element.182) | copy-start | bytes 1769476
  357.0 19.4 %copy-start.61 = (bf16[512,1536]{1,0:T(8,128)(2,1)S(1)}, bf16[512,1536]{1,0:T(8,128)(2,1)}, u32[]{:S(2)}) copy-start(bf16[512,1536]{1,0:T(8,128)(2,1)} %copy-done.60) | copy-start | bytes 4718596
  357.0 19.4 %copy-start.63 = (bf16[512,768]{1,0:T(8,128)(2,1)S(1)}, bf16[512,768]{1,0:T(8,128)(2,1)}, u32[]{:S(2)}) copy-start(bf16[512,768]{1,0:T(8,128)(2,1)} %copy-done.62) | copy-start | bytes 2359300
  376.0 41.6 %collective-permute-start.15 = (bf16[2,1152,256]{2,1,0:T(8,128)(2,1)}, bf16[2,1152,256]{2,1,0:T(8,128)(2,1)S(1)}, u32[]{:S(2)}, u32[]{:S(2)}) collective-permute-start(bf16[2,1152,256]{2,1,0:T(8,128)(2,1)} %get-tuple-element.157), channel_id=1, source_target_pairs={{0,8},{2,10},{4,12},{6,14},{8,0},{10,2},{12,4},{14,6},{16,24},{18,... | collective-permute-start | bytes 3538952 | tf_op jit(solution)/shard_map/ppermute | solution.py:905
  376.4 3.8 copy-start.16
  376.4 3.8 copy-start.43
  380.3 6.2 %copy-start.40 = (f32[2,1536]{1,0:T(2,128)S(1)}, f32[2,1536]{1,0:T(2,128)}, u32[]{:S(2)}) copy-start(f32[2,1536]{1,0:T(2,128)} %copy-done.39) | copy-start | bytes 36868
  387.1 23.3 %collective-permute-start.10 = (f32[6,1536]{1,0:T(8,128)}, f32[6,1536]{1,0:T(8,128)}, u32[]{:S(2)}, u32[]{:S(2)}) collective-permute-start(f32[6,1536]{1,0:T(8,128)} %pad_maximum_fusion), channel_id=1, source_target_pairs={{0,2},{2,0},{4,6},{6,4},{8,10},{10,8},{12,14},{14,12},{16,18},{18,... | collective-permute-start | bytes 110600 | tf_op jit(solution)/shard_map/ppermute | solution.py:168
  389.3 49.1 %collective-permute-start.22 = (bf16[1152,256]{1,0:T(8,128)(2,1)}, bf16[1152,256]{1,0:T(8,128)(2,1)}, u32[]{:S(2)}, u32[]{:S(2)}) collective-permute-start(bf16[1152,256]{1,0:T(8,128)(2,1)} %get-tuple-element.180), channel_id=1, source_target_pairs={{0,16},{2,18},{4,20},{6,22},{8,24},{10,26},{12,28},{14,30},{16,0},... | collective-permute-start | bytes 1769480 | tf_op jit(solution)/shard_map/ppermute | solution.py:905
  406.5 72.3 %all-to-all-start.5 = ((bf16[4,4,96,768]{3,2,1,0:T(8,128)(2,1)}), bf16[4,4,96,768]{3,2,1,0:T(8,128)(2,1)S(1)}, u32[]{:S(2)}, u32[]{:S(2)}) async-start(bf16[4,4,96,768]{3,2,1,0:T(8,128)(2,1)} %copy-done.13), calls=%async_computation.5 | async-start | bytes 4718592 | tf_op jit(solution)/shard_map/all_to_all | solution.py:900
  410.4 71.8 %collective-permute-start.23 = (bf16[1152,256]{1,0:T(8,128)(2,1)}, bf16[1152,256]{1,0:T(8,128)(2,1)}, u32[]{:S(2)}, u32[]{:S(2)}) collective-permute-start(bf16[1152,256]{1,0:T(8,128)(2,1)} %copy-done.49), channel_id=1, source_target_pairs={{0,16},{2,18},{4,20},{6,22},{8,24},{10,26},{12,28},{14,30},{16,0},... | collective-permute-start | bytes 1769480 | tf_op jit(solution)/shard_map/ppermute | solution.py:905
  413.9 5.7 copy-start.4
  417.6 20.4 %collective-permute-start.11 = (f32[6,1536]{1,0:T(8,128)S(1)}, f32[6,1536]{1,0:T(8,128)S(1)}, u32[]{:S(2)}, u32[]{:S(2)}) collective-permute-start(f32[6,1536]{1,0:T(8,128)S(1)} %fusion.9), channel_id=1, source_target_pairs={{0,4},{2,6},{4,0},{6,2},{8,12},{10,14},{12,8},{14,10},{16,20},{18,... | collective-permute-start | bytes 110600 | tf_op jit(solution)/shard_map/ppermute | solution.py:168
  421.6 55.3 %collective-permute-start.17 = (bf16[2,288,768]{2,1,0:T(8,128)(2,1)S(1)}, bf16[2,288,768]{2,1,0:T(8,128)(2,1)S(1)}, u32[]{:S(2)}, u32[]{:S(2)}) collective-permute-start(bf16[2,288,768]{2,1,0:T(8,128)(2,1)S(1)} %get-tuple-element.166), channel_id=1, source_target_pairs={{0,8},{2,10},{4,12},{6,14},{8,0},{10,2},{12,4},{14,6},{16,24},{18,... | collective-permute-start | bytes 2654216 | tf_op jit(solution)/shard_map/ppermute | solution.py:905
  422.1 10.7 %copy-start.15 = (bf16[512,1536]{1,0:T(8,128)(2,1)S(1)}, bf16[512,1536]{1,0:T(8,128)(2,1)}, u32[]{:S(2)}) copy-start(bf16[512,1536]{1,0:T(8,128)(2,1)} %copy-done.14) | copy-start | bytes 4718596
  422.1 10.7 %copy-start.91 = (f32[512,1536]{1,0:T(8,128)S(1)}, f32[512,1536]{1,0:T(8,128)}, u32[]{:S(2)}) copy-start(f32[512,1536]{1,0:T(8,128)} %get-tuple-element.108.refs_0_) | copy-start | bytes 9437188
  431.2 7.2 %copy-start.22 = (f32[1152,256]{1,0:T(8,128)S(1)}, f32[1152,256]{1,0:T(8,128)}, u32[]{:S(2)}) copy-start(f32[1152,256]{1,0:T(8,128)} %copy-done.21) | copy-start | bytes 3538948
  431.2 48.9 %collective-permute-start.16 = (bf16[2,576,384]{2,1,0:T(8,128)(2,1)}, bf16[2,576,384]{2,1,0:T(8,128)(2,1)}, u32[]{:S(2)}, u32[]{:S(2)}) collective-permute-start(bf16[2,576,384]{2,1,0:T(8,128)(2,1)} %get-tuple-element.163), channel_id=1, source_target_pairs={{0,8},{2,10},{4,12},{6,14},{8,0},{10,2},{12,4},{14,6},{16,24},{18,... | collective-permute-start | bytes 2654216 | tf_op jit(solution)/shard_map/ppermute | solution.py:905
  438.0 35.4 %collective-permute-start.12 = (f32[6,1536]{1,0:T(8,128)S(1)}, f32[6,1536]{1,0:T(8,128)S(1)}, u32[]{:S(2)}, u32[]{:S(2)}) collective-permute-start(f32[6,1536]{1,0:T(8,128)S(1)} %add.108), channel_id=1, source_target_pairs={{0,8},{2,10},{4,12},{6,14},{8,0},{10,2},{12,4},{14,6},{16,24},{18,... | collective-permute-start | bytes 110600 | tf_op jit(solution)/shard_map/ppermute | solution.py:168
  474.0 26.6 %collective-permute-start.13 = (f32[6,1536]{1,0:T(8,128)}, f32[6,1536]{1,0:T(8,128)}, u32[]{:S(2)}, u32[]{:S(2)}) collective-permute-start(f32[6,1536]{1,0:T(8,128)} %add.109), channel_id=1, source_target_pairs={{0,16},{2,18},{4,20},{6,22},{8,24},{10,26},{12,28},{14,30},{16,0},... | collective-permute-start | bytes 110600 | tf_op jit(solution)/shard_map/ppermute | solution.py:168
  474.5 51.4 %collective-permute-start.24 = (bf16[1152,256]{1,0:T(8,128)(2,1)}, bf16[1152,256]{1,0:T(8,128)(2,1)}, u32[]{:S(2)}, u32[]{:S(2)}) collective-permute-start(bf16[1152,256]{1,0:T(8,128)(2,1)} %get-tuple-element.184), channel_id=1, source_target_pairs={{0,16},{2,18},{4,20},{6,22},{8,24},{10,26},{12,28},{14,30},{16,0},... | collective-permute-start | bytes 1769480 | tf_op jit(solution)/shard_map/ppermute | solution.py:905
  481.6 39.0 %collective-permute-start.18 = (bf16[576,384]{1,0:T(8,128)(2,1)S(1)}, bf16[576,384]{1,0:T(8,128)(2,1)S(1)}, u32[]{:S(2)}, u32[]{:S(2)}) collective-permute-start(bf16[576,384]{1,0:T(8,128)(2,1)S(1)} %get-tuple-element.171), channel_id=1, source_target_pairs={{0,16},{2,18},{4,20},{6,22},{8,24},{10,26},{12,28},{14,30},{16,0},... | collective-permute-start | bytes 1327112 | tf_op jit(solution)/shard_map/ppermute | solution.py:905
  520.6 5.2 copy-start.26
  521.7 19.9 %all-to-all-start.6 = ((bf16[4,96,576]{2,1,0:T(8,128)(2,1)}), bf16[4,96,576]{2,1,0:T(8,128)(2,1)}, u32[]{:S(2)}, u32[]{:S(2)}) async-start(bf16[4,96,576]{2,1,0:T(8,128)(2,1)} %bitcast.21), calls=%async_computation.6 | async-start | bytes 983040 | tf_op jit(solution)/shard_map/all_to_all | solution.py:900
  525.9 5.2 copy-start.90
  528.3 18.7 %collective-permute-start.19 = (bf16[2,96,768]{2,1,0:T(8,128)(2,1)S(1)}, bf16[2,96,768]{2,1,0:T(8,128)(2,1)S(1)}, u32[]{:S(2)}, u32[]{:S(2)}) collective-permute-start(bf16[2,96,768]{2,1,0:T(8,128)(2,1)S(1)} %copy-done.53), channel_id=1, source_target_pairs={{0,8},{2,10},{4,12},{6,14},{8,0},{10,2},{12,4},{14,6},{16,24},{18,... | collective-permute-start | bytes 884744 | tf_op jit(solution)/shard_map/ppermute | solution.py:905
  528.4 22.8 %collective-permute-start.21 = (bf16[288,768]{1,0:T(8,128)(2,1)S(1)}, bf16[288,768]{1,0:T(8,128)(2,1)}, u32[]{:S(2)}, u32[]{:S(2)}) collective-permute-start(bf16[288,768]{1,0:T(8,128)(2,1)S(1)} %copy-done.51), channel_id=1, source_target_pairs={{0,16},{2,18},{4,20},{6,22},{8,24},{10,26},{12,28},{14,30},{16,0},... | collective-permute-start | bytes 1327112 | tf_op jit(solution)/shard_map/ppermute | solution.py:905
  541.7 9.6 %copy-start.28 = (f32[288,768]{1,0:T(8,128)S(1)}, f32[288,768]{1,0:T(8,128)}, u32[]{:S(2)}) copy-start(f32[288,768]{1,0:T(8,128)} %copy-done.27) | copy-start | bytes 2654212
  541.7 24.9 %all-to-all-start.7 = ((bf16[4,3,96,768]{3,2,1,0:T(8,128)(2,1)}), bf16[4,3,96,768]{3,2,1,0:T(8,128)(2,1)}, u32[]{:S(2)}, u32[]{:S(2)}) async-start(bf16[4,3,96,768]{3,2,1,0:T(8,128)(2,1)} %reshape.123), calls=%async_computation.7 | async-start | bytes 3538944 | tf_op jit(solution)/shard_map/all_to_all | solution.py:900
  547.7 8.1 %collective-permute-start.20 = (bf16[96,768]{1,0:T(8,128)(2,1)S(1)}, bf16[96,768]{1,0:T(8,128)(2,1)S(1)}, u32[]{:S(2)}, u32[]{:S(2)}) collective-permute-start(bf16[96,768]{1,0:T(8,128)(2,1)S(1)} %get-tuple-element.176), channel_id=1, source_target_pairs={{0,16},{2,18},{4,20},{6,22},{8,24},{10,26},{12,28},{14,30},{16,0},... | collective-permute-start | bytes 442376 | tf_op jit(solution)/shard_map/ppermute | solution.py:905
  (66 other events, 99.3 us)
